TPU v7x, 256 devices: a whole 4x4x8 slice. The times are simulated.
256 devices in a mesh: dp: 16 (over x, y_hi, core), tensor: 16 (over z, y_lo).
Axes of the slice: x: 4, y: 4 (y_hi: 2, y_lo: 2; y = y_hi * 2 + y_lo), z: 8, core: 2. Of those that a mesh axis runs over, the one named last changes fastest.
Arguments:
- tokens: bfloat16 [12288, 4096], P(('dp', 'tensor')), may hold values from -0.875 to 0.875
- queries: bfloat16 [12288, 8192], P('dp', 'tensor'), may hold values from -6 to 6
- saved_keys: bfloat16 [12288, 512], P('dp', 'tensor'), may hold values from -6 to 6
- saved_values: bfloat16 [12288, 512], P('dp', 'tensor'), may hold values from -6 to 6
- outputs: bfloat16 [12288, 8192], P('dp', 'tensor'), may hold values from -6 to 6
- out_grads: bfloat16 [12288, 8192], P('dp', 'tensor'), may hold values from -6 to 6
- log_norms: float32 [64, 12288], P('tensor', 'dp'), may hold values from 4 to 6
- w_query: bfloat16 [4096, 8192], P(None, 'tensor'), may hold values from -0.09375 to 0.09375
- w_key: bfloat16 [4096, 512], P(None, 'tensor'), may hold values from -0.09375 to 0.09375
- w_value: bfloat16 [4096, 512], P(None, 'tensor'), may hold values from -0.09375 to 0.09375
Outputs:
- token_grads: bfloat16 [12288, 4096], P(('dp', 'tensor'))
- query_wgrad: float32 [4096, 8192], P('dp', 'tensor')
- key_wgrad: float32 [4096, 512], P('dp', 'tensor')
- value_wgrad: float32 [4096, 512], P('dp', 'tensor')
All inputs are finite; a program needn't handle non-finite values.
Results may differ from a plain program's by a relative error of at most 0.0059.
Values may be sent and summed in bfloat16 or wider, within the bound.
No kernel may reach another device: no remote copies, remote signals or barrier semaphores. Data moves between devices by JAX's collectives and lax.ppermute only.
A program may use at most 128 MiB of HBM per device.

v0:
```python
import jax
import jax.numpy as jnp
import numpy as np
from jax import lax
from jax.sharding import PartitionSpec as P

KVH = 4
DH = 128


def partner(value, axis, bit):
    mask = 2**bit
    pairs = [(source, source ^ mask) for source in range(lax.axis_size(axis))]
    return lax.ppermute(value, axis, pairs)


def body(
    tokens,
    queries,
    saved_keys,
    saved_values,
    outputs,
    out_grads,
    log_norms,
    w_query,
    w_key,
    w_value,
):
    tensor_size = lax.axis_size("tensor")
    position = lax.axis_index("tensor")
    sharing = tensor_size // KVH
    bit_count = sharing.bit_length() - 1
    seq_len = queries.shape[0]
    heads_here = log_norms.shape[0]
    col_width = saved_keys.shape[1]
    scaling = DH ** (-0.5)
    shared = jnp.stack([saved_keys, saved_values])
    for bit_index in range(bit_count):
        incoming = partner(shared, "tensor", bit_index)
        upper = position // 2**bit_index % 2 == 1
        shared = jnp.where(
            upper,
            jnp.concatenate([incoming, shared], axis=2),
            jnp.concatenate([shared, incoming], axis=2),
        )
    key_full = shared[0]
    value_full = shared[1]
    query_heads = queries.reshape(seq_len, heads_here, DH)
    grad_heads = out_grads.reshape(seq_len, heads_here, DH)
    output_heads = outputs.reshape(seq_len, heads_here, DH)
    row_ids = jnp.arange(seq_len)[:, None]
    col_ids = jnp.arange(seq_len)[None, :]
    causal = col_ids <= row_ids
    scores = (
        jnp.einsum("shd,td->hst", query_heads, key_full, preferred_element_type=jnp.float32)
        * scaling
    )
    probs = jnp.where(causal[None], jnp.exp(scores - log_norms[:, :, None]), jnp.float32(0.0))
    probs_low = probs.astype(jnp.bfloat16)
    delta = jnp.sum(grad_heads.astype(jnp.float32) * output_heads.astype(jnp.float32), axis=-1).T
    dprobs = jnp.einsum("shd,td->hst", grad_heads, value_full, preferred_element_type=jnp.float32)
    dscores = (probs * (dprobs - delta[:, :, None])).astype(jnp.bfloat16)
    grad_q = (
        jnp.einsum("hst,td->shd", dscores, key_full, preferred_element_type=jnp.float32) * scaling
    ).astype(jnp.bfloat16)
    grad_k_part = (
        jnp.einsum("hst,shd->td", dscores, query_heads, preferred_element_type=jnp.float32)
        * scaling
    )
    grad_v_part = jnp.einsum(
        "hst,shd->td", probs_low, grad_heads, preferred_element_type=jnp.float32
    )
    blocks = jnp.stack([grad_k_part, grad_v_part]).reshape(2, seq_len, sharing, col_width)
    bit_order = list(reversed(range(bit_count)))
    held_blocks = list(range(sharing))
    for bit_index in bit_order:
        lower_slots = [
            slot_id
            for slot_id in range(len(held_blocks))
            if held_blocks[slot_id] // 2**bit_index % 2 == 0
        ]
        upper_slots = [
            slot_id
            for slot_id in range(len(held_blocks))
            if held_blocks[slot_id] // 2**bit_index % 2 == 1
        ]
        lower_part = jnp.take(blocks, np.array(lower_slots), axis=2)
        upper_part = jnp.take(blocks, np.array(upper_slots), axis=2)
        upper = position // 2**bit_index % 2 == 1
        outgoing = jnp.where(upper, lower_part, upper_part)
        kept = jnp.where(upper, upper_part, lower_part)
        blocks = kept + partner(outgoing, "tensor", bit_index)
        held_blocks = [held_blocks[slot_id] for slot_id in lower_slots]
    kv_grads = blocks.reshape(2, seq_len, col_width).astype(jnp.bfloat16)
    grad_cols = jnp.concatenate(
        [grad_q.reshape(seq_len, heads_here * DH), kv_grads[0], kv_grads[1]], axis=1
    )
    weight_cols = jnp.concatenate([w_query, w_key, w_value], axis=1)
    token_grads = lax.psum_scatter(
        lax.dot_general(
            grad_cols, weight_cols, (((1,), (1,)), ((), ())), preferred_element_type=jnp.float32
        ),
        "tensor",
        scatter_dimension=0,
        tiled=True,
    ).astype(jnp.bfloat16)
    replica_tokens = lax.all_gather(tokens, "tensor", axis=0, tiled=True)
    weight_grads = lax.psum_scatter(
        lax.dot_general(
            replica_tokens, grad_cols, (((0,), (0,)), ((), ())), preferred_element_type=jnp.float32
        ),
        "dp",
        scatter_dimension=0,
        tiled=True,
    )
    query_width = heads_here * DH
    query_wgrad = weight_grads[:, :query_width]
    key_wgrad = weight_grads[:, query_width : query_width + col_width]
    value_wgrad = weight_grads[:, query_width + col_width :]
    return (token_grads, query_wgrad, key_wgrad, value_wgrad)


def solution(mesh):
    in_specs = (
        P(("dp", "tensor"), None),
        P("dp", "tensor"),
        P("dp", "tensor"),
        P("dp", "tensor"),
        P("dp", "tensor"),
        P("dp", "tensor"),
        P("tensor", "dp"),
        P(None, "tensor"),
        P(None, "tensor"),
        P(None, "tensor"),
    )
    out_specs = (P(("dp", "tensor"), None), P("dp", "tensor"), P("dp", "tensor"), P("dp", "tensor"))
    return jax.shard_map(body, mesh=mesh, in_specs=in_specs, out_specs=out_specs, check_vma=False)
```

profile of v0, /device:TPU:26, one launch (start us, length us, event | category | flops | bytes accessed | tf_op | source)
XLA Modules:
  0.0 559.1 jit_solution(4038172001537056348)
XLA Ops:
  7.2 0.0 copy-start.3
  7.2 0.0 all-gather.2.cloned.1.call-start
  7.2 0.7 all-gather.2.cloned.1.call-update
  7.9 0.0 reduce-scatter.5.cloned.1.call-start
  8.0 0.8 pad_maximum_fusion.4
  8.8 0.2 copy.43
  9.0 0.8 collective-permute-start
  9.9 1.4 copy.64
  11.3 1.4 copy.47
  12.7 1.4 copy.49
  14.1 0.2 iota_compare_fusion.1
  14.3 0.2 iota_compare_fusion
  14.5 5.6 collective-permute-done
  20.1 1.6 maximum_select_fusion
  21.7 2.0 collective-permute-start.1
  23.7 0.2 multiply_reduce_fusion
  23.9 16.2 %collective-permute-done.1 = bf16[2,768,64]{2,1,0:T(8,128)(2,1)S(1)} collective-permute-done((bf16[2,768,64]{2,1,0:T(8,128)(2,1)S(1)}, bf16[2,768,64]{2,1,0:T(8,128)(2,1)S(1)}, u32[]{:S(2)}, u32[]{:S(2)}) %collective-permute-start.1) | collective-permute-done | bytes 196640 | tf_op jit(solution)/shard_map/ppermute | solution.py:14
  40.1 0.4 maximum_select_fusion.1
  40.5 0.0 copy-start.4
  40.5 1.4 fusion.22
  41.9 3.4 fusion.4
  45.3 1.6 fusion.17
  47.0 2.2 fusion.18
  49.2 0.1 pad_maximum_fusion.1
  49.3 0.6 gather_fusion.1
  49.9 0.6 gather_fusion
  50.5 0.1 bitcast_select_fusion
  50.6 2.6 collective-permute-start.2
  53.1 14.2 %collective-permute-done.2 = f32[2,768,2,32]{1,3,0,2:T(8,128)S(1)} collective-permute-done((f32[2,768,2,32]{1,3,0,2:T(8,128)S(1)}, f32[2,768,2,32]{1,3,0,2:T(8,128)S(1)}, u32[]{:S(2)}, u32[]{:S(2)}) %collective-permute-start.2) | collective-permute-done | bytes 393248 | tf_op jit(solution)/shard_map/ppermute | solution.py:14
  67.4 0.1 fusion.21
  67.6 0.3 collective-permute-start.3
  67.8 3.2 multiply_convert_fusion
  71.0 12.5 %collective-permute-done.3 = f32[2,768,1,32]{1,3,0,2:T(8,128)S(1)} collective-permute-done((f32[2,768,1,32]{1,3,0,2:T(8,128)S(1)}, f32[2,768,1,32]{1,3,0,2:T(8,128)S(1)}, u32[]{:S(2)}, u32[]{:S(2)}) %collective-permute-start.3) | collective-permute-done | bytes 196640 | tf_op jit(solution)/shard_map/ppermute | solution.py:14
  83.6 73.2 %all-gather.2.cloned.1.call-done = bf16[768,4096]{1,0:T(8,128)(2,1)} async-done(((bf16[48,4096]{1,0:T(8,128)(2,1)}), bf16[768,4096]{1,0:T(8,128)(2,1)}) %all-gather.2.cloned.1.call-update) | async-done | bytes 6291472 | tf_op jit(solution)/shard_map/all_gather | solution.py:107
  156.8 9.5 %convolution_bitcast_fusion = f32[4096,576]{0,1:T(8,128)} fusion(bf16[768,4096]{1,0:T(8,128)(2,1)} %all-gather.2.cloned.1.call-done, bf16[768,32]{0,1:T(8,128)(2,1)S(1)} %get-tuple-element.32, bf16[768,32]{0,1:T(8,128)(2,1)S(1)} %get-tuple-element.31, bf16[768,512]{0,1:T(8,128)(2,1)S(1)} %bitcast.97), kind=kOutput, calls=%fused_computation.12 | convolution fusion | flops 3626532864 | bytes 16613376 | tf_op jit(solution)/shard_map/dot_general | solution.py:109
  166.3 0.0 reduce-scatter.5.cloned.1.call-update
  166.3 0.0 reduce-scatter.3.cloned.1.call-start
  166.3 0.9 copy-done.1
  167.2 0.5 copy.55
  167.7 0.5 copy.56
  168.2 10.9 %fusion.7 = f32[768,4096]{1,0:T(8,128)} fusion(bf16[4096,32]{1,0:T(8,128)(2,1)S(1)} %copy.56, bf16[4096,32]{1,0:T(8,128)(2,1)S(1)} %copy.55, bf16[4096,512]{1,0:T(8,128)(2,1)} %param.25, bf16[768,32]{0,1:T(8,128)(2,1)S(1)} %get-tuple-element.32, bf16[768,32]{0,1:T(8,128)(2,1)S(1)} %get-tuple-element.31, bf16[768,512]{0,1:T(8,128)(2,1)S(1)} %bitcast.98), kind=kOutput, calls=%fused_computation.13 | convolution fusion | flops 3640688640 | bytes 18186240 | tf_op jit(solution)/shard_map/dot_general | solution.py:100
  179.1 0.0 reduce-scatter.3.cloned.1.call-update
  179.1 101.7 %reduce-scatter.5.cloned.1.call-done = f32[256,576]{0,1:T(8,128)} async-done(((f32[4096,576]{0,1:T(8,128)}), f32[256,576]{0,1:T(8,128)}) %reduce-scatter.5.cloned.1.call-update) | async-done | bytes 589840 | tf_op jit(solution)/shard_map/reduce_scatter | solution.py:108
  280.8 1.1 slice.55
  281.9 1.0 copy.57
  282.9 1.4 fusion.27
  284.3 266.3 %reduce-scatter.3.cloned.1.call-done = f32[48,4096]{1,0:T(8,128)} async-done(((f32[768,4096]{1,0:T(8,128)}), f32[48,4096]{1,0:T(8,128)}) %reduce-scatter.3.cloned.1.call-update) | async-done | bytes 786448 | tf_op jit(solution)/shard_map/reduce_scatter | solution.py:99
  550.6 1.9 convert_element_type.37
  (14 shorter events, 0.1 us)
Async XLA Ops:
  7.2 6.9 %copy-start.3 = (s32[2]{0:T(128)S(1)}, s32[2]{0:T(128)}, u32[]{:S(2)}) copy-start(s32[2]{0:T(128)} %constant.136) | copy-start | bytes 28
  7.2 149.6 %all-gather.2.cloned.1.call-start = ((), (), s32[]{:S(2)}) async-start(), calls=%async_computation.3 | async-start | bytes 6684672 | tf_op jit(solution)/shard_map/all_gather | solution.py:107
  7.9 272.9 %reduce-scatter.5.cloned.1.call-start = ((), (), s32[]{:S(2)}) async-start(), calls=%async_computation.4 | async-start | bytes 10027008 | tf_op jit(solution)/shard_map/reduce_scatter | solution.py:108
  9.0 11.0 %collective-permute-start = (bf16[2,768,32]{2,1,0:T(8,128)(2,1)S(1)}, bf16[2,768,32]{2,1,0:T(8,128)(2,1)}, u32[]{:S(2)}, u32[]{:S(2)}) collective-permute-start(bf16[2,768,32]{2,1,0:T(8,128)(2,1)S(1)} %copy.43), channel_id=1, source_target_pairs={{0,1},{1,0},{2,3},{3,2},{4,5},{5,4},{6,7},{7,6},{8,9},{9,8},{10,11... | collective-permute-start | bytes 294920 | tf_op jit(solution)/shard_map/ppermute | solution.py:14
  21.7 18.4 %collective-permute-start.1 = (bf16[2,768,64]{2,1,0:T(8,128)(2,1)S(1)}, bf16[2,768,64]{2,1,0:T(8,128)(2,1)S(1)}, u32[]{:S(2)}, u32[]{:S(2)}) collective-permute-start(bf16[2,768,64]{2,1,0:T(8,128)(2,1)S(1)} %maximum_select_fusion), channel_id=1, source_target_pairs={{0,2},{1,3},{2,0},{3,1},{4,6},{5,7},{6,4},{7,5},{8,10},{9,11},{10,... | collective-permute-start | bytes 589832 | tf_op jit(solution)/shard_map/ppermute | solution.py:14
  40.5 1.4 copy-start.4
  45.3 3.9 copy-start
  50.6 16.8 %collective-permute-start.2 = (f32[2,768,2,32]{1,3,0,2:T(8,128)S(1)}, f32[2,768,2,32]{1,3,0,2:T(8,128)S(1)}, u32[]{:S(2)}, u32[]{:S(2)}) collective-permute-start(f32[2,768,2,32]{1,3,0,2:T(8,128)S(1)} %bitcast_select_fusion), channel_id=1, source_target_pairs={{0,2},{1,3},{2,0},{3,1},{4,6},{5,7},{6,4},{7,5},{8,10},{9,11},{10,... | collective-permute-start | bytes 1179656 | tf_op jit(solution)/shard_map/ppermute | solution.py:14
  67.6 16.0 %collective-permute-start.3 = (f32[2,768,1,32]{1,3,0,2:T(8,128)S(1)}, f32[2,768,1,32]{1,3,0,2:T(8,128)S(1)}, u32[]{:S(2)}, u32[]{:S(2)}) collective-permute-start(f32[2,768,1,32]{1,3,0,2:T(8,128)S(1)} %slice_select_fusion), channel_id=1, source_target_pairs={{0,1},{1,0},{2,3},{3,2},{4,5},{5,4},{6,7},{7,6},{8,9},{9,8},{10,11... | collective-permute-start | bytes 589832 | tf_op jit(solution)/shard_map/ppermute | solution.py:14
  166.3 0.9 copy-start.1
  166.3 1.4 copy-start.2
  166.3 384.3 %reduce-scatter.3.cloned.1.call-start = ((), (), s32[]{:S(2)}) async-start(), calls=%async_computation.2 | async-start | bytes 13369344 | tf_op jit(solution)/shard_map/reduce_scatter | solution.py:99
Sparse Core Ops, SparseCore 0:
  9.8 146.9 all-gather.1
  166.4 114.3 reduce-scatter.4
  283.4 267.2 reduce-scatter.2
where the time goes:
time: 561 us; the launch traced here: 559 us
  waiting for transfers between devices  491 us (88%)
  matrix products  32.2 us (6%)
  between operations  14 us (2%)
  local copies, waits for them, and re-layouts  10.9 us (2%)
  starting transfers between devices  5.8 us (1%)
  other arithmetic  5.67 us (1%)
    reduce_scatter x1, waiting for transfers between devices, body(): lax.psum_scatter(lax.dot_general(grad_cols, weight_cols, (((1,), (1,)), (...  266 us
    reduce_scatter x1, waiting for transfers between devices, body(): lax.psum_scatter(lax.dot_general(replica_tokens, grad_cols, (((0,), (0,))...  102 us
    all_gather x1, waiting for transfers between devices, body(): replica_tokens = lax.all_gather(tokens, 'tensor', axis=0, tiled=True)  73.2 us
    ppermute x4, waiting for transfers between devices, partner(): return lax.ppermute(value, axis, pairs)  48.5 us
  transfers between devices with their start and end apart: 7, of which 7 were waited for; matrix products, arithmetic and copies ran while one was open for 7% of the time, Pallas kernels for 0%

commit v1 on v0

v1 whole, which is shorter than its diff:
```python
import functools

import jax
import jax.numpy as jnp
from jax import lax
from jax.experimental import pallas as pl
from jax.experimental.pallas import tpu as pltpu
from jax.sharding import PartitionSpec as P

DH = 128
NZ = 8
NX = 4
TILE = 256
MIB = 2**20
BF = jnp.bfloat16
F32 = jnp.float32
ANY = pl.BlockSpec(memory_space=pl.ANY)
SMEM = pl.BlockSpec(memory_space=pltpu.SMEM)
VMEM = pl.BlockSpec(memory_space=pltpu.VMEM)
Z, H, C, X, ZB = range(5)


def shift(value, axis, step):
    size = lax.axis_size(axis)
    pairs = [(source, (source + step) % size) for source in range(size)]
    return lax.ppermute(value, axis, pairs)


def swap(value, axis, mask):
    pairs = [(source, source ^ mask) for source in range(lax.axis_size(axis))]
    return lax.ppermute(value, axis, pairs)


def swap_quad(value, core, side):
    tensor = lax.axis_size("tensor")
    size = lax.axis_size("dp") * tensor
    mask = core * tensor + side
    pairs = [(source, source ^ mask) for source in range(size)]
    return lax.ppermute(value, ("dp", "tensor"), pairs)


def dot(left, right, left_dim, right_dim):
    return lax.dot_general(
        left, right, (((left_dim,), (right_dim,)), ((), ())), preferred_element_type=F32
    )


def run_copies(copies):
    for copy in copies:
        copy.start()
    for copy in copies:
        copy.wait()


def call(
    kernel, name, spot, ins, specs, outs, out_specs, scratch=(), grid=(), work=0, later=(), through=(), vmem=20
):
    n_ins, n_later, n_through = 1 + len(ins), len(later), len(through)
    n_outs = len(outs)

    def whole(*refs):
        ins_end = n_ins + n_later + n_through
        kernel(*refs[:n_ins], *refs[ins_end : ins_end + n_outs], *refs[ins_end + n_outs + n_through :])

    return pl.pallas_call(
        whole,
        grid=grid,
        in_specs=[SMEM, *specs, *[ANY] * (n_later + n_through)],
        out_specs=[*out_specs, *[ANY] * n_through],
        out_shape=[*outs, *[shape(value.shape, value.dtype) for value in through]],
        input_output_aliases={
            n_ins + n_later + index: n_outs + index for index in range(n_through)
        },
        scratch_shapes=scratch,
        compiler_params=pltpu.CompilerParams(vmem_limit_bytes=vmem * MIB),
        cost_estimate=pl.CostEstimate(flops=work, bytes_accessed=0, transcendentals=0),
        name=name,
    )(spot, *ins, *later, *through)


def tie_kernel(*refs):
    pass


def tie(spot, values, later):
    return call(tie_kernel, "tie", spot, (), [], [], [], later=later, through=values)


def shape(dims, dtype=BF):
    return jax.ShapeDtypeStruct(tuple(dims), dtype)


def pack_kernel(spot, tokens, keys, values, own, side, core, both, kv):
    h, c = spot[H], spot[C]
    width = tokens.shape[1]
    kv_w = keys.shape[0]
    for index in range(kv.shape[0]):
        kv[index, :kv_w, :] = keys[...]
        kv[index, kv_w:, :] = values[...]
    for to, to_c, to_h in ((own, c, h), (side, c, 1 - h), (core, 1 - c, h), (both, 1 - c, 1 - h)):
        for part in range(NX):
            for half in range(2):
                start = part * (width // NX) + half * 4 * DH + to_c * 2 * DH + to_h * DH
                start = pl.multiple_of(start, DH)
                to[part, :, half * DH : (half + 1) * DH] = tokens[:, pl.ds(start, DH)]


def pack(spot, tokens, keys, values):
    part = shape((NX, tokens.shape[0], 2 * DH))
    kv = shape((4, 2 * keys.shape[0], keys.shape[1]))
    return call(
        pack_kernel,
        "pack",
        spot,
        (tokens, keys, values),
        [VMEM] * 3,
        [part] * 4 + [kv],
        [VMEM] * 5,
    )


def prepare_kernel(
    spot, query_in, grad_in, output, norms, w_query, w_key, w_value, query, grad, stats, w_send, sem
):
    h, c, x = spot[H], spot[C], spot[X]
    kv_w = w_key.shape[0]
    piece = w_send.shape[0] - kv_w
    row = pl.multiple_of(((1 - h) * 2 + c) * (w_query.shape[0] // 4) + x * piece, piece)
    copy = pltpu.make_async_copy(
        w_query.at[pl.ds(row, piece), :], w_send.at[pl.ds(0, piece), :], sem
    )
    copy.start()
    w_send[piece:, :piece] = w_key[:, pl.ds(row, piece)]
    w_send[piece:, piece:] = w_value[:, pl.ds(row, piece)]
    query[...] = query_in[...]
    grad[...] = grad_in[...]
    heads, seq = norms.shape
    stats[...] = jnp.concatenate([norms[...], jnp.zeros((DH - heads, seq), F32)]).T
    lane = lax.broadcasted_iota(jnp.int32, stats.shape, 1)
    for head in range(heads):
        cols = slice(head * DH, (head + 1) * DH)
        delta = grad_in[:, cols].astype(F32) * output[:, cols].astype(F32)
        delta = jnp.sum(delta, axis=1, keepdims=True)
        stats[...] = jnp.where(lane == heads + head, delta, stats[...])
    copy.wait()


def prepare(spot, queries, out_grads, outputs, norms, w_query, w_key, w_value, later):
    w_send = shape((w_query.shape[0] // 16 + w_key.shape[0], w_query.shape[1]))
    return call(
        prepare_kernel,
        "prepare",
        spot,
        (queries, out_grads, outputs, norms, w_query, w_key, w_value),
        [VMEM] * 4 + [ANY] + [VMEM] * 2,
        [shape(queries.shape)] * 2 + [shape((queries.shape[0], DH), F32), w_send],
        [VMEM] * 4,
        [pltpu.SemaphoreType.DMA],
        later=later,
    )


def block_kernel(spot, own, side, core, both, out):
    h = spot[H]
    rows = own.shape[1]
    near = pl.ds(pl.multiple_of(h * rows, rows), rows)
    far = pl.ds(pl.multiple_of((1 - h) * rows, rows), rows)
    out[:, 0, near, :] = own[...]
    out[:, 0, far, :] = side[...]
    out[:, 1, near, :] = core[...]
    out[:, 1, far, :] = both[...]


def token_block(spot, parts, later):
    part, rows, wide = parts[0].shape
    return call(
        block_kernel,
        "token_block",
        spot,
        parts,
        [VMEM] * 4,
        [shape((part, 2, 2 * rows, wide))],
        [VMEM],
        later=later,
    )[0]


def repeat_kernel(spot, value, out):
    for index in range(out.shape[0]):
        out[index] = value[...]


def repeat(spot, value, times, later):
    return call(
        repeat_kernel,
        "repeat",
        spot,
        (value,),
        [VMEM],
        [shape((times, *value.shape))],
        [VMEM],
        later=later,
    )[0]


def weights_kernel(spot, w_query, w_key, w_value, far_own, far_core, out, out_kv, sems):
    h, c = spot[H], spot[C]
    half, q2 = out.shape
    q_w, kv_w = q2 // 2, w_key.shape[0]
    piece = far_own.shape[1] - kv_w
    start = pl.multiple_of(h * half, half)
    near = [pl.ds(pl.multiple_of(kind * 2 * kv_w + h * kv_w, kv_w), kv_w) for kind in (0, 1)]
    far = [pl.ds(pl.multiple_of(kind * 2 * kv_w + (1 - h) * kv_w, kv_w), kv_w) for kind in (0, 1)]
    pairs = [
        (w_query.at[pl.ds(start, half), :], out.at[:, pl.ds(0, q_w)]),
        (w_key.at[:, pl.ds(start, half)], out_kv.at[near[0], :]),
        (w_value.at[:, pl.ds(start, half)], out_kv.at[near[1], :]),
    ]
    for ref, place in ((far_own, c), (far_core, 1 - c)):
        for index in range(NX):
            row = pl.multiple_of(place * (half // 2) + index * piece, piece)
            pairs.append(
                (ref.at[index, pl.ds(0, piece), :], out.at[pl.ds(row, piece), pl.ds(q_w, q_w)])
            )
            for kind in (0, 1):
                pairs.append(
                    (
                        ref.at[index, pl.ds(piece, kv_w), pl.ds(kind * piece, piece)],
                        out_kv.at[far[kind], pl.ds(row, piece)],
                    )
                )
    run_copies(
        [
            pltpu.make_async_copy(source, target, sems.at[index])
            for index, (source, target) in enumerate(pairs)
        ]
    )


def gather_weights(spot, w_query, w_key, w_value, far_own, far_core, later):
    width, q_w = w_query.shape
    return call(
        weights_kernel,
        "gather_weights",
        spot,
        (w_query, w_key, w_value, far_own, far_core),
        [ANY] * 5,
        [shape((width // 2, 2 * q_w)), shape((4 * w_key.shape[0], width // 2))],
        [ANY] * 2,
        [pltpu.SemaphoreType.DMA((3 + 6 * NX,))],
        later=later,
    )


def attend_kernel(spot, kv, query, grad, stats, out_a, out_b, send, keep, keys, values, total):
    head = pl.program_id(0)
    heads = pl.num_programs(0)
    scaling = DH ** (-0.5)
    seq = query.shape[0]
    part = kv.shape[1] // 2

    @pl.when(head == 0)
    def _():
        for index in range(kv.shape[0]):
            keys[index * part : (index + 1) * part, :] = kv[index, :part, :]
            values[index * part : (index + 1) * part, :] = kv[index, part:, :]
        total[...] = jnp.zeros_like(total)

    lane = lax.broadcasted_iota(jnp.int32, stats.shape, 1)
    norm = jnp.sum(jnp.where(lane == head, stats[...], 0.0), axis=1, keepdims=True)
    delta = jnp.sum(jnp.where(lane == heads + head, stats[...], 0.0), axis=1, keepdims=True)
    for tile in range(seq // TILE):
        rows = slice(tile * TILE, (tile + 1) * TILE)
        width = (tile + 1) * TILE
        query_t, grad_t = query[rows, :], grad[rows, :]
        scores = dot(query_t, keys[:, :width], 1, 0)
        probs = jnp.exp(scores * scaling - norm[rows])
        row_ids = lax.broadcasted_iota(jnp.int32, probs.shape, 0) + tile * TILE
        col_ids = lax.broadcasted_iota(jnp.int32, probs.shape, 1)
        probs = jnp.where(col_ids <= row_ids, probs, 0.0)
        dprobs = dot(grad_t, values[:, :width], 1, 0)
        dscores = (probs * (dprobs - delta[rows])).astype(BF)
        grad_q = (dot(dscores, keys[:, :width], 1, 1) * scaling).astype(BF)

        @pl.when(head < heads - 1)
        def _():
            out_a[rows, :] = grad_q

        @pl.when(head == heads - 1)
        def _():
            out_b[rows, :] = grad_q

        total[0, :, :width] += dot(query_t, dscores, 0, 0)
        total[1, :, :width] += dot(grad_t, probs.astype(BF), 0, 0)

    @pl.when(head == heads - 1)
    def _():
        half = DH // 2
        mine = spot[ZB]
        near = pl.ds(pl.multiple_of(mine * half, half), half)
        far = pl.ds(pl.multiple_of((1 - mine) * half, half), half)
        for index, factor in enumerate((scaling, 1.0)):
            keep[index] = total[index, near, :] * factor
            send[index] = (total[index, far, :] * factor).astype(BF)


def attend(spot, kv, queries, out_grads, stats, later):
    seq = queries.shape[0]
    heads = queries.shape[1] // DH
    cols = pl.BlockSpec((seq, DH), lambda head: (0, head))
    full = lambda a: pl.BlockSpec(a.shape, lambda head: (0,) * len(a.shape))
    outs = [
        shape((seq, (heads - 1) * DH)),
        shape((seq, DH)),
        shape((2, DH // 2, seq)),
        shape((2, DH // 2, seq), F32),
    ]
    return call(
        attend_kernel,
        "attend",
        spot,
        (kv, queries, out_grads, stats),
        [full(kv), cols, cols, full(stats)],
        outs,
        [
            pl.BlockSpec((seq, DH), lambda head: (0, jnp.minimum(head, heads - 2))),
            *[full(out) for out in outs[1:]],
        ],
        [
            pltpu.VMEM((DH, seq), BF),
            pltpu.VMEM((DH, seq), BF),
            pltpu.VMEM((2, DH, seq), F32),
        ],
        grid=(heads,),
        work=10**9,
        later=later,
    )


def middle_kernel(spot, keep, arrived, out, send):
    total = keep[...] + arrived[...].astype(F32)
    out[...] = total
    send[...] = total.astype(BF)


def middle(spot, keep, arrived, later, through):
    return call(
        middle_kernel,
        "kv_middle",
        spot,
        (keep, arrived),
        [VMEM] * 2,
        [shape(keep.shape, F32), shape(keep.shape)],
        [VMEM] * 2,
        later=later,
        through=through,
    )


def final_kv_kernel(spot, keep, arrived, out):
    total = keep[...] + arrived[...].astype(F32)
    out[...] = total.reshape(out.shape[1], out.shape[0]).T.astype(BF)


def final_kv(spot, keep, arrived, later, through):
    return call(
        final_kv_kernel,
        "kv_final",
        spot,
        (keep, arrived),
        [VMEM] * 2,
        [shape((keep.shape[2], keep.shape[0] * keep.shape[1]))],
        [VMEM],
        later=later,
        through=through,
    )


def offsets(pieces):
    starts, at = [], 0
    for piece in pieces:
        starts.append(at)
        at += piece.shape[1]
    return starts, at


def load_rows(aways, z, pieces, held, sems):
    starts, _ = offsets(pieces)
    rows = pieces[0].shape[0] // NZ
    copies = []
    for slot, away in enumerate(aways):
        row = pl.multiple_of(lax.rem(z + away + NZ, NZ) * rows, rows)
        for index, piece in enumerate(pieces):
            copies.append(
                pltpu.make_async_copy(
                    piece.at[pl.ds(row, rows), :],
                    held.at[pl.ds(slot * rows, rows), pl.ds(starts[index], piece.shape[1])],
                    sems.at[slot, index],
                )
            )
    return copies


def first_kernel(spot, weights, weights_kv, *rest):
    pieces, (last_up, last_down, up, down, held, sems, last_sems) = rest[:5], rest[5:]
    copies = load_rows((NZ // 2,), spot[Z], pieces, held, sems)
    wide = up.shape[1] // 2
    half, pair, _, cols = last_up.shape
    for index, (last, out, first) in enumerate(((last_up, up, 0), (last_down, down, half // 2))):
        for part in range(half // 2):
            for rep in range(pair):
                slot = part * pair + rep
                copies.append(
                    pltpu.make_async_copy(
                        last.at[first + part, rep],
                        out.at[:, pl.ds(wide + slot * cols, cols)],
                        last_sems.at[index, slot],
                    )
                )
    for copy in copies:
        copy.start()
    for copy in copies[: len(pieces)]:
        copy.wait()
    deep = weights.shape[1]
    left, left_kv = held[:, :deep], held[:, deep:]
    for index, out in enumerate((up, down)):
        part = slice(index * wide, (index + 1) * wide)
        out[:, :wide] = (
            dot(left, weights[part, :], 1, 1) + dot(left_kv, weights_kv[:, part], 1, 0)
        ).astype(BF)
    for copy in copies[len(pieces) :]:
        copy.wait()


def first_parts(spot, weights, weights_kv, pieces, last_up, last_down):
    rows = pieces[0].shape[0] // NZ
    width, deep = weights.shape
    depth = deep + weights_kv.shape[0]
    return call(
        first_kernel,
        "first_parts",
        spot,
        (weights, weights_kv, *pieces, last_up, last_down),
        [VMEM] * 2 + [ANY] * 7,
        [shape((rows, width))] * 2,
        [VMEM] * 2,
        [
            pltpu.VMEM((rows, depth), BF),
            pltpu.SemaphoreType.DMA((1, 5)),
            pltpu.SemaphoreType.DMA((2, 4)),
        ],
    )


def token_kernel(aways, spot, weights, weights_kv, *rest):
    pieces, (out, held, sems) = rest[:5], rest[5:]

    @pl.when(pl.program_id(0) == 0)
    def _():
        run_copies(load_rows(aways, spot[Z], pieces, held, sems))

    deep = weights.shape[1]
    total = dot(held[:, :deep], weights[...], 1, 1) + dot(held[:, deep:], weights_kv[...], 1, 0)
    out[...] = total.reshape(out.shape)


def token_parts(aways, spot, weights, weights_kv, pieces, later):
    rows = pieces[0].shape[0] // NZ
    width, deep = weights.shape
    depth = deep + weights_kv.shape[0]
    wide = 512
    return call(
        functools.partial(token_kernel, aways),
        "token_parts",
        spot,
        (weights, weights_kv, *pieces),
        [
            pl.BlockSpec((wide, deep), lambda step: (step, 0)),
            pl.BlockSpec((depth - deep, wide), lambda step: (0, step)),
            *[ANY] * 5,
        ],
        [shape((len(aways), rows, width), F32)],
        [pl.BlockSpec((len(aways), rows, wide), lambda step: (0, 0, step))],
        [
            pltpu.VMEM((len(aways) * rows, depth), BF),
            pltpu.SemaphoreType.DMA((len(aways), 5)),
        ],
        grid=(width // wide,),
        work=10**9,
        later=later,
    )[0]


def ring_kernel(kind, spot, up, down, ups, downs, *outs):
    wide = up.shape[1] // 2
    if kind == "first":
        for arrived, part, out, start in ((up, ups, outs[0], 0), (down, downs, outs[1], wide)):
            out[...] = part[0].astype(BF)
            cols = slice(start, start + wide)
            out[:, cols] = (part[0, :, cols] + arrived[:, :wide].astype(F32)).astype(BF)
    elif kind == "next":
        for arrived, part, out in ((up, ups, outs[0]), (down, downs, outs[1])):
            out[...] = (part[0] + arrived[...].astype(F32)).astype(BF)
    else:
        own, send = outs
        h = spot[H]
        rows = own.shape[0]
        for out, side in ((own, h), (send, 1 - h)):
            here = pl.ds(pl.multiple_of(side * rows, rows), rows)
            total = ups[0, here, :] + up[here, :].astype(F32) + down[here, :].astype(F32)
            out[...] = total.astype(BF)


def ring_step(kind, spot, up, down, parts, slots, later):
    _, rows, width = parts.shape
    whole = lambda a: pl.BlockSpec(a.shape, lambda step: (0,) * len(a.shape))
    term = [pl.BlockSpec((1, rows, width), lambda step, slot=slot: (slot, 0, 0)) for slot in slots]
    out = shape((rows // 2 if kind == "last" else rows, width))
    return call(
        functools.partial(ring_kernel, kind),
        "ring_step",
        spot,
        (up, down, parts, parts),
        [whole(up), whole(down), *term],
        [out] * 2,
        [whole(out)] * 2,
        grid=(1,),
        later=later,
    )


def wgrad_kernel(spot, *rest):
    blocks, (up, down), rest = rest[: NZ - 1], rest[NZ - 1 : NZ + 1], rest[NZ + 1 :]
    pieces, (out, held, lefts, sems, left_sems, last_sems) = rest[:10], rest[10:]
    starts, _ = offsets(pieces[:5])
    z = spot[Z]
    rows = blocks[0].shape[2]
    cols = blocks[0].shape[3]
    places = (0, -1, 1, -2, 2, -3, 3)

    @pl.when(pl.program_id(0) == 0)
    def _():
        def place(away):
            return pl.ds(pl.multiple_of(lax.rem(z + away + NZ, NZ) * rows, rows), rows)

        copies = [
            pltpu.make_async_copy(
                piece,
                held.at[index // 5, :, pl.ds(starts[index % 5], piece.shape[1])],
                sems.at[index],
            )
            for index, piece in enumerate(pieces)
        ]
        for index, (block, away) in enumerate(zip(blocks, places)):
            copies.append(
                pltpu.make_async_copy(
                    block, lefts.at[:, :, place(away), :], left_sems.at[index]
                )
            )
        for index, last in enumerate((up, down)):
            for slot in range(NX):
                copies.append(
                    pltpu.make_async_copy(
                        last.at[:, pl.ds(last.shape[1] // 2 + slot * cols, cols)],
                        lefts.at[index * (NX // 2) + slot // 2, slot % 2, place(NZ // 2), :],
                        last_sems.at[index, slot],
                    )
                )
        run_copies(copies)

    left = lefts[pl.program_id(0)]
    left = left.reshape(left.shape[0] * left.shape[1], left.shape[2])
    right = held[...].reshape(left.shape[0], held.shape[2])
    out[0] = dot(left, right, 0, 0).astype(out.dtype)


def wgrad_parts(spot, blocks, up, down, here, there, later):
    seq = here[0].shape[0]
    _, depth = offsets(here)
    wide = blocks[0].shape[3]
    return call(
        wgrad_kernel,
        "wgrad_parts",
        spot,
        (*blocks, up, down, *here, *there),
        [ANY] * (NZ + 11),
        [shape((NX, wide, depth))],
        [pl.BlockSpec((1, wide, depth), lambda step: (step, 0, 0))],
        [
            pltpu.VMEM((2, seq, depth), BF),
            pltpu.VMEM((NX, 2, seq, wide), BF),
            pltpu.SemaphoreType.DMA((10,)),
            pltpu.SemaphoreType.DMA((NZ - 1,)),
            pltpu.SemaphoreType.DMA((2, NX)),
        ],
        grid=(NX,),
        work=10**10,
        later=later,
    )[0]


def wgrad_sum_kernel(spot, terms, own, own_kv, send):
    total = terms[0].astype(F32)
    for index in range(1, terms.shape[0]):
        total += terms[index].astype(F32)
    q_w = own.shape[1]
    own[...] = total[:, :q_w]
    own_kv[...] = total[:, 2 * q_w :]
    send[...] = total[:, q_w:].astype(BF)


def wgrad_sum(spot, terms, q_w):
    _, rows, depth = terms.shape
    return call(
        wgrad_sum_kernel,
        "wgrad_sum",
        spot,
        (terms,),
        [VMEM],
        [shape((rows, q_w), F32), shape((rows, depth - 2 * q_w), F32), shape((rows, depth - q_w))],
        [VMEM] * 3,
    )


def wgrad_final_kernel(spot, own, own_kv, arrived, out, out_k, out_v, turned):
    h = spot[H]
    rows, q_w = own.shape
    kv_w = out_k.shape[0]
    near = pl.ds(pl.multiple_of(h * rows, rows), rows)
    far = pl.ds(pl.multiple_of((1 - h) * rows, rows), rows)
    out[near, :] = own[...]
    out[far, :] = arrived[:, :q_w].astype(F32)
    for cols, value in ((near, own_kv[...]), (far, arrived[:, q_w:].astype(F32))):
        turned[...] = value.T
        for index, to in enumerate((out_k, out_v)):
            start = pl.multiple_of((2 * index + h) * kv_w, kv_w)
            to[:, cols] = turned[pl.ds(start, kv_w), :]


def wgrad_final(spot, own, own_kv, arrived, kv_w):
    rows, q_w = own.shape
    return call(
        wgrad_final_kernel,
        "wgrad_final",
        spot,
        (own, own_kv, arrived),
        [VMEM] * 3,
        [shape((2 * rows, q_w), F32)] + [shape((kv_w, 2 * rows), F32)] * 2,
        [VMEM] * 3,
        [pltpu.VMEM((own_kv.shape[1], rows), F32)],
    )


def body(
    tokens,
    queries,
    saved_keys,
    saved_values,
    outputs,
    out_grads,
    log_norms,
    w_query,
    w_key,
    w_value,
):
    t = lax.axis_index("tensor")
    d = lax.axis_index("dp")
    h = t % 2
    spot = jnp.stack([t // 2, h, d % 2, d // 4, t // 2 % 2]).astype(jnp.int32)
    kv_w = saved_keys.shape[1]
    q_w = queries.shape[1]
    n_own = tokens.shape[0]
    heads4 = [[4 * k + j for j in range(4)] for k in range(4)]
    ring_x = [[r + 4 * k for k in range(NX)] for r in range(4)]
    plane = [[r + 2 * k for k in range(8)] for r in range(2)]

    w_key, w_value = w_key.T, w_value.T
    own, side, core, both, kv = pack(spot, tokens, saved_keys.T, saved_values.T)
    side = swap_quad(side, 0, 1)
    core = swap_quad(core, 1, 0)
    both = swap_quad(both, 1, 1)
    kv = lax.all_to_all(kv, "tensor", 0, 0, axis_index_groups=heads4, tiled=True)
    queries, out_grads, stats, w_send = prepare(
        spot, queries, out_grads, outputs, log_norms, w_query, w_key, w_value, [own]
    )
    w_side = swap(w_send, "tensor", 1)

    block = token_block(spot, (own, side, core, both), [stats])
    up1, down1 = shift(block, "tensor", 2), shift(block, "tensor", -2)
    own_a, own_b, kv_send, kv_keep = attend(spot, kv, queries, out_grads, stats, [block])
    far_a = swap(own_a, "tensor", 1)
    kv_z = swap(kv_send, "tensor", 2)
    up1, down1, own_b = tie(spot, [up1, down1, own_b], [])
    up2, down2 = shift(up1, "tensor", 2), shift(down1, "tensor", -2)
    w_side = repeat(spot, w_side, NX, [up1])
    w_far = lax.all_to_all(w_side, "dp", 0, 0, axis_index_groups=ring_x, tiled=True)
    kv_keep, kv_send = middle(spot, kv_keep, kv_z, [w_side], [])
    up2, down2, far_a, w_far, kv_send = tie(spot, [up2, down2, far_a, w_far, kv_send], [])
    up3, down3 = shift(up2, "tensor", 2), shift(down2, "tensor", -2)
    kv_y = swap(kv_send, "tensor", 1)
    far_b = swap(own_b, "tensor", 1)
    w_core = swap(w_far, "dp", 1)
    weights, weights_kv = gather_weights(spot, w_query, w_key, w_value, w_far, w_core, [])
    (kv_grad,) = final_kv(spot, kv_keep, kv_y, [weights_kv, far_b], [])
    here = [own_a, own_b, far_a, far_b, kv_grad]
    there = [swap(value, "dp", 1) for value in here]

    up, down = first_parts(spot, weights, weights_kv, here, up3, down3)
    up_next, down_next = shift(up, "tensor", 2), shift(down, "tensor", -2)
    last_up, last_down = up_next, down_next
    parts = token_parts((3, -3, 2, -2, 1, -1, 0), spot, weights, weights_kv, here, [up])
    up, down = ring_step("first", spot, up_next, down_next, parts, (0, 1), [])
    up_next, down_next = shift(up, "tensor", 2), shift(down, "tensor", -2)
    blocks = [block, up1, down1, up2, down2, up3, down3]
    terms = wgrad_parts(spot, blocks, last_up, last_down, here, there, [parts])
    for slots in ((2, 3), (4, 5)):
        up, down = ring_step("next", spot, up_next, down_next, parts, slots, [])
        up_next, down_next = shift(up, "tensor", 2), shift(down, "tensor", -2)
    mine, other = ring_step("last", spot, up_next, down_next, parts, (6, 6), [])
    other = swap(other, "tensor", 1)
    token_grads = jnp.where(
        h == 1,
        jnp.concatenate([other, mine], axis=1),
        jnp.concatenate([mine, other], axis=1),
    )

    terms = terms.reshape(8, DH, terms.shape[2])
    terms = lax.all_to_all(terms, "dp", 0, 0, axis_index_groups=plane, tiled=True)
    own, own_kv, send = wgrad_sum(spot, terms, q_w)
    query_wgrad, key_wgrad, value_wgrad = wgrad_final(
        spot, own, own_kv, swap(send, "tensor", 1), kv_w
    )
    return token_grads, query_wgrad, key_wgrad.T, value_wgrad.T


def solution(mesh):
    in_specs = (
        P(("dp", "tensor"), None),
        P("dp", "tensor"),
        P("dp", "tensor"),
        P("dp", "tensor"),
        P("dp", "tensor"),
        P("dp", "tensor"),
        P("tensor", "dp"),
        P(None, "tensor"),
        P(None, "tensor"),
        P(None, "tensor"),
    )
    out_specs = (P(("dp", "tensor"), None), P("dp", "tensor"), P("dp", "tensor"), P("dp", "tensor"))
    return jax.shard_map(body, mesh=mesh, in_specs=in_specs, out_specs=out_specs, check_vma=False)
```

time: 561 us -> 166 us (0.30)
  waiting for transfers between devices: 491 us -> 45.4 us
  starting transfers between devices: 5.8 us -> 51.7 us
  Pallas kernels: 0 us -> 37.3 us
  matrix products: 32.2 us -> 0 us
  local copies, waits for them, and re-layouts: 10.9 us -> 28.7 us
  between operations: 14 us -> 1.06 us
    reduce_scatter x2 -> x0, waiting for transfers between devices: 368 us -> none  [the longest x1 266 us: body(): lax.psum_scatter(lax.dot_general(grad_cols, weight_cols, (((1,), (1,)), (...]
    all_gather x1 -> x0, waiting for transfers between devices: 73.2 us -> none  [body(): replica_tokens = lax.all_gather(tokens, 'tensor', axis=0, tiled=True)]
    pallas_call x0 -> x19, Pallas kernels: none -> 37.3 us  [call(): pl.pallas_call(whole, grid=grid, in_specs=[SMEM, *specs, *[ANY] * (n_late...]
    dot_general x7 -> x0, matrix products: 32.2 us -> none  [the longest x1 10.9 us: body(): lax.dot_general(grad_cols, weight_cols, (((1,), (1,)), ((), ())), preferr...]
    ppermute x4 -> x30, starting transfers between devices: 5.68 us -> 34.9 us  [the longest x14 25.8 us: shift(): return lax.ppermute(value, axis, pairs)]
    unnamed x14 -> x84, local copies, waits for them, and re-layouts: 4.25 us -> 28.6 us
    all_to_all x0 -> x3, starting transfers between devices: none -> 16.8 us  [the longest x1 7.34 us: body(): lax.all_to_all(terms, 'dp', 0, 0, axis_index_groups=plane, tiled=True)]
    ppermute x4 -> x30, waiting for transfers between devices: 48.5 us -> 45.4 us  [the longest x14 25.4 us: shift(): return lax.ppermute(value, axis, pairs)]
  transfers between devices with their start and end apart: 7 -> 33, of which waited for: 7 -> 10; matrix products, arithmetic and copies ran while one was open for 7% -> 1% of each run, Pallas kernels for 0% -> 16%
where the time goes in v1:
time: 166 us; the launch traced here: 165 us
  starting transfers between devices  51.7 us (31%)
  waiting for transfers between devices  45.4 us (27%)
  Pallas kernels  37.3 us (22%)
  local copies, waits for them, and re-layouts  28.7 us (17%)
    pallas_call x19, Pallas kernels, call(): pl.pallas_call(whole, grid=grid, in_specs=[SMEM, *specs, *[ANY] * (n_late...  37.3 us
    unnamed x84, local copies, waits for them, and re-layouts  28.6 us
    ppermute x14, starting transfers between devices, shift(): return lax.ppermute(value, axis, pairs)  25.8 us
    ppermute x14, waiting for transfers between devices, shift(): return lax.ppermute(value, axis, pairs)  25.4 us
    ppermute x13, waiting for transfers between devices, swap(): return lax.ppermute(value, axis, pairs)  20 us
    all_to_all x1, starting transfers between devices, body(): lax.all_to_all(terms, 'dp', 0, 0, axis_index_groups=plane, tiled=True)  7.34 us
    ppermute x13, starting transfers between devices, swap(): return lax.ppermute(value, axis, pairs)  6.96 us
    all_to_all x1, starting transfers between devices, body(): lax.all_to_all(w_side, 'dp', 0, 0, axis_index_groups=ring_x, tiled=True)  4.82 us
  transfers between devices with their start and end apart: 33, of which 10 were waited for; matrix products, arithmetic and copies ran while one was open for 1% of the time, Pallas kernels for 16%

profile of v1, /device:TPU:26, one launch (start us, length us, event | category | flops | bytes accessed | tf_op | source)
XLA Modules:
  0.0 165.0 jit_solution(541842629596452331)
XLA Ops:
  0.8 1.0 copy-done.16
  3.4 1.4 pack.1
  4.8 4.6 %all-to-all-start = ((bf16[4,64,768]{2,1,0:T(8,128)(2,1)}), bf16[4,64,768]{2,1,0:T(8,128)(2,1)S(1)}, u32[]{:S(2)}, u32[]{:S(2)}) async-start(bf16[4,64,768]{2,1,0:T(8,128)(2,1)} %get-tuple-element.50), calls=%async_computation | async-start | bytes 786432 | tf_op jit(solution)/shard_map/all_to_all | solution.py:682
  9.4 2.1 %collective-permute-start.2 = (bf16[4,48,256]{2,1,0:T(8,128)(2,1)S(1)}, bf16[4,48,256]{2,1,0:T(8,128)(2,1)S(1)}, u32[]{:S(2)}, u32[]{:S(2)}) collective-permute-start(bf16[4,48,256]{2,1,0:T(8,128)(2,1)S(1)} %get-tuple-element.48), channel_id=1, source_target_pairs={{0,17},{1,16},{2,19},{3,18},{4,21},{5,20},{6,23},{7,22},{8,25},{9,... | collective-permute-start | bytes 294920 | tf_op jit(solution)/shard_map/ppermute | solution.py:39
  11.5 2.2 %copy-done.2 = bf16[4096,512]{1,0:T(8,128)(2,1)S(1)} copy-done((bf16[4096,512]{1,0:T(8,128)(2,1)S(1)}, bf16[4096,512]{1,0:T(8,128)(2,1)}, u32[]{:S(2)}) %copy-start.2) | copy-done | bytes 4194328
  15.6 1.1 copy-done.9
  16.8 1.1 copy-done.10
  17.9 1.1 copy-done.11
  19.7 1.2 prepare.1
  22.5 1.5 collective-permute-start.3
  24.0 4.5 %collective-permute-start.4 = (bf16[4,2,96,256]{3,2,1,0:T(8,128)(2,1)S(1)}, bf16[4,2,96,256]{3,2,1,0:T(8,128)(2,1)S(1)}, u32[]{:S(2)}, u32[]{:S(2)}) collective-permute-start(bf16[4,2,96,256]{3,2,1,0:T(8,128)(2,1)S(1)} %token_block.1.refs_5_.refs_1_), channel_id=1, source_target_pairs={{0,14},{1,15},{2,0},{3,1},{4,2},{5,3},{6,4},{7,5},{8,6},{9,7},{10,... | collective-permute-start | bytes 1179656 | tf_op jit(solution)/shard_map/ppermute | solution.py:26
  29.0 1.1 copy-done.38
  30.2 1.1 copy-done.40
  31.3 9.0 %attend.1 = (bf16[768,384]{1,0:T(8,128)(2,1)S(1)}, bf16[768,128]{1,0:T(8,128)(2,1)S(1)}, bf16[2,64,768]{2,1,0:T(8,128)(2,1)S(1)}, f32[2,64,768]{2,1,0:T(8,128)S(1)}) custom-call(s32[5]{0:T(128)S(1)} %stack.23.refs_0_, bf16[4,64,768]{2,1,0:T(8,128)(2,1)S(1)} %all-to-all-done.refs_1_, bf16[768,512]{1,0:T(8,128)(2,1)S(1)} %copy-done.38, ...), custom_call_target="tpu_custom_call" | custom-call | flops 1000000000 | tf_op jit(solution)/shard_map/attend/pallas_call | solution.py:65
  41.1 1.6 repeat.1.refs_3_
  42.7 4.8 %all-to-all-start.1 = ((bf16[4,288,512]{2,1,0:T(8,128)(2,1)}), bf16[4,288,512]{2,1,0:T(8,128)(2,1)S(1)}, u32[]{:S(2)}, u32[]{:S(2)}) async-start(bf16[4,288,512]{2,1,0:T(8,128)(2,1)} %repeat.1.refs_3_), calls=%async_computation.1 | async-start | bytes 2359296 | tf_op jit(solution)/shard_map/all_to_all | solution.py:696
  47.5 1.5 collective-permute-start.7
  49.1 3.2 %collective-permute-start.6 = (bf16[4,2,96,256]{3,2,1,0:T(8,128)(2,1)}, bf16[4,2,96,256]{3,2,1,0:T(8,128)(2,1)S(1)}, u32[]{:S(2)}, u32[]{:S(2)}) collective-permute-start(bf16[4,2,96,256]{3,2,1,0:T(8,128)(2,1)} %copy-done.14), channel_id=1, source_target_pairs={{0,14},{1,15},{2,0},{3,1},{4,2},{5,3},{6,4},{7,5},{8,6},{9,7},{10,... | collective-permute-start | bytes 1179656 | tf_op jit(solution)/shard_map/ppermute | solution.py:26
  52.3 10.8 %collective-permute-done.9.refs_2_ = bf16[2,64,768]{2,1,0:T(8,128)(2,1)S(1)} collective-permute-done((bf16[2,64,768]{2,1,0:T(8,128)(2,1)}, bf16[2,64,768]{2,1,0:T(8,128)(2,1)S(1)}, u32[]{:S(2)}, u32[]{:S(2)}) %collective-permute-start.9) | collective-permute-done | bytes 196640 | tf_op jit(solution)/shard_map/ppermute | solution.py:31
  63.1 1.0 copy-done.22
  67.7 1.0 copy-done.24
  68.7 1.0 copy-done.28
  73.2 3.2 %collective-permute-start.14 = (bf16[4,2,96,256]{3,2,1,0:T(8,128)(2,1)}, bf16[4,2,96,256]{3,2,1,0:T(8,128)(2,1)S(1)}, u32[]{:S(2)}, u32[]{:S(2)}) collective-permute-start(bf16[4,2,96,256]{3,2,1,0:T(8,128)(2,1)} %copy-done.29), channel_id=1, source_target_pairs={{0,14},{1,15},{2,0},{3,1},{4,2},{5,3},{6,4},{7,5},{8,6},{9,7},{10,... | collective-permute-start | bytes 1179656 | tf_op jit(solution)/shard_map/ppermute | solution.py:26
  76.4 1.5 collective-permute-start.12
  77.8 2.3 %collective-permute-done.11.refs_4_.refs_6_.refs_13_ = bf16[768,128]{1,0:T(8,128)(2,1)S(1)} collective-permute-done((bf16[768,128]{1,0:T(8,128)(2,1)S(1)}, bf16[768,128]{1,0:T(8,128)(2,1)S(1)}, u32[]{:S(2)}, u32[]{:S(2)}) %collective-permute-start.11) | collective-permute-done | bytes 196640 | tf_op jit(solution)/shard_map/ppermute | solution.py:31
  80.1 3.2 %collective-permute-done.12.refs_2_ = bf16[2,64,768]{2,1,0:T(8,128)(2,1)S(1)} collective-permute-done((bf16[2,64,768]{2,1,0:T(8,128)(2,1)}, bf16[2,64,768]{2,1,0:T(8,128)(2,1)S(1)}, u32[]{:S(2)}, u32[]{:S(2)}) %collective-permute-start.12) | collective-permute-done | bytes 196640 | tf_op jit(solution)/shard_map/ppermute | solution.py:31
  83.9 2.2 %copy-done.3 = bf16[4096,512]{1,0:T(8,128)(2,1)S(1)} copy-done((bf16[4096,512]{1,0:T(8,128)(2,1)S(1)}, bf16[4096,512]{1,0:T(8,128)(2,1)}, u32[]{:S(2)}) %copy-start.3) | copy-done | bytes 4194328
  86.1 1.5 gather_weights.1
  88.4 2.3 %first_parts.1 = (bf16[96,2048]{1,0:T(8,128)(2,1)S(1)}, bf16[96,2048]{1,0:T(8,128)(2,1)S(1)}) custom-call(s32[5]{0:T(128)S(1)} %stack.23.refs_0_, bf16[2048,1024]{1,0:T(8,128)(2,1)S(1)} %get-tuple-element.62.refs_1_, bf16[128,2048]{1,0:T(8,128)(2,1)S(1)} %get-tuple-element.63.refs_3_.refs_2_, bf16[768,384]{1,0:T(8,128)(2,1)S(1)} %get-tuple-element.56.refs_3_.refs_10_, ...), custom_call_target="tpu_custom_call" | custom-call | tf_op jit(solution)/shard_map/first_parts/pallas_call | solution.py:65
  90.9 3.2 %collective-permute-start.16 = (bf16[96,2048]{1,0:T(8,128)(2,1)S(1)}, bf16[96,2048]{1,0:T(8,128)(2,1)S(1)}, u32[]{:S(2)}, u32[]{:S(2)}) collective-permute-start(bf16[96,2048]{1,0:T(8,128)(2,1)S(1)} %get-tuple-element.71), channel_id=1, source_target_pairs={{0,14},{1,15},{2,0},{3,1},{4,2},{5,3},{6,4},{7,5},{8,6},{9,7},{10,... | collective-permute-start | bytes 1179656 | tf_op jit(solution)/shard_map/ppermute | solution.py:26
  94.1 5.8 %token_parts.1.refs_3_.refs_4_.refs_20_ = f32[7,96,2048]{2,1,0:T(8,128)S(1)} custom-call(s32[5]{0:T(128)S(1)} %stack.23.refs_0_, bf16[2048,1024]{1,0:T(8,128)(2,1)S(1)} %get-tuple-element.62.refs_1_, bf16[128,2048]{1,0:T(8,128)(2,1)S(1)} %get-tuple-element.63.refs_3_.refs_2_, bf16[768,384]{1,0:T(8,128)(2,1)S(1)} %get-tuple-element.56.refs_3_.refs_10_, ...), custom_call_target="tpu_custom_call" | custom-call | flops 1000000000 | tf_op jit(solution)/shard_map/token_parts/pallas_call | solution.py:65
  100.0 3.5 %collective-permute-done.15.refs_1_.refs_8_ = bf16[96,2048]{1,0:T(8,128)(2,1)S(1)} collective-permute-done((bf16[96,2048]{1,0:T(8,128)(2,1)S(1)}, bf16[96,2048]{1,0:T(8,128)(2,1)S(1)}, u32[]{:S(2)}, u32[]{:S(2)}) %collective-permute-start.15) | collective-permute-done | bytes 393248 | tf_op jit(solution)/shard_map/ppermute | solution.py:26
  103.8 6.7 %wgrad_parts.1 = bf16[4,256,1152]{2,1,0:T(8,128)(2,1)S(1)} custom-call(s32[5]{0:T(128)S(1)} %stack.23.refs_0_, bf16[4,2,96,256]{3,2,1,0:T(8,128)(2,1)S(1)} %copy-done.18, bf16[4,2,96,256]{3,2,1,0:T(8,128)(2,1)S(1)} %get-tuple-element.54.refs_2_, bf16[4,2,96,256]{3,2,1,0:T(8,128)(2,1)S(1)} %copy-done.15, bf16[4,2,96,256]{3,2,1,0:T(8,128)(2,1)S(1)} %copy-done.26, ...), custom_call_target="tpu_custom_call" | custom-call | flops 10000000000 | tf_op jit(solution)/shard_map/wgrad_parts/pallas_call | solution.py:65
  110.5 1.4 copy-done.4
  112.0 7.3 %all-to-all-start.2 = ((bf16[8,128,1152]{2,1,0:T(8,128)(2,1)}), bf16[8,128,1152]{2,1,0:T(8,128)(2,1)S(1)}, u32[]{:S(2)}, u32[]{:S(2)}) async-start(bf16[8,128,1152]{2,1,0:T(8,128)(2,1)} %bitcast.12), calls=%async_computation.2 | async-start | bytes 4718592 | tf_op jit(solution)/shard_map/all_to_all | solution.py:728
  119.3 2.6 %copy-done.1 = f32[7,96,2048]{2,1,0:T(8,128)S(1)} copy-done((f32[7,96,2048]{2,1,0:T(8,128)S(1)}, f32[7,96,2048]{2,1,0:T(8,128)}, u32[]{:S(2)}) %copy-start.1) | copy-done | bytes 5505048
  122.5 1.8 %collective-permute-start.17 = (bf16[96,2048]{1,0:T(8,128)(2,1)S(1)}, bf16[96,2048]{1,0:T(8,128)(2,1)S(1)}, u32[]{:S(2)}, u32[]{:S(2)}) collective-permute-start(bf16[96,2048]{1,0:T(8,128)(2,1)S(1)} %get-tuple-element.72), channel_id=1, source_target_pairs={{0,2},{1,3},{2,4},{3,5},{4,6},{5,7},{6,8},{7,9},{8,10},{9,11},{10,... | collective-permute-start | bytes 1179656 | tf_op jit(solution)/shard_map/ppermute | solution.py:26
  124.3 1.5 collective-permute-start.18
  125.8 8.1 %collective-permute-done.17.refs_1_ = bf16[96,2048]{1,0:T(8,128)(2,1)S(1)} collective-permute-done((bf16[96,2048]{1,0:T(8,128)(2,1)S(1)}, bf16[96,2048]{1,0:T(8,128)(2,1)S(1)}, u32[]{:S(2)}, u32[]{:S(2)}) %collective-permute-start.17) | collective-permute-done | bytes 393248 | tf_op jit(solution)/shard_map/ppermute | solution.py:26
  134.6 1.5 collective-permute-start.19
  136.1 1.9 %collective-permute-start.20 = (bf16[96,2048]{1,0:T(8,128)(2,1)S(1)}, bf16[96,2048]{1,0:T(8,128)(2,1)S(1)}, u32[]{:S(2)}, u32[]{:S(2)}) collective-permute-start(bf16[96,2048]{1,0:T(8,128)(2,1)S(1)} %get-tuple-element.75), channel_id=1, source_target_pairs={{0,14},{1,15},{2,0},{3,1},{4,2},{5,3},{6,4},{7,5},{8,6},{9,7},{10,... | collective-permute-start | bytes 1179656 | tf_op jit(solution)/shard_map/ppermute | solution.py:26
  138.0 7.2 %collective-permute-done.19.refs_1_ = bf16[96,2048]{1,0:T(8,128)(2,1)S(1)} collective-permute-done((bf16[96,2048]{1,0:T(8,128)(2,1)S(1)}, bf16[96,2048]{1,0:T(8,128)(2,1)S(1)}, u32[]{:S(2)}, u32[]{:S(2)}) %collective-permute-start.19) | collective-permute-done | bytes 393248 | tf_op jit(solution)/shard_map/ppermute | solution.py:26
  145.8 1.4 collective-permute-start.21
  147.2 1.9 %collective-permute-start.22 = (bf16[96,2048]{1,0:T(8,128)(2,1)S(1)}, bf16[96,2048]{1,0:T(8,128)(2,1)S(1)}, u32[]{:S(2)}, u32[]{:S(2)}) collective-permute-start(bf16[96,2048]{1,0:T(8,128)(2,1)S(1)} %get-tuple-element.77), channel_id=1, source_target_pairs={{0,14},{1,15},{2,0},{3,1},{4,2},{5,3},{6,4},{7,5},{8,6},{9,7},{10,... | collective-permute-start | bytes 1179656 | tf_op jit(solution)/shard_map/ppermute | solution.py:26
  149.2 6.3 %collective-permute-done.21.refs_1_ = bf16[96,2048]{1,0:T(8,128)(2,1)S(1)} collective-permute-done((bf16[96,2048]{1,0:T(8,128)(2,1)S(1)}, bf16[96,2048]{1,0:T(8,128)(2,1)S(1)}, u32[]{:S(2)}, u32[]{:S(2)}) %collective-permute-start.21) | collective-permute-done | bytes 393248 | tf_op jit(solution)/shard_map/ppermute | solution.py:26
  157.5 1.7 %collective-permute-start.29 = (bf16[128,640]{1,0:T(8,128)(2,1)S(1)}, bf16[128,640]{1,0:T(8,128)(2,1)S(1)}, u32[]{:S(2)}, u32[]{:S(2)}) collective-permute-start(bf16[128,640]{1,0:T(8,128)(2,1)S(1)} %get-tuple-element.82), channel_id=1, source_target_pairs={{0,1},{1,0},{2,3},{3,2},{4,5},{5,4},{6,7},{7,6},{8,9},{9,8},{10,11... | collective-permute-start | bytes 491528 | tf_op jit(solution)/shard_map/ppermute | solution.py:31
  159.2 2.7 %collective-permute-done.23 = bf16[48,2048]{1,0:T(8,128)(2,1)S(1)} collective-permute-done((bf16[48,2048]{1,0:T(8,128)(2,1)S(1)}, bf16[48,2048]{1,0:T(8,128)(2,1)S(1)}, u32[]{:S(2)}, u32[]{:S(2)}) %collective-permute-start.23) | collective-permute-done | bytes 196640 | tf_op jit(solution)/shard_map/ppermute | solution.py:31
  163.6 1.4 wgrad_final.1
  (123 shorter events, 21.7 us)
Async XLA Ops:
  4.8 24.3 %all-to-all-start = ((bf16[4,64,768]{2,1,0:T(8,128)(2,1)}), bf16[4,64,768]{2,1,0:T(8,128)(2,1)S(1)}, u32[]{:S(2)}, u32[]{:S(2)}) async-start(bf16[4,64,768]{2,1,0:T(8,128)(2,1)} %get-tuple-element.50), calls=%async_computation | async-start | bytes 786432 | tf_op jit(solution)/shard_map/all_to_all | solution.py:682
  9.4 12.4 %collective-permute-start = (bf16[4,48,256]{2,1,0:T(8,128)(2,1)S(1)}, bf16[4,48,256]{2,1,0:T(8,128)(2,1)S(1)}, u32[]{:S(2)}, u32[]{:S(2)}) collective-permute-start(bf16[4,48,256]{2,1,0:T(8,128)(2,1)S(1)} %get-tuple-element.46), channel_id=1, source_target_pairs={{0,1},{1,0},{2,3},{3,2},{4,5},{5,4},{6,7},{7,6},{8,9},{9,8},{10,11... | collective-permute-start | bytes 294920 | tf_op jit(solution)/shard_map/ppermute | solution.py:39
  9.4 12.4 %collective-permute-start.1 = (bf16[4,48,256]{2,1,0:T(8,128)(2,1)S(1)}, bf16[4,48,256]{2,1,0:T(8,128)(2,1)S(1)}, u32[]{:S(2)}, u32[]{:S(2)}) collective-permute-start(bf16[4,48,256]{2,1,0:T(8,128)(2,1)S(1)} %get-tuple-element.47), channel_id=1, source_target_pairs={{0,16},{1,17},{2,18},{3,19},{4,20},{5,21},{6,22},{7,23},{8,24},{9,... | collective-permute-start | bytes 294920 | tf_op jit(solution)/shard_map/ppermute | solution.py:39
  9.4 12.4 %collective-permute-start.2 = (bf16[4,48,256]{2,1,0:T(8,128)(2,1)S(1)}, bf16[4,48,256]{2,1,0:T(8,128)(2,1)S(1)}, u32[]{:S(2)}, u32[]{:S(2)}) collective-permute-start(bf16[4,48,256]{2,1,0:T(8,128)(2,1)S(1)} %get-tuple-element.48), channel_id=1, source_target_pairs={{0,17},{1,16},{2,19},{3,18},{4,21},{5,20},{6,23},{7,22},{8,25},{9,... | collective-permute-start | bytes 294920 | tf_op jit(solution)/shard_map/ppermute | solution.py:39
  11.5 2.2 %copy-start.2 = (bf16[4096,512]{1,0:T(8,128)(2,1)S(1)}, bf16[4096,512]{1,0:T(8,128)(2,1)}, u32[]{:S(2)}) copy-start(bf16[4096,512]{1,0:T(8,128)(2,1)} %refs_1_.5) | copy-start | bytes 12582916
  21.8 6.6 %copy-start.37 = (bf16[768,512]{1,0:T(8,128)(2,1)}, bf16[768,512]{1,0:T(8,128)(2,1)S(1)}, u32[]{:S(2)}) copy-start(bf16[768,512]{1,0:T(8,128)(2,1)S(1)} %get-tuple-element.51.refs_2_) | copy-start | bytes 2359300
  22.5 20.3 %copy-start.17 = (bf16[4,2,96,256]{3,2,1,0:T(8,128)(2,1)}, bf16[4,2,96,256]{3,2,1,0:T(8,128)(2,1)S(1)}, u32[]{:S(2)}) copy-start(bf16[4,2,96,256]{3,2,1,0:T(8,128)(2,1)S(1)} %token_block.1.refs_5_.refs_1_) | copy-start | bytes 1179652
  22.5 17.8 %collective-permute-start.3 = (bf16[4,2,96,256]{3,2,1,0:T(8,128)(2,1)S(1)}, bf16[4,2,96,256]{3,2,1,0:T(8,128)(2,1)S(1)}, u32[]{:S(2)}, u32[]{:S(2)}) collective-permute-start(bf16[4,2,96,256]{3,2,1,0:T(8,128)(2,1)S(1)} %token_block.1.refs_5_.refs_1_), channel_id=1, source_target_pairs={{0,2},{1,3},{2,4},{3,5},{4,6},{5,7},{6,8},{7,9},{8,10},{9,11},{10,... | collective-permute-start | bytes 1179656 | tf_op jit(solution)/shard_map/ppermute | solution.py:26
  24.0 16.3 %collective-permute-start.4 = (bf16[4,2,96,256]{3,2,1,0:T(8,128)(2,1)S(1)}, bf16[4,2,96,256]{3,2,1,0:T(8,128)(2,1)S(1)}, u32[]{:S(2)}, u32[]{:S(2)}) collective-permute-start(bf16[4,2,96,256]{3,2,1,0:T(8,128)(2,1)S(1)} %token_block.1.refs_5_.refs_1_), channel_id=1, source_target_pairs={{0,14},{1,15},{2,0},{3,1},{4,2},{5,3},{6,4},{7,5},{8,6},{9,7},{10,... | collective-permute-start | bytes 1179656 | tf_op jit(solution)/shard_map/ppermute | solution.py:26
  28.5 12.6 %collective-permute-start.8 = (bf16[288,512]{1,0:T(8,128)(2,1)S(1)}, bf16[288,512]{1,0:T(8,128)(2,1)S(1)}, u32[]{:S(2)}, u32[]{:S(2)}) collective-permute-start(bf16[288,512]{1,0:T(8,128)(2,1)S(1)} %get-tuple-element.57), channel_id=1, source_target_pairs={{0,1},{1,0},{2,3},{3,2},{4,5},{5,4},{6,7},{7,6},{8,9},{9,8},{10,11... | collective-permute-start | bytes 884744 | tf_op jit(solution)/shard_map/ppermute | solution.py:31
  41.0 6.5 %copy-start.14 = (bf16[4,2,96,256]{3,2,1,0:T(8,128)(2,1)}, bf16[4,2,96,256]{3,2,1,0:T(8,128)(2,1)S(1)}, u32[]{:S(2)}) copy-start(bf16[4,2,96,256]{3,2,1,0:T(8,128)(2,1)S(1)} %get-tuple-element.55.refs_3_) | copy-start | bytes 1179652
  42.7 25.0 %all-to-all-start.1 = ((bf16[4,288,512]{2,1,0:T(8,128)(2,1)}), bf16[4,288,512]{2,1,0:T(8,128)(2,1)S(1)}, u32[]{:S(2)}, u32[]{:S(2)}) async-start(bf16[4,288,512]{2,1,0:T(8,128)(2,1)} %repeat.1.refs_3_), calls=%async_computation.1 | async-start | bytes 2359296 | tf_op jit(solution)/shard_map/all_to_all | solution.py:696
  47.5 36.3 %copy-start.6 = (bf16[4096,32]{0,1:T(8,128)(2,1)S(1)}, bf16[4096,32]{0,1:T(8,128)(2,1)}, u32[]{:S(2)}) copy-start(bf16[4096,32]{0,1:T(8,128)(2,1)} %param.18) | copy-start | bytes 786436
  47.5 36.3 %copy-start.8 = (bf16[4096,32]{0,1:T(8,128)(2,1)S(1)}, bf16[4096,32]{0,1:T(8,128)(2,1)}, u32[]{:S(2)}) copy-start(bf16[4096,32]{0,1:T(8,128)(2,1)} %param.19) | copy-start | bytes 786436
  47.5 20.1 %collective-permute-start.7 = (bf16[768,384]{1,0:T(8,128)(2,1)S(1)}, bf16[768,384]{1,0:T(8,128)(2,1)S(1)}, u32[]{:S(2)}, u32[]{:S(2)}) collective-permute-start(bf16[768,384]{1,0:T(8,128)(2,1)S(1)} %get-tuple-element.56.refs_3_.refs_10_), channel_id=1, source_target_pairs={{0,1},{1,0},{2,3},{3,2},{4,5},{5,4},{6,7},{7,6},{8,9},{9,8},{10,11... | collective-permute-start | bytes 1769480 | tf_op jit(solution)/shard_map/ppermute | solution.py:31
  49.1 17.1 %collective-permute-start.5 = (bf16[4,2,96,256]{3,2,1,0:T(8,128)(2,1)S(1)}, bf16[4,2,96,256]{3,2,1,0:T(8,128)(2,1)S(1)}, u32[]{:S(2)}, u32[]{:S(2)}) collective-permute-start(bf16[4,2,96,256]{3,2,1,0:T(8,128)(2,1)S(1)} %get-tuple-element.54.refs_2_), channel_id=1, source_target_pairs={{0,2},{1,3},{2,4},{3,5},{4,6},{5,7},{6,8},{7,9},{8,10},{9,11},{10,... | collective-permute-start | bytes 1179656 | tf_op jit(solution)/shard_map/ppermute | solution.py:26
  49.1 17.1 %collective-permute-start.6 = (bf16[4,2,96,256]{3,2,1,0:T(8,128)(2,1)}, bf16[4,2,96,256]{3,2,1,0:T(8,128)(2,1)S(1)}, u32[]{:S(2)}, u32[]{:S(2)}) collective-permute-start(bf16[4,2,96,256]{3,2,1,0:T(8,128)(2,1)} %copy-done.14), channel_id=1, source_target_pairs={{0,14},{1,15},{2,0},{3,1},{4,2},{5,3},{6,4},{7,5},{8,6},{9,7},{10,... | collective-permute-start | bytes 1179656 | tf_op jit(solution)/shard_map/ppermute | solution.py:26
  52.3 10.8 %collective-permute-start.9 = (bf16[2,64,768]{2,1,0:T(8,128)(2,1)}, bf16[2,64,768]{2,1,0:T(8,128)(2,1)S(1)}, u32[]{:S(2)}, u32[]{:S(2)}) collective-permute-start(bf16[2,64,768]{2,1,0:T(8,128)(2,1)} %copy-done.41), channel_id=1, source_target_pairs={{0,2},{1,3},{2,0},{3,1},{4,6},{5,7},{6,4},{7,5},{8,10},{9,11},{10,... | collective-permute-start | bytes 589832 | tf_op jit(solution)/shard_map/ppermute | solution.py:31
  71.8 11.5 %collective-permute-start.10 = (bf16[4,288,512]{2,1,0:T(8,128)(2,1)S(1)}, bf16[4,288,512]{2,1,0:T(8,128)(2,1)S(1)}, u32[]{:S(2)}, u32[]{:S(2)}) collective-permute-start(bf16[4,288,512]{2,1,0:T(8,128)(2,1)S(1)} %get-tuple-element.61.refs_4_), channel_id=1, source_target_pairs={{0,16},{16,0},{32,48},{48,32},{64,80},{80,64},{96,112},{112,96},{1... | collective-permute-start | bytes 3538952 | tf_op jit(solution)/shard_map/ppermute | solution.py:31
  72.6 7.5 %collective-permute-start.11 = (bf16[768,128]{1,0:T(8,128)(2,1)S(1)}, bf16[768,128]{1,0:T(8,128)(2,1)S(1)}, u32[]{:S(2)}, u32[]{:S(2)}) collective-permute-start(bf16[768,128]{1,0:T(8,128)(2,1)S(1)} %get-tuple-element.64.refs_4_.refs_11_), channel_id=1, source_target_pairs={{0,1},{1,0},{2,3},{3,2},{4,5},{5,4},{6,7},{7,6},{8,9},{9,8},{10,11... | collective-permute-start | bytes 589832 | tf_op jit(solution)/shard_map/ppermute | solution.py:31
  73.1 15.1 %collective-permute-start.13 = (bf16[4,2,96,256]{3,2,1,0:T(8,128)(2,1)}, bf16[4,2,96,256]{3,2,1,0:T(8,128)(2,1)S(1)}, u32[]{:S(2)}, u32[]{:S(2)}) collective-permute-start(bf16[4,2,96,256]{3,2,1,0:T(8,128)(2,1)} %copy-done.25), channel_id=1, source_target_pairs={{0,2},{1,3},{2,4},{3,5},{4,6},{5,7},{6,8},{7,9},{8,10},{9,11},{10,... | collective-permute-start | bytes 1179656 | tf_op jit(solution)/shard_map/ppermute | solution.py:26
  73.2 15.2 %collective-permute-start.14 = (bf16[4,2,96,256]{3,2,1,0:T(8,128)(2,1)}, bf16[4,2,96,256]{3,2,1,0:T(8,128)(2,1)S(1)}, u32[]{:S(2)}, u32[]{:S(2)}) collective-permute-start(bf16[4,2,96,256]{3,2,1,0:T(8,128)(2,1)} %copy-done.29), channel_id=1, source_target_pairs={{0,14},{1,15},{2,0},{3,1},{4,2},{5,3},{6,4},{7,5},{8,6},{9,7},{10,... | collective-permute-start | bytes 1179656 | tf_op jit(solution)/shard_map/ppermute | solution.py:26
  76.4 7.0 %collective-permute-start.12 = (bf16[2,64,768]{2,1,0:T(8,128)(2,1)}, bf16[2,64,768]{2,1,0:T(8,128)(2,1)S(1)}, u32[]{:S(2)}, u32[]{:S(2)}) collective-permute-start(bf16[2,64,768]{2,1,0:T(8,128)(2,1)} %copy-done.33), channel_id=1, source_target_pairs={{0,1},{1,0},{2,3},{3,2},{4,5},{5,4},{6,7},{7,6},{8,9},{9,8},{10,11... | collective-permute-start | bytes 589832 | tf_op jit(solution)/shard_map/ppermute | solution.py:31
  80.1 19.8 %collective-permute-start.24 = (bf16[768,384]{1,0:T(8,128)(2,1)S(1)}, bf16[768,384]{1,0:T(8,128)(2,1)S(1)}, u32[]{:S(2)}, u32[]{:S(2)}) collective-permute-start(bf16[768,384]{1,0:T(8,128)(2,1)S(1)} %get-tuple-element.56.refs_3_.refs_10_), channel_id=1, source_target_pairs={{0,16},{16,0},{32,48},{48,32},{64,80},{80,64},{96,112},{112,96},{1... | collective-permute-start | bytes 1769480 | tf_op jit(solution)/shard_map/ppermute | solution.py:31
  83.3 16.6 %collective-permute-start.26 = (bf16[768,384]{1,0:T(8,128)(2,1)S(1)}, bf16[768,384]{1,0:T(8,128)(2,1)S(1)}, u32[]{:S(2)}, u32[]{:S(2)}) collective-permute-start(bf16[768,384]{1,0:T(8,128)(2,1)S(1)} %get-tuple-element.65.refs_5_.refs_12_), channel_id=1, source_target_pairs={{0,16},{16,0},{32,48},{48,32},{64,80},{80,64},{96,112},{112,96},{1... | collective-permute-start | bytes 1769480 | tf_op jit(solution)/shard_map/ppermute | solution.py:31
  83.4 7.5 %collective-permute-start.25 = (bf16[768,128]{1,0:T(8,128)(2,1)S(1)}, bf16[768,128]{1,0:T(8,128)(2,1)S(1)}, u32[]{:S(2)}, u32[]{:S(2)}) collective-permute-start(bf16[768,128]{1,0:T(8,128)(2,1)S(1)} %get-tuple-element.64.refs_4_.refs_11_), channel_id=1, source_target_pairs={{0,16},{16,0},{32,48},{48,32},{64,80},{80,64},{96,112},{112,96},{1... | collective-permute-start | bytes 589832 | tf_op jit(solution)/shard_map/ppermute | solution.py:31
  83.9 2.2 %copy-start.3 = (bf16[4096,512]{1,0:T(8,128)(2,1)S(1)}, bf16[4096,512]{1,0:T(8,128)(2,1)}, u32[]{:S(2)}) copy-start(bf16[4096,512]{1,0:T(8,128)(2,1)} %refs_1_.5) | copy-start | bytes 12582916
  88.3 5.8 %collective-permute-start.27 = (bf16[768,128]{1,0:T(8,128)(2,1)S(1)}, bf16[768,128]{1,0:T(8,128)(2,1)S(1)}, u32[]{:S(2)}, u32[]{:S(2)}) collective-permute-start(bf16[768,128]{1,0:T(8,128)(2,1)S(1)} %collective-permute-done.11.refs_4_.refs_6_.refs_13_), channel_id=1, source_target_pairs={{0,16},{16,0},{32,48},{48,32},{64,80},{80,64},{96,112},{112,96},{1... | collective-permute-start | bytes 589832 | tf_op jit(solution)/shard_map/ppermute | solution.py:31
  90.7 12.8 %collective-permute-start.15 = (bf16[96,2048]{1,0:T(8,128)(2,1)S(1)}, bf16[96,2048]{1,0:T(8,128)(2,1)S(1)}, u32[]{:S(2)}, u32[]{:S(2)}) collective-permute-start(bf16[96,2048]{1,0:T(8,128)(2,1)S(1)} %get-tuple-element.70.refs_8_), channel_id=1, source_target_pairs={{0,2},{1,3},{2,4},{3,5},{4,6},{5,7},{6,8},{7,9},{8,10},{9,11},{10,... | collective-permute-start | bytes 1179656 | tf_op jit(solution)/shard_map/ppermute | solution.py:26
  90.8 12.9 %copy-start.15 = (bf16[4,2,96,256]{3,2,1,0:T(8,128)(2,1)S(1)}, bf16[4,2,96,256]{3,2,1,0:T(8,128)(2,1)}, u32[]{:S(2)}) copy-start(bf16[4,2,96,256]{3,2,1,0:T(8,128)(2,1)} %copy-done.14) | copy-start | bytes 1179652
  90.8 12.9 %copy-start.18 = (bf16[4,2,96,256]{3,2,1,0:T(8,128)(2,1)S(1)}, bf16[4,2,96,256]{3,2,1,0:T(8,128)(2,1)}, u32[]{:S(2)}) copy-start(bf16[4,2,96,256]{3,2,1,0:T(8,128)(2,1)} %copy-done.17) | copy-start | bytes 1179652
  90.9 12.9 %copy-start.26 = (bf16[4,2,96,256]{3,2,1,0:T(8,128)(2,1)S(1)}, bf16[4,2,96,256]{3,2,1,0:T(8,128)(2,1)}, u32[]{:S(2)}) copy-start(bf16[4,2,96,256]{3,2,1,0:T(8,128)(2,1)} %copy-done.25) | copy-start | bytes 1179652
  90.9 12.9 %copy-start.30 = (bf16[4,2,96,256]{3,2,1,0:T(8,128)(2,1)S(1)}, bf16[4,2,96,256]{3,2,1,0:T(8,128)(2,1)}, u32[]{:S(2)}) copy-start(bf16[4,2,96,256]{3,2,1,0:T(8,128)(2,1)} %copy-done.29) | copy-start | bytes 1179652
  90.9 12.9 %collective-permute-start.16 = (bf16[96,2048]{1,0:T(8,128)(2,1)S(1)}, bf16[96,2048]{1,0:T(8,128)(2,1)S(1)}, u32[]{:S(2)}, u32[]{:S(2)}) collective-permute-start(bf16[96,2048]{1,0:T(8,128)(2,1)S(1)} %get-tuple-element.71), channel_id=1, source_target_pairs={{0,14},{1,15},{2,0},{3,1},{4,2},{5,3},{6,4},{7,5},{8,6},{9,7},{10,... | collective-permute-start | bytes 1179656 | tf_op jit(solution)/shard_map/ppermute | solution.py:26
  94.1 5.8 %collective-permute-start.28 = (bf16[768,128]{1,0:T(8,128)(2,1)S(1)}, bf16[768,128]{1,0:T(8,128)(2,1)S(1)}, u32[]{:S(2)}, u32[]{:S(2)}) collective-permute-start(bf16[768,128]{1,0:T(8,128)(2,1)S(1)} %kv_final.1.refs_7_.refs_14_), channel_id=1, source_target_pairs={{0,16},{16,0},{32,48},{48,32},{64,80},{80,64},{96,112},{112,96},{1... | collective-permute-start | bytes 589832 | tf_op jit(solution)/shard_map/ppermute | solution.py:31
  99.9 10.6 %copy-start = (f32[7,96,2048]{2,1,0:T(8,128)}, f32[7,96,2048]{2,1,0:T(8,128)S(1)}, u32[]{:S(2)}) copy-start(f32[7,96,2048]{2,1,0:T(8,128)S(1)} %token_parts.1.refs_3_.refs_4_.refs_20_) | copy-start | bytes 16515076
  103.8 6.7 %copy-start.12 = (bf16[96,2048]{1,0:T(8,128)(2,1)}, bf16[96,2048]{1,0:T(8,128)(2,1)S(1)}, u32[]{:S(2)}) copy-start(bf16[96,2048]{1,0:T(8,128)(2,1)S(1)} %collective-permute-done.16.refs_2_.refs_9_) | copy-start | bytes 1179652
  112.0 7.3 %copy-start.13 = (bf16[96,2048]{1,0:T(8,128)(2,1)S(1)}, bf16[96,2048]{1,0:T(8,128)(2,1)}, u32[]{:S(2)}) copy-start(bf16[96,2048]{1,0:T(8,128)(2,1)} %copy-done.12) | copy-start | bytes 1179652
  112.0 44.7 %all-to-all-start.2 = ((bf16[8,128,1152]{2,1,0:T(8,128)(2,1)}), bf16[8,128,1152]{2,1,0:T(8,128)(2,1)S(1)}, u32[]{:S(2)}, u32[]{:S(2)}) async-start(bf16[8,128,1152]{2,1,0:T(8,128)(2,1)} %bitcast.12), calls=%async_computation.2 | async-start | bytes 4718592 | tf_op jit(solution)/shard_map/all_to_all | solution.py:728
  119.3 2.6 %copy-start.1 = (f32[7,96,2048]{2,1,0:T(8,128)S(1)}, f32[7,96,2048]{2,1,0:T(8,128)}, u32[]{:S(2)}) copy-start(f32[7,96,2048]{2,1,0:T(8,128)} %copy-done) | copy-start | bytes 16515076
  122.5 11.4 %collective-permute-start.17 = (bf16[96,2048]{1,0:T(8,128)(2,1)S(1)}, bf16[96,2048]{1,0:T(8,128)(2,1)S(1)}, u32[]{:S(2)}, u32[]{:S(2)}) collective-permute-start(bf16[96,2048]{1,0:T(8,128)(2,1)S(1)} %get-tuple-element.72), channel_id=1, source_target_pairs={{0,2},{1,3},{2,4},{3,5},{4,6},{5,7},{6,8},{7,9},{8,10},{9,11},{10,... | collective-permute-start | bytes 1179656 | tf_op jit(solution)/shard_map/ppermute | solution.py:26
  124.3 9.7 %collective-permute-start.18 = (bf16[96,2048]{1,0:T(8,128)(2,1)S(1)}, bf16[96,2048]{1,0:T(8,128)(2,1)S(1)}, u32[]{:S(2)}, u32[]{:S(2)}) collective-permute-start(bf16[96,2048]{1,0:T(8,128)(2,1)S(1)} %get-tuple-element.73), channel_id=1, source_target_pairs={{0,14},{1,15},{2,0},{3,1},{4,2},{5,3},{6,4},{7,5},{8,6},{9,7},{10,... | collective-permute-start | bytes 1179656 | tf_op jit(solution)/shard_map/ppermute | solution.py:26
  134.6 10.5 %collective-permute-start.19 = (bf16[96,2048]{1,0:T(8,128)(2,1)S(1)}, bf16[96,2048]{1,0:T(8,128)(2,1)S(1)}, u32[]{:S(2)}, u32[]{:S(2)}) collective-permute-start(bf16[96,2048]{1,0:T(8,128)(2,1)S(1)} %get-tuple-element.74), channel_id=1, source_target_pairs={{0,2},{1,3},{2,4},{3,5},{4,6},{5,7},{6,8},{7,9},{8,10},{9,11},{10,... | collective-permute-start | bytes 1179656 | tf_op jit(solution)/shard_map/ppermute | solution.py:26
  136.1 9.0 %collective-permute-start.20 = (bf16[96,2048]{1,0:T(8,128)(2,1)S(1)}, bf16[96,2048]{1,0:T(8,128)(2,1)S(1)}, u32[]{:S(2)}, u32[]{:S(2)}) collective-permute-start(bf16[96,2048]{1,0:T(8,128)(2,1)S(1)} %get-tuple-element.75), channel_id=1, source_target_pairs={{0,14},{1,15},{2,0},{3,1},{4,2},{5,3},{6,4},{7,5},{8,6},{9,7},{10,... | collective-permute-start | bytes 1179656 | tf_op jit(solution)/shard_map/ppermute | solution.py:26
  145.8 9.6 %collective-permute-start.21 = (bf16[96,2048]{1,0:T(8,128)(2,1)S(1)}, bf16[96,2048]{1,0:T(8,128)(2,1)S(1)}, u32[]{:S(2)}, u32[]{:S(2)}) collective-permute-start(bf16[96,2048]{1,0:T(8,128)(2,1)S(1)} %get-tuple-element.76), channel_id=1, source_target_pairs={{0,2},{1,3},{2,4},{3,5},{4,6},{5,7},{6,8},{7,9},{8,10},{9,11},{10,... | collective-permute-start | bytes 1179656 | tf_op jit(solution)/shard_map/ppermute | solution.py:26
  147.2 8.2 %collective-permute-start.22 = (bf16[96,2048]{1,0:T(8,128)(2,1)S(1)}, bf16[96,2048]{1,0:T(8,128)(2,1)S(1)}, u32[]{:S(2)}, u32[]{:S(2)}) collective-permute-start(bf16[96,2048]{1,0:T(8,128)(2,1)S(1)} %get-tuple-element.77), channel_id=1, source_target_pairs={{0,14},{1,15},{2,0},{3,1},{4,2},{5,3},{6,4},{7,5},{8,6},{9,7},{10,... | collective-permute-start | bytes 1179656 | tf_op jit(solution)/shard_map/ppermute | solution.py:26
  156.1 5.8 %collective-permute-start.23 = (bf16[48,2048]{1,0:T(8,128)(2,1)S(1)}, bf16[48,2048]{1,0:T(8,128)(2,1)S(1)}, u32[]{:S(2)}, u32[]{:S(2)}) collective-permute-start(bf16[48,2048]{1,0:T(8,128)(2,1)S(1)} %get-tuple-element.78), channel_id=1, source_target_pairs={{0,1},{1,0},{2,3},{3,2},{4,5},{5,4},{6,7},{7,6},{8,9},{9,8},{10,11... | collective-permute-start | bytes 589832 | tf_op jit(solution)/shard_map/ppermute | solution.py:31
  157.5 6.2 %collective-permute-start.29 = (bf16[128,640]{1,0:T(8,128)(2,1)S(1)}, bf16[128,640]{1,0:T(8,128)(2,1)S(1)}, u32[]{:S(2)}, u32[]{:S(2)}) collective-permute-start(bf16[128,640]{1,0:T(8,128)(2,1)S(1)} %get-tuple-element.82), channel_id=1, source_target_pairs={{0,1},{1,0},{2,3},{3,2},{4,5},{5,4},{6,7},{7,6},{8,9},{9,8},{10,11... | collective-permute-start | bytes 491528 | tf_op jit(solution)/shard_map/ppermute | solution.py:31
  (27 other events, 25.8 us)

commit v2 on v1

--- a/solution.py
+++ b/solution.py
@@ -78,14 +78,6 @@
     )(spot, *ins, *later, *through)
 
 
-def tie_kernel(*refs):
-    pass
-
-
-def tie(spot, values, later):
-    return call(tie_kernel, "tie", spot, (), [], [], [], later=later, through=values)
-
-
 def shape(dims, dtype=BF):
     return jax.ShapeDtypeStruct(tuple(dims), dtype)
 
@@ -116,51 +108,12 @@
         [VMEM] * 3,
         [part] * 4 + [kv],
         [VMEM] * 5,
-    )
-
-
-def prepare_kernel(
-    spot, query_in, grad_in, output, norms, w_query, w_key, w_value, query, grad, stats, w_send, sem
-):
-    h, c, x = spot[H], spot[C], spot[X]
-    kv_w = w_key.shape[0]
-    piece = w_send.shape[0] - kv_w
-    row = pl.multiple_of(((1 - h) * 2 + c) * (w_query.shape[0] // 4) + x * piece, piece)
-    copy = pltpu.make_async_copy(
-        w_query.at[pl.ds(row, piece), :], w_send.at[pl.ds(0, piece), :], sem
-    )
-    copy.start()
-    w_send[piece:, :piece] = w_key[:, pl.ds(row, piece)]
-    w_send[piece:, piece:] = w_value[:, pl.ds(row, piece)]
-    query[...] = query_in[...]
-    grad[...] = grad_in[...]
-    heads, seq = norms.shape
-    stats[...] = jnp.concatenate([norms[...], jnp.zeros((DH - heads, seq), F32)]).T
-    lane = lax.broadcasted_iota(jnp.int32, stats.shape, 1)
-    for head in range(heads):
-        cols = slice(head * DH, (head + 1) * DH)
-        delta = grad_in[:, cols].astype(F32) * output[:, cols].astype(F32)
-        delta = jnp.sum(delta, axis=1, keepdims=True)
-        stats[...] = jnp.where(lane == heads + head, delta, stats[...])
-    copy.wait()
-
-
-def prepare(spot, queries, out_grads, outputs, norms, w_query, w_key, w_value, later):
-    w_send = shape((w_query.shape[0] // 16 + w_key.shape[0], w_query.shape[1]))
-    return call(
-        prepare_kernel,
-        "prepare",
-        spot,
-        (queries, out_grads, outputs, norms, w_query, w_key, w_value),
-        [VMEM] * 4 + [ANY] + [VMEM] * 2,
-        [shape(queries.shape)] * 2 + [shape((queries.shape[0], DH), F32), w_send],
-        [VMEM] * 4,
-        [pltpu.SemaphoreType.DMA],
-        later=later,
-    )
-
-
-def block_kernel(spot, own, side, core, both, out):
+        vmem=64,
+    )
+
+
+def block_kernel(quarter, spot, own, side, core, both, out, start):
+    start[0] = ((1 - spot[H]) * 2 + spot[C]) * quarter + spot[X] * (quarter // NX)
     h = spot[H]
     rows = own.shape[1]
     near = pl.ds(pl.multiple_of(h * rows, rows), rows)
@@ -171,23 +124,48 @@
     out[:, 1, far, :] = both[...]
 
 
-def token_block(spot, parts, later):
+def token_block(spot, parts, quarter, later):
     part, rows, wide = parts[0].shape
     return call(
-        block_kernel,
+        functools.partial(block_kernel, quarter),
         "token_block",
         spot,
         parts,
         [VMEM] * 4,
-        [shape((part, 2, 2 * rows, wide))],
-        [VMEM],
-        later=later,
-    )[0]
+        [shape((part, 2, 2 * rows, wide)), shape((1,), jnp.int32)],
+        [VMEM, SMEM],
+        later=later,
+    )
+
+
+def halves_kernel(spot, up, down, out_up, out_down):
+    out_up[...] = up[...]
+    out_down[...] = down[...]
+
+
+def halves(spot, up, down, later):
+    part = (up.shape[0] // 2, *up.shape[1:])
+    zeros = (0,) * (len(part) - 1)
+    first = pl.BlockSpec(part, lambda step: (0, *zeros))
+    return call(
+        halves_kernel,
+        "halves",
+        spot,
+        (up, down),
+        [first, pl.BlockSpec(part, lambda step: (1, *zeros))],
+        [shape(part)] * 2,
+        [first] * 2,
+        grid=(1,),
+        later=later,
+    )
 
 
 def repeat_kernel(spot, value, out):
-    for index in range(out.shape[0]):
-        out[index] = value[...]
+    if len(value.shape) == len(out.shape):
+        out[...] = value[...]
+    else:
+        for index in range(out.shape[0]):
+            out[index] = value[...]
 
 
 def repeat(spot, value, times, later):
@@ -197,7 +175,7 @@
         spot,
         (value,),
         [VMEM],
-        [shape((times, *value.shape))],
+        [shape((times, *value.shape) if times else value.shape)],
         [VMEM],
         later=later,
     )[0]
@@ -252,7 +230,9 @@
     )
 
 
-def attend_kernel(spot, kv, query, grad, stats, out_a, out_b, send, keep, keys, values, total):
+def attend_kernel(
+    spot, kv, query, grad, output, norms, out_a, out_b, send, keep, keys, values, total, turned, grads
+):
     head = pl.program_id(0)
     heads = pl.num_programs(0)
     scaling = DH ** (-0.5)
@@ -265,10 +245,11 @@
             keys[index * part : (index + 1) * part, :] = kv[index, :part, :]
             values[index * part : (index + 1) * part, :] = kv[index, part:, :]
         total[...] = jnp.zeros_like(total)
-
-    lane = lax.broadcasted_iota(jnp.int32, stats.shape, 1)
-    norm = jnp.sum(jnp.where(lane == head, stats[...], 0.0), axis=1, keepdims=True)
-    delta = jnp.sum(jnp.where(lane == heads + head, stats[...], 0.0), axis=1, keepdims=True)
+        filler = jnp.zeros((DH - norms.shape[0], seq), F32)
+        turned[...] = jnp.concatenate([norms[...], filler]).T
+
+    which = lax.broadcasted_iota(jnp.int32, turned.shape, 1) == head
+    norm = jnp.sum(jnp.where(which, turned[...], 0.0), axis=1, keepdims=True)
     for tile in range(seq // TILE):
         rows = slice(tile * TILE, (tile + 1) * TILE)
         width = (tile + 1) * TILE
@@ -278,23 +259,20 @@
         row_ids = lax.broadcasted_iota(jnp.int32, probs.shape, 0) + tile * TILE
         col_ids = lax.broadcasted_iota(jnp.int32, probs.shape, 1)
         probs = jnp.where(col_ids <= row_ids, probs, 0.0)
+        delta = jnp.sum(grad_t.astype(F32) * output[rows, :].astype(F32), axis=1, keepdims=True)
         dprobs = dot(grad_t, values[:, :width], 1, 0)
-        dscores = (probs * (dprobs - delta[rows])).astype(BF)
-        grad_q = (dot(dscores, keys[:, :width], 1, 1) * scaling).astype(BF)
-
-        @pl.when(head < heads - 1)
-        def _():
-            out_a[rows, :] = grad_q
-
-        @pl.when(head == heads - 1)
-        def _():
-            out_b[rows, :] = grad_q
-
+        dscores = (probs * (dprobs - delta)).astype(BF)
+        grads[rows, :] = (dot(dscores, keys[:, :width], 1, 1) * scaling).astype(BF)
         total[0, :, :width] += dot(query_t, dscores, 0, 0)
         total[1, :, :width] += dot(grad_t, probs.astype(BF), 0, 0)
 
+    @pl.when(head < heads - 1)
+    def _():
+        out_a[...] = grads[...]
+
     @pl.when(head == heads - 1)
     def _():
+        out_b[...] = grads[...]
         half = DH // 2
         mine = spot[ZB]
         near = pl.ds(pl.multiple_of(mine * half, half), half)
@@ -304,7 +282,7 @@
             send[index] = (total[index, far, :] * factor).astype(BF)
 
 
-def attend(spot, kv, queries, out_grads, stats, later):
+def attend(spot, kv, queries, out_grads, outputs, norms, later):
     seq = queries.shape[0]
     heads = queries.shape[1] // DH
     cols = pl.BlockSpec((seq, DH), lambda head: (0, head))
@@ -319,8 +297,8 @@
         attend_kernel,
         "attend",
         spot,
-        (kv, queries, out_grads, stats),
-        [full(kv), cols, cols, full(stats)],
+        (kv, queries, out_grads, outputs, norms),
+        [full(kv), cols, cols, cols, full(norms)],
         outs,
         [
             pl.BlockSpec((seq, DH), lambda head: (0, jnp.minimum(head, heads - 2))),
@@ -330,6 +308,8 @@
             pltpu.VMEM((DH, seq), BF),
             pltpu.VMEM((DH, seq), BF),
             pltpu.VMEM((2, DH, seq), F32),
+            pltpu.VMEM((seq, DH), F32),
+            pltpu.VMEM((seq, DH), BF),
         ],
         grid=(heads,),
         work=10**9,
@@ -382,6 +362,9 @@
         starts.append(at)
         at += piece.shape[1]
     return starts, at
+
+
+AWAYS = (4, 3, -3, 2, -2, 1, -1, 0)
 
 
 def load_rows(aways, z, pieces, held, sems):
@@ -401,90 +384,102 @@
     return copies
 
 
-def first_kernel(spot, weights, weights_kv, *rest):
-    pieces, (last_up, last_down, up, down, held, sems, last_sems) = rest[:5], rest[5:]
-    copies = load_rows((NZ // 2,), spot[Z], pieces, held, sems)
-    wide = up.shape[1] // 2
-    half, pair, _, cols = last_up.shape
-    for index, (last, out, first) in enumerate(((last_up, up, 0), (last_down, down, half // 2))):
-        for part in range(half // 2):
-            for rep in range(pair):
-                slot = part * pair + rep
-                copies.append(
-                    pltpu.make_async_copy(
-                        last.at[first + part, rep],
-                        out.at[:, pl.ds(wide + slot * cols, cols)],
-                        last_sems.at[index, slot],
-                    )
-                )
-    for copy in copies:
-        copy.start()
-    for copy in copies[: len(pieces)]:
-        copy.wait()
-    deep = weights.shape[1]
-    left, left_kv = held[:, :deep], held[:, deep:]
+def early_kernel(spot, weights, *rest):
+    pieces, (out, held, sems) = rest[:3], rest[3:]
+
+    @pl.when(pl.program_id(0) == 0)
+    def _():
+        run_copies(load_rows(AWAYS, spot[Z], pieces, held, sems))
+
+    total = dot(held[...], weights[:, : held.shape[1]], 1, 1)
+    out[...] = total.reshape(out.shape)
+
+
+def early_parts(spot, weights, pieces, later):
+    seq = pieces[0].shape[0]
+    width, deep = weights.shape
+    _, depth = offsets(pieces)
+    wide = 512
+    return call(
+        early_kernel,
+        "early_parts",
+        spot,
+        (weights, *pieces),
+        [pl.BlockSpec((wide, deep), lambda step: (step, 0)), *[ANY] * 3],
+        [shape((NZ, seq // NZ, width), F32)],
+        [pl.BlockSpec((NZ, seq // NZ, wide), lambda step: (0, 0, step))],
+        [pltpu.VMEM((seq, depth), BF), pltpu.SemaphoreType.DMA((NZ, 3))],
+        grid=(width // wide,),
+        work=10**9,
+        later=later,
+    )[0]
+
+
+def first_kernel(spot, weights, weights_kv, base, far, kv, up, down, held, sems):
+    run_copies(load_rows(AWAYS[:1], spot[Z], (far, kv), held, sems))
+    wide = up.shape[1]
+    deep = far.shape[1]
     for index, out in enumerate((up, down)):
         part = slice(index * wide, (index + 1) * wide)
-        out[:, :wide] = (
-            dot(left, weights[part, :], 1, 1) + dot(left_kv, weights_kv[:, part], 1, 0)
-        ).astype(BF)
-    for copy in copies[len(pieces) :]:
-        copy.wait()
-
-
-def first_parts(spot, weights, weights_kv, pieces, last_up, last_down):
-    rows = pieces[0].shape[0] // NZ
-    width, deep = weights.shape
-    depth = deep + weights_kv.shape[0]
+        total = dot(held[:, :deep], weights[part, :], 1, 1)
+        total += dot(held[:, deep:], weights_kv[:, part], 1, 0)
+        out[...] = (base[0, :, part] + total).astype(BF)
+
+
+def first_parts(spot, weights, weights_kv, base, far, kv):
+    _, rows, width = base.shape
+    depth, deep = far.shape[1] + kv.shape[1], far.shape[1]
+    last = weights.shape[1] // deep - 1
+    out = pl.BlockSpec((rows, width // 2), lambda step: (0, 0))
     return call(
         first_kernel,
         "first_parts",
         spot,
-        (weights, weights_kv, *pieces, last_up, last_down),
-        [VMEM] * 2 + [ANY] * 7,
-        [shape((rows, width))] * 2,
-        [VMEM] * 2,
+        (weights, weights_kv, base, far, kv),
         [
-            pltpu.VMEM((rows, depth), BF),
-            pltpu.SemaphoreType.DMA((1, 5)),
-            pltpu.SemaphoreType.DMA((2, 4)),
+            pl.BlockSpec((width, deep), lambda step: (0, last)),
+            pl.BlockSpec(weights_kv.shape, lambda step: (0, 0)),
+            pl.BlockSpec((1, rows, width), lambda step: (0, 0, 0)),
+            ANY,
+            ANY,
         ],
-    )
-
-
-def token_kernel(aways, spot, weights, weights_kv, *rest):
-    pieces, (out, held, sems) = rest[:5], rest[5:]
-
+        [shape((rows, width // 2))] * 2,
+        [out] * 2,
+        [pltpu.VMEM((rows, depth), BF), pltpu.SemaphoreType.DMA((1, 2))],
+        grid=(1,),
+    )
+
+
+def rest_kernel(spot, weights, weights_kv, base, far, kv, out, held, sems):
     @pl.when(pl.program_id(0) == 0)
     def _():
-        run_copies(load_rows(aways, spot[Z], pieces, held, sems))
-
-    deep = weights.shape[1]
+        run_copies(load_rows(AWAYS[1:], spot[Z], (far, kv), held, sems))
+
+    deep = far.shape[1]
     total = dot(held[:, :deep], weights[...], 1, 1) + dot(held[:, deep:], weights_kv[...], 1, 0)
-    out[...] = total.reshape(out.shape)
-
-
-def token_parts(aways, spot, weights, weights_kv, pieces, later):
-    rows = pieces[0].shape[0] // NZ
-    width, deep = weights.shape
-    depth = deep + weights_kv.shape[0]
+    out[...] = (base[1:] + total.reshape(out.shape)).astype(BF)
+
+
+def rest_parts(spot, weights, weights_kv, base, far, kv, later):
+    count, rows, width = base.shape
+    depth, deep = far.shape[1] + kv.shape[1], far.shape[1]
+    last = weights.shape[1] // deep - 1
     wide = 512
     return call(
-        functools.partial(token_kernel, aways),
-        "token_parts",
-        spot,
-        (weights, weights_kv, *pieces),
+        rest_kernel,
+        "rest_parts",
+        spot,
+        (weights, weights_kv, base, far, kv),
         [
-            pl.BlockSpec((wide, deep), lambda step: (step, 0)),
-            pl.BlockSpec((depth - deep, wide), lambda step: (0, step)),
-            *[ANY] * 5,
+            pl.BlockSpec((wide, deep), lambda step: (step, last)),
+            pl.BlockSpec((kv.shape[1], wide), lambda step: (0, step)),
+            pl.BlockSpec((count, rows, wide), lambda step: (0, 0, step)),
+            ANY,
+            ANY,
         ],
-        [shape((len(aways), rows, width), F32)],
-        [pl.BlockSpec((len(aways), rows, wide), lambda step: (0, 0, step))],
-        [
-            pltpu.VMEM((len(aways) * rows, depth), BF),
-            pltpu.SemaphoreType.DMA((len(aways), 5)),
-        ],
+        [shape((count - 1, rows, width))],
+        [pl.BlockSpec((count - 1, rows, wide), lambda step: (0, 0, step))],
+        [pltpu.VMEM(((count - 1) * rows, depth), BF), pltpu.SemaphoreType.DMA((count - 1, 2))],
         grid=(width // wide,),
         work=10**9,
         later=later,
@@ -492,22 +487,22 @@
 
 
 def ring_kernel(kind, spot, up, down, ups, downs, *outs):
-    wide = up.shape[1] // 2
+    wide = up.shape[1]
     if kind == "first":
         for arrived, part, out, start in ((up, ups, outs[0], 0), (down, downs, outs[1], wide)):
-            out[...] = part[0].astype(BF)
+            out[...] = part[0]
             cols = slice(start, start + wide)
-            out[:, cols] = (part[0, :, cols] + arrived[:, :wide].astype(F32)).astype(BF)
+            out[:, cols] = (part[0, :, cols].astype(F32) + arrived[...].astype(F32)).astype(BF)
     elif kind == "next":
         for arrived, part, out in ((up, ups, outs[0]), (down, downs, outs[1])):
-            out[...] = (part[0] + arrived[...].astype(F32)).astype(BF)
+            out[...] = (part[0].astype(F32) + arrived[...].astype(F32)).astype(BF)
     else:
         own, send = outs
         h = spot[H]
         rows = own.shape[0]
         for out, side in ((own, h), (send, 1 - h)):
             here = pl.ds(pl.multiple_of(side * rows, rows), rows)
-            total = ups[0, here, :] + up[here, :].astype(F32) + down[here, :].astype(F32)
+            total = ups[0, here, :].astype(F32) + up[here, :].astype(F32) + down[here, :].astype(F32)
             out[...] = total.astype(BF)
 
 
@@ -535,7 +530,6 @@
     starts, _ = offsets(pieces[:5])
     z = spot[Z]
     rows = blocks[0].shape[2]
-    cols = blocks[0].shape[3]
     places = (0, -1, 1, -2, 2, -3, 3)
 
     @pl.when(pl.program_id(0) == 0)
@@ -558,14 +552,14 @@
                 )
             )
         for index, last in enumerate((up, down)):
-            for slot in range(NX):
-                copies.append(
-                    pltpu.make_async_copy(
-                        last.at[:, pl.ds(last.shape[1] // 2 + slot * cols, cols)],
-                        lefts.at[index * (NX // 2) + slot // 2, slot % 2, place(NZ // 2), :],
-                        last_sems.at[index, slot],
-                    )
+            half = NX // 2
+            copies.append(
+                pltpu.make_async_copy(
+                    last,
+                    lefts.at[pl.ds(index * half, half), :, place(NZ // 2), :],
+                    last_sems.at[index],
                 )
+            )
         run_copies(copies)
 
     left = lefts[pl.program_id(0)]
@@ -591,7 +585,7 @@
             pltpu.VMEM((NX, 2, seq, wide), BF),
             pltpu.SemaphoreType.DMA((10,)),
             pltpu.SemaphoreType.DMA((NZ - 1,)),
-            pltpu.SemaphoreType.DMA((2, NX)),
+            pltpu.SemaphoreType.DMA((2,)),
         ],
         grid=(NX,),
         work=10**10,
@@ -609,7 +603,7 @@
     send[...] = total[:, q_w:].astype(BF)
 
 
-def wgrad_sum(spot, terms, q_w):
+def wgrad_sum(spot, terms, q_w, later):
     _, rows, depth = terms.shape
     return call(
         wgrad_sum_kernel,
@@ -619,6 +613,7 @@
         [VMEM],
         [shape((rows, q_w), F32), shape((rows, depth - 2 * q_w), F32), shape((rows, depth - q_w))],
         [VMEM] * 3,
+        later=later,
     )
 
 
@@ -680,56 +675,69 @@
     core = swap_quad(core, 1, 0)
     both = swap_quad(both, 1, 1)
     kv = lax.all_to_all(kv, "tensor", 0, 0, axis_index_groups=heads4, tiled=True)
-    queries, out_grads, stats, w_send = prepare(
-        spot, queries, out_grads, outputs, log_norms, w_query, w_key, w_value, [own]
+    quarter = tokens.shape[1] // 4
+    block, start = token_block(spot, (own, side, core, both), quarter, [])
+    up1, down1 = shift(block, "tensor", 2), shift(block, "tensor", -2)
+    piece = quarter // NX
+    row = start[0]
+    w_send = jnp.concatenate(
+        [
+            lax.dynamic_slice_in_dim(w_query, row, piece, 0),
+            jnp.concatenate(
+                [lax.dynamic_slice_in_dim(w, row, piece, 1) for w in (w_key, w_value)], axis=1
+            ),
+        ]
     )
     w_side = swap(w_send, "tensor", 1)
 
-    block = token_block(spot, (own, side, core, both), [stats])
-    up1, down1 = shift(block, "tensor", 2), shift(block, "tensor", -2)
-    own_a, own_b, kv_send, kv_keep = attend(spot, kv, queries, out_grads, stats, [block])
+    own_a, own_b, kv_send, kv_keep = attend(
+        spot, kv, queries, out_grads, outputs, log_norms, [block]
+    )
+    w_side = repeat(spot, w_side, NX, [own_a, up1, down1])
+    w_far = lax.all_to_all(w_side, "dp", 0, 0, axis_index_groups=ring_x, tiled=True)
     far_a = swap(own_a, "tensor", 1)
     kv_z = swap(kv_send, "tensor", 2)
-    up1, down1, own_b = tie(spot, [up1, down1, own_b], [])
     up2, down2 = shift(up1, "tensor", 2), shift(down1, "tensor", -2)
-    w_side = repeat(spot, w_side, NX, [up1])
-    w_far = lax.all_to_all(w_side, "dp", 0, 0, axis_index_groups=ring_x, tiled=True)
-    kv_keep, kv_send = middle(spot, kv_keep, kv_z, [w_side], [])
-    up2, down2, far_a, w_far, kv_send = tie(spot, [up2, down2, far_a, w_far, kv_send], [])
-    up3, down3 = shift(up2, "tensor", 2), shift(down2, "tensor", -2)
+    kv_keep, kv_send = middle(spot, kv_keep, kv_z, [up2, down2, far_a], [])
     kv_y = swap(kv_send, "tensor", 1)
     far_b = swap(own_b, "tensor", 1)
+    up3, down3 = shift(up2, "tensor", 2), shift(down2, "tensor", -2)
+    w_far = repeat(spot, w_far, 0, [kv_send])
     w_core = swap(w_far, "dp", 1)
-    weights, weights_kv = gather_weights(spot, w_query, w_key, w_value, w_far, w_core, [])
-    (kv_grad,) = final_kv(spot, kv_keep, kv_y, [weights_kv, far_b], [])
+    weights, weights_kv = gather_weights(
+        spot, w_query, w_key, w_value, w_far, w_core, [kv_send]
+    )
+    base = early_parts(spot, weights, [own_a, own_b, far_a], [])
+    up4, down4 = halves(spot, up3, down3, [base])
+    up4, down4 = shift(up4, "tensor", 2), shift(down4, "tensor", -2)
+    (kv_grad,) = final_kv(spot, kv_keep, kv_y, [base, far_b], [])
     here = [own_a, own_b, far_a, far_b, kv_grad]
     there = [swap(value, "dp", 1) for value in here]
 
-    up, down = first_parts(spot, weights, weights_kv, here, up3, down3)
+    up, down = first_parts(spot, weights, weights_kv, base, far_b, kv_grad)
     up_next, down_next = shift(up, "tensor", 2), shift(down, "tensor", -2)
-    last_up, last_down = up_next, down_next
-    parts = token_parts((3, -3, 2, -2, 1, -1, 0), spot, weights, weights_kv, here, [up])
-    up, down = ring_step("first", spot, up_next, down_next, parts, (0, 1), [])
-    up_next, down_next = shift(up, "tensor", 2), shift(down, "tensor", -2)
+    parts = rest_parts(spot, weights, weights_kv, base, far_b, kv_grad, [up])
     blocks = [block, up1, down1, up2, down2, up3, down3]
-    terms = wgrad_parts(spot, blocks, last_up, last_down, here, there, [parts])
-    for slots in ((2, 3), (4, 5)):
-        up, down = ring_step("next", spot, up_next, down_next, parts, slots, [])
+    terms = wgrad_parts(
+        spot, blocks, up4, down4, here, there, [parts, up_next, down_next]
+    )
+    for kind, slots in (("first", (0, 1)), ("next", (2, 3)), ("next", (4, 5))):
+        up, down = ring_step(kind, spot, up_next, down_next, parts, slots, [terms])
         up_next, down_next = shift(up, "tensor", 2), shift(down, "tensor", -2)
-    mine, other = ring_step("last", spot, up_next, down_next, parts, (6, 6), [])
+
+    terms = terms.reshape(8, DH, terms.shape[2])
+    terms = lax.all_to_all(terms, "dp", 0, 0, axis_index_groups=plane, tiled=True)
+    w_own, w_own_kv, w_send = wgrad_sum(spot, terms, q_w, [up])
+    w_other = swap(w_send, "tensor", 1)
+
+    mine, other = ring_step("last", spot, up_next, down_next, parts, (6, 6), [w_send])
     other = swap(other, "tensor", 1)
     token_grads = jnp.where(
         h == 1,
         jnp.concatenate([other, mine], axis=1),
         jnp.concatenate([mine, other], axis=1),
     )
-
-    terms = terms.reshape(8, DH, terms.shape[2])
-    terms = lax.all_to_all(terms, "dp", 0, 0, axis_index_groups=plane, tiled=True)
-    own, own_kv, send = wgrad_sum(spot, terms, q_w)
-    query_wgrad, key_wgrad, value_wgrad = wgrad_final(
-        spot, own, own_kv, swap(send, "tensor", 1), kv_w
-    )
+    query_wgrad, key_wgrad, value_wgrad = wgrad_final(spot, w_own, w_own_kv, w_other, kv_w)
     return token_grads, query_wgrad, key_wgrad.T, value_wgrad.T
 
 

time: 166 us -> 173 us (1.042)
  local copies, waits for them, and re-layouts: 28.7 us -> 20.5 us
  waiting for transfers between devices: 45.4 us -> 49.8 us
  starting transfers between devices: 51.7 us -> 55.4 us
  Pallas kernels: 37.3 us -> 40.7 us
  between operations: 1.06 us -> 3 us
    unnamed x84 -> x66, local copies, waits for them, and re-layouts: 28.6 us -> 17.9 us
    ppermute x13, waiting for transfers between devices: 20 us -> 27.3 us  [swap(): return lax.ppermute(value, axis, pairs)]
    ppermute x14 -> x16, starting transfers between devices: 25.8 us -> 29.7 us  [shift(): return lax.ppermute(value, axis, pairs)]
    pallas_call x19, Pallas kernels: 37.3 us -> 40.7 us  [call(): pl.pallas_call(whole, grid=grid, in_specs=[SMEM, *specs, *[ANY] * (n_late...]
    ppermute x14 -> x16, waiting for transfers between devices: 25.4 us -> 22.4 us  [shift(): return lax.ppermute(value, axis, pairs)]
    dynamic_slice x0 -> x2, local copies, waits for them, and re-layouts: none -> 1.86 us  [the longest x1 1.02 us: body(): lax.dynamic_slice_in_dim(w_query, row, piece, 0)]
  transfers between devices with their start and end apart: 33 -> 35, of which waited for: 10 -> 11; matrix products, arithmetic and copies ran while one was open for 1% -> 1% of each run, Pallas kernels for 16% -> 16%
where the time goes in v2:
time: 173 us; the launch traced here: 171 us
  starting transfers between devices  55.4 us (32%)
  waiting for transfers between devices  49.8 us (29%)
  Pallas kernels  40.7 us (24%)
  local copies, waits for them, and re-layouts  20.5 us (12%)
  between operations  3 us (2%)
  other arithmetic  1.88 us (1%)
    pallas_call x19, Pallas kernels, call(): pl.pallas_call(whole, grid=grid, in_specs=[SMEM, *specs, *[ANY] * (n_late...  40.7 us
    ppermute x16, starting transfers between devices, shift(): return lax.ppermute(value, axis, pairs)  29.7 us
    ppermute x13, waiting for transfers between devices, swap(): return lax.ppermute(value, axis, pairs)  27.3 us
    ppermute x16, waiting for transfers between devices, shift(): return lax.ppermute(value, axis, pairs)  22.4 us
    unnamed x66, local copies, waits for them, and re-layouts  17.9 us
    all_to_all x1, starting transfers between devices, body(): lax.all_to_all(terms, 'dp', 0, 0, axis_index_groups=plane, tiled=True)  7.32 us
    ppermute x13, starting transfers between devices, swap(): return lax.ppermute(value, axis, pairs)  6.74 us
    all_to_all x1, starting transfers between devices, body(): lax.all_to_all(w_side, 'dp', 0, 0, axis_index_groups=ring_x, tiled=True)  4.83 us
  transfers between devices with their start and end apart: 35, of which 11 were waited for; matrix products, arithmetic and copies ran while one was open for 1% of the time, Pallas kernels for 16%

profile of v2, /device:TPU:26, one launch (start us, length us, event | category | flops | bytes accessed | tf_op | source)
XLA Modules:
  0.0 171.2 jit_solution(4493095660785182835)
XLA Ops:
  1.3 2.0 %pack.1 = (bf16[4,48,256]{2,1,0:T(8,128)(2,1)}, bf16[4,48,256]{2,1,0:T(8,128)(2,1)}, bf16[4,48,256]{2,1,0:T(8,128)(2,1)}, bf16[4,48,256]{2,1,0:T(8,128)(2,1)}, bf16[4,64,768]{2,1,0:T(8,128)(2,1)}) custom-call(s32[5]{0:T(128)} %stack.23.refs_0_, bf16[48,4096]{1,0:T(8,128)(2,1)} %refs_1_.2, bf16[32,768]{1,0:T(8,128)(2,1)} %bitcast.20, bf16[32,768]{1,0:T(8,128)(2,1)} %bitcast.21), custom_call_target="tpu_custom_call" | custom-call | tf_op jit(solution)/shard_map/pack/pallas_call | solution.py:65
  4.1 1.4 collective-permute-start.2
  5.5 4.6 %all-to-all-start = ((bf16[4,64,768]{2,1,0:T(8,128)(2,1)}), bf16[4,64,768]{2,1,0:T(8,128)(2,1)S(1)}, u32[]{:S(2)}, u32[]{:S(2)}) async-start(bf16[4,64,768]{2,1,0:T(8,128)(2,1)} %get-tuple-element.42), calls=%async_computation | async-start | bytes 786432 | tf_op jit(solution)/shard_map/all_to_all | solution.py:677
  11.7 1.3 token_block.1
  13.1 1.5 collective-permute-start.4
  14.6 4.5 %collective-permute-start.5 = (bf16[4,2,96,256]{3,2,1,0:T(8,128)(2,1)}, bf16[4,2,96,256]{3,2,1,0:T(8,128)(2,1)S(1)}, u32[]{:S(2)}, u32[]{:S(2)}) collective-permute-start(bf16[4,2,96,256]{3,2,1,0:T(8,128)(2,1)} %get-tuple-element.43.refs_6_.refs_1_), channel_id=1, source_target_pairs={{0,14},{1,15},{2,0},{3,1},{4,2},{5,3},{6,4},{7,5},{8,6},{9,7},{10,... | collective-permute-start | bytes 1179656 | tf_op jit(solution)/shard_map/ppermute | solution.py:26
  21.9 1.0 constant_dynamic-slice_fusion
  23.6 1.1 copy-done.30
  24.7 1.1 copy-done.31
  26.5 6.4 %attend.1 = (bf16[768,384]{1,0:T(8,128)(2,1)S(1)}, bf16[768,128]{1,0:T(8,128)(2,1)S(1)}, bf16[2,64,768]{2,1,0:T(8,128)(2,1)S(1)}, f32[2,64,768]{2,1,0:T(8,128)S(1)}) custom-call(s32[5]{0:T(128)S(1)} %copy-done.25, bf16[4,64,768]{2,1,0:T(8,128)(2,1)S(1)} %all-to-all-done.refs_1_, bf16[768,512]{1,0:T(8,128)(2,1)S(1)} %copy-done.29, ...), custom_call_target="tpu_custom_call" | custom-call | flops 1000000000 | tf_op jit(solution)/shard_map/attend/pallas_call | solution.py:65
  33.7 1.6 repeat.2
  35.4 4.8 %all-to-all-start.1 = ((bf16[4,288,512]{2,1,0:T(8,128)(2,1)}), bf16[4,288,512]{2,1,0:T(8,128)(2,1)S(1)}, u32[]{:S(2)}, u32[]{:S(2)}) async-start(bf16[4,288,512]{2,1,0:T(8,128)(2,1)} %repeat.2), calls=%async_computation.1 | async-start | bytes 2359296 | tf_op jit(solution)/shard_map/all_to_all | solution.py:697
  40.2 1.5 collective-permute-start.9
  41.7 3.2 %collective-permute-start.8 = (bf16[4,2,96,256]{3,2,1,0:T(8,128)(2,1)S(1)}, bf16[4,2,96,256]{3,2,1,0:T(8,128)(2,1)S(1)}, u32[]{:S(2)}, u32[]{:S(2)}) collective-permute-start(bf16[4,2,96,256]{3,2,1,0:T(8,128)(2,1)S(1)} %collective-permute-done.5.refs_4_.refs_3_), channel_id=1, source_target_pairs={{0,14},{1,15},{2,0},{3,1},{4,2},{5,3},{6,4},{7,5},{8,6},{9,7},{10,... | collective-permute-start | bytes 1179656 | tf_op jit(solution)/shard_map/ppermute | solution.py:26
  44.9 10.7 %collective-permute-done.6.refs_2_ = bf16[2,64,768]{2,1,0:T(8,128)(2,1)S(1)} collective-permute-done((bf16[2,64,768]{2,1,0:T(8,128)(2,1)S(1)}, bf16[2,64,768]{2,1,0:T(8,128)(2,1)S(1)}, u32[]{:S(2)}, u32[]{:S(2)}) %collective-permute-start.6) | collective-permute-done | bytes 196640 | tf_op jit(solution)/shard_map/ppermute | solution.py:31
  55.6 1.2 copy-done.14
  61.3 5.6 %collective-permute-done.11.refs_4_.refs_13_ = bf16[768,128]{1,0:T(8,128)(2,1)S(1)} collective-permute-done((bf16[768,128]{1,0:T(8,128)(2,1)S(1)}, bf16[768,128]{1,0:T(8,128)(2,1)S(1)}, u32[]{:S(2)}, u32[]{:S(2)}) %collective-permute-start.11) | collective-permute-done | bytes 196640 | tf_op jit(solution)/shard_map/ppermute | solution.py:31
  66.9 3.0 %collective-permute-start.16 = (bf16[4,2,96,256]{3,2,1,0:T(8,128)(2,1)S(1)}, bf16[4,2,96,256]{3,2,1,0:T(8,128)(2,1)S(1)}, u32[]{:S(2)}, u32[]{:S(2)}) collective-permute-start(bf16[4,2,96,256]{3,2,1,0:T(8,128)(2,1)S(1)} %copy-done.12), channel_id=1, source_target_pairs={{0,14},{1,15},{2,0},{3,1},{4,2},{5,3},{6,4},{7,5},{8,6},{9,7},{10,... | collective-permute-start | bytes 1179656 | tf_op jit(solution)/shard_map/ppermute | solution.py:26
  69.9 2.5 %collective-permute-done.15.refs_1_.refs_6_ = bf16[4,2,96,256]{3,2,1,0:T(8,128)(2,1)S(1)} collective-permute-done((bf16[4,2,96,256]{3,2,1,0:T(8,128)(2,1)S(1)}, bf16[4,2,96,256]{3,2,1,0:T(8,128)(2,1)S(1)}, u32[]{:S(2)}, u32[]{:S(2)}) %collective-permute-start.15) | collective-permute-done | bytes 393248 | tf_op jit(solution)/shard_map/ppermute | solution.py:26
  73.1 5.5 %collective-permute-done.12.refs_2_ = bf16[2,64,768]{2,1,0:T(8,128)(2,1)S(1)} collective-permute-done((bf16[2,64,768]{2,1,0:T(8,128)(2,1)S(1)}, bf16[2,64,768]{2,1,0:T(8,128)(2,1)S(1)}, u32[]{:S(2)}, u32[]{:S(2)}) %collective-permute-start.12) | collective-permute-done | bytes 196640 | tf_op jit(solution)/shard_map/ppermute | solution.py:31
  79.1 2.2 %copy-done.2 = bf16[4096,512]{1,0:T(8,128)(2,1)S(1)} copy-done((bf16[4096,512]{1,0:T(8,128)(2,1)S(1)}, bf16[4096,512]{1,0:T(8,128)(2,1)}, u32[]{:S(2)}) %copy-start.2) | copy-done | bytes 4194328
  83.2 1.5 gather_weights.1
  84.7 5.5 %early_parts.1.refs_3_ = f32[8,96,2048]{2,1,0:T(8,128)S(1)} custom-call(s32[5]{0:T(128)S(1)} %copy-done.25, bf16[2048,1024]{1,0:T(8,128)(2,1)S(1)} %get-tuple-element.48.refs_1_, bf16[768,384]{1,0:T(8,128)(2,1)S(1)} %get-tuple-element.44.refs_2_.refs_10_, bf16[768,128]{1,0:T(8,128)(2,1)S(1)} %get-tuple-element.50.refs_3_.refs_11_, ...), custom_call_target="tpu_custom_call" | custom-call | flops 1000000000 | tf_op jit(solution)/shard_map/early_parts/pallas_call | solution.py:65
  90.9 1.0 first_parts.1
  92.7 3.2 %collective-permute-start.14 = (bf16[96,1024]{1,0:T(8,128)(2,1)S(1)}, bf16[96,1024]{1,0:T(8,128)(2,1)S(1)}, u32[]{:S(2)}, u32[]{:S(2)}) collective-permute-start(bf16[96,1024]{1,0:T(8,128)(2,1)S(1)} %get-tuple-element.53), channel_id=1, source_target_pairs={{0,14},{1,15},{2,0},{3,1},{4,2},{5,3},{6,4},{7,5},{8,6},{9,7},{10,... | collective-permute-start | bytes 589832 | tf_op jit(solution)/shard_map/ppermute | solution.py:26
  95.9 3.3 %collective-permute-start.18 = (bf16[2,2,96,256]{3,2,1,0:T(8,128)(2,1)S(1)}, bf16[2,2,96,256]{3,2,1,0:T(8,128)(2,1)S(1)}, u32[]{:S(2)}, u32[]{:S(2)}) collective-permute-start(bf16[2,2,96,256]{3,2,1,0:T(8,128)(2,1)S(1)} %get-tuple-element.55), channel_id=1, source_target_pairs={{0,14},{1,15},{2,0},{3,1},{4,2},{5,3},{6,4},{7,5},{8,6},{9,7},{10,... | collective-permute-start | bytes 589832 | tf_op jit(solution)/shard_map/ppermute | solution.py:26
  99.2 3.6 %rest_parts.1.refs_20_.refs_3_.refs_4_ = bf16[7,96,2048]{2,1,0:T(8,128)(2,1)S(1)} custom-call(s32[5]{0:T(128)S(1)} %copy-done.25, bf16[2048,1024]{1,0:T(8,128)(2,1)S(1)} %get-tuple-element.48.refs_1_, bf16[128,2048]{1,0:T(8,128)(2,1)S(1)} %get-tuple-element.49.refs_2_, f32[8,96,2048]{2,1,0:T(8,128)S(1)} %early_parts.1.refs_3_, ...), custom_call_target="tpu_custom_call" | custom-call | flops 1000000000 | tf_op jit(solution)/shard_map/rest_parts/pallas_call | solution.py:65
  102.8 1.4 collective-permute-done.17.refs_8_
  104.3 7.2 %wgrad_parts.1.refs_5_ = bf16[4,256,1152]{2,1,0:T(8,128)(2,1)S(1)} custom-call(s32[5]{0:T(128)S(1)} %copy-done.25, bf16[4,2,96,256]{3,2,1,0:T(8,128)(2,1)} %get-tuple-element.43.refs_6_.refs_1_, bf16[4,2,96,256]{3,2,1,0:T(8,128)(2,1)S(1)} %copy-done.6, bf16[4,2,96,256]{3,2,1,0:T(8,128)(2,1)S(1)} %copy-done.8, bf16[4,2,96,256]{3,2,1,0:T(8,128)(2,1)S(1)} %copy-done.10, ...), custom_call_target="tpu_custom_call" | custom-call | flops 10000000000 | tf_op jit(solution)/shard_map/wgrad_parts/pallas_call | solution.py:65
  111.5 1.4 copy-done
  112.9 7.3 %all-to-all-start.2 = ((bf16[8,128,1152]{2,1,0:T(8,128)(2,1)}), bf16[8,128,1152]{2,1,0:T(8,128)(2,1)}, u32[]{:S(2)}, u32[]{:S(2)}) async-start(bf16[8,128,1152]{2,1,0:T(8,128)(2,1)} %bitcast.17), calls=%async_computation.2 | async-start | bytes 4718592 | tf_op jit(solution)/shard_map/all_to_all | solution.py:729
  120.3 1.7 copy-done.1
  122.6 1.8 %collective-permute-start.24 = (bf16[96,2048]{1,0:T(8,128)(2,1)S(1)}, bf16[96,2048]{1,0:T(8,128)(2,1)S(1)}, u32[]{:S(2)}, u32[]{:S(2)}) collective-permute-start(bf16[96,2048]{1,0:T(8,128)(2,1)S(1)} %get-tuple-element.56), channel_id=1, source_target_pairs={{0,2},{1,3},{2,4},{3,5},{4,6},{5,7},{6,8},{7,9},{8,10},{9,11},{10,... | collective-permute-start | bytes 1179656 | tf_op jit(solution)/shard_map/ppermute | solution.py:26
  124.4 2.2 %collective-permute-start.25 = (bf16[96,2048]{1,0:T(8,128)(2,1)S(1)}, bf16[96,2048]{1,0:T(8,128)(2,1)S(1)}, u32[]{:S(2)}, u32[]{:S(2)}) collective-permute-start(bf16[96,2048]{1,0:T(8,128)(2,1)S(1)} %get-tuple-element.57), channel_id=1, source_target_pairs={{0,14},{1,15},{2,0},{3,1},{4,2},{5,3},{6,4},{7,5},{8,6},{9,7},{10,... | collective-permute-start | bytes 1179656 | tf_op jit(solution)/shard_map/ppermute | solution.py:26
  126.6 7.3 %collective-permute-done.24.refs_1_ = bf16[96,2048]{1,0:T(8,128)(2,1)S(1)} collective-permute-done((bf16[96,2048]{1,0:T(8,128)(2,1)S(1)}, bf16[96,2048]{1,0:T(8,128)(2,1)S(1)}, u32[]{:S(2)}, u32[]{:S(2)}) %collective-permute-start.24) | collective-permute-done | bytes 393248 | tf_op jit(solution)/shard_map/ppermute | solution.py:26
  134.6 2.4 %collective-permute-start.26 = (bf16[96,2048]{1,0:T(8,128)(2,1)S(1)}, bf16[96,2048]{1,0:T(8,128)(2,1)S(1)}, u32[]{:S(2)}, u32[]{:S(2)}) collective-permute-start(bf16[96,2048]{1,0:T(8,128)(2,1)S(1)} %get-tuple-element.58), channel_id=1, source_target_pairs={{0,2},{1,3},{2,4},{3,5},{4,6},{5,7},{6,8},{7,9},{8,10},{9,11},{10,... | collective-permute-start | bytes 1179656 | tf_op jit(solution)/shard_map/ppermute | solution.py:26
  137.0 1.0 collective-permute-start.27
  138.0 6.7 %collective-permute-done.26.refs_1_ = bf16[96,2048]{1,0:T(8,128)(2,1)S(1)} collective-permute-done((bf16[96,2048]{1,0:T(8,128)(2,1)S(1)}, bf16[96,2048]{1,0:T(8,128)(2,1)S(1)}, u32[]{:S(2)}, u32[]{:S(2)}) %collective-permute-start.26) | collective-permute-done | bytes 393248 | tf_op jit(solution)/shard_map/ppermute | solution.py:26
  145.2 1.5 ring_step.6
  146.8 1.8 %collective-permute-start.28 = (bf16[96,2048]{1,0:T(8,128)(2,1)}, bf16[96,2048]{1,0:T(8,128)(2,1)S(1)}, u32[]{:S(2)}, u32[]{:S(2)}) collective-permute-start(bf16[96,2048]{1,0:T(8,128)(2,1)} %get-tuple-element.60.refs_2_), channel_id=1, source_target_pairs={{0,2},{1,3},{2,4},{3,5},{4,6},{5,7},{6,8},{7,9},{8,10},{9,11},{10,... | collective-permute-start | bytes 1179656 | tf_op jit(solution)/shard_map/ppermute | solution.py:26
  148.6 1.4 collective-permute-start.29
  150.0 2.5 %wgrad_sum.1 = (f32[128,512]{1,0:T(8,128)S(1)}, f32[128,128]{1,0:T(8,128)S(1)}, bf16[128,640]{1,0:T(8,128)(2,1)}) custom-call(s32[5]{0:T(128)S(1)} %copy-done.25, bf16[8,128,1152]{2,1,0:T(8,128)(2,1)} %all-to-all-done.2.refs_1_, bf16[96,2048]{1,0:T(8,128)(2,1)} %get-tuple-element.60.refs_2_), custom_call_target="tpu_custom_call" | custom-call | tf_op jit(solution)/shard_map/wgrad_sum/pallas_call | solution.py:65
  152.5 3.5 %collective-permute-done.28.refs_1_ = bf16[96,2048]{1,0:T(8,128)(2,1)S(1)} collective-permute-done((bf16[96,2048]{1,0:T(8,128)(2,1)}, bf16[96,2048]{1,0:T(8,128)(2,1)S(1)}, u32[]{:S(2)}, u32[]{:S(2)}) %collective-permute-start.28) | collective-permute-done | bytes 393248 | tf_op jit(solution)/shard_map/ppermute | solution.py:26
  156.6 1.3 ring_step.7
  159.3 1.3 collective-permute-start.31
  160.6 5.6 %collective-permute-done.31.refs_3_ = bf16[128,640]{1,0:T(8,128)(2,1)S(1)} collective-permute-done((bf16[128,640]{1,0:T(8,128)(2,1)}, bf16[128,640]{1,0:T(8,128)(2,1)S(1)}, u32[]{:S(2)}, u32[]{:S(2)}) %collective-permute-start.31) | collective-permute-done | bytes 163872 | tf_op jit(solution)/shard_map/ppermute | solution.py:31
  168.0 1.4 wgrad_final.1
  169.4 1.9 %maximum_select_fusion = bf16[48,4096]{1,0:T(8,128)(2,1)} fusion(bf16[48,2048]{1,0:T(8,128)(2,1)} %copy-done.19, bf16[48,2048]{1,0:T(8,128)(2,1)S(1)} %collective-permute-done.30, pred[]{:T(512)S(6)} %eq.7), kind=kLoop, calls=%fused_computation | loop fusion | flops 1769472 | bytes 786433 | tf_op jit(solution)/shard_map/jit(_where)/select_n | solution.py:735
  (112 shorter events, 20.9 us)
Async XLA Ops:
  3.4 20.2 %copy-start.25 = (s32[5]{0:T(128)S(1)}, s32[5]{0:T(128)}, u32[]{:S(2)}) copy-start(s32[5]{0:T(128)} %stack.23.refs_0_) | copy-start | bytes 64
  3.4 20.2 %copy-start.29 = (bf16[768,512]{1,0:T(8,128)(2,1)S(1)}, bf16[768,512]{1,0:T(8,128)(2,1)}, u32[]{:S(2)}) copy-start(bf16[768,512]{1,0:T(8,128)(2,1)} %refs_2_.1) | copy-start | bytes 2359300
  3.4 6.8 %collective-permute-start = (bf16[4,48,256]{2,1,0:T(8,128)(2,1)}, bf16[4,48,256]{2,1,0:T(8,128)(2,1)S(1)}, u32[]{:S(2)}, u32[]{:S(2)}) collective-permute-start(bf16[4,48,256]{2,1,0:T(8,128)(2,1)} %get-tuple-element.38), channel_id=1, source_target_pairs={{0,1},{1,0},{2,3},{3,2},{4,5},{5,4},{6,7},{7,6},{8,9},{9,8},{10,11... | collective-permute-start | bytes 294920 | tf_op jit(solution)/shard_map/ppermute | solution.py:39
  4.1 6.1 %collective-permute-start.1 = (bf16[4,48,256]{2,1,0:T(8,128)(2,1)}, bf16[4,48,256]{2,1,0:T(8,128)(2,1)S(1)}, u32[]{:S(2)}, u32[]{:S(2)}) collective-permute-start(bf16[4,48,256]{2,1,0:T(8,128)(2,1)} %get-tuple-element.39), channel_id=1, source_target_pairs={{0,16},{1,17},{2,18},{3,19},{4,20},{5,21},{6,22},{7,23},{8,24},{9,... | collective-permute-start | bytes 294920 | tf_op jit(solution)/shard_map/ppermute | solution.py:39
  4.1 6.1 %collective-permute-start.2 = (bf16[4,48,256]{2,1,0:T(8,128)(2,1)}, bf16[4,48,256]{2,1,0:T(8,128)(2,1)S(1)}, u32[]{:S(2)}, u32[]{:S(2)}) collective-permute-start(bf16[4,48,256]{2,1,0:T(8,128)(2,1)} %get-tuple-element.40), channel_id=1, source_target_pairs={{0,17},{1,16},{2,19},{3,18},{4,21},{5,20},{6,23},{7,22},{8,25},{9,... | collective-permute-start | bytes 294920 | tf_op jit(solution)/shard_map/ppermute | solution.py:39
  5.5 18.0 %all-to-all-start = ((bf16[4,64,768]{2,1,0:T(8,128)(2,1)}), bf16[4,64,768]{2,1,0:T(8,128)(2,1)S(1)}, u32[]{:S(2)}, u32[]{:S(2)}) async-start(bf16[4,64,768]{2,1,0:T(8,128)(2,1)} %get-tuple-element.42), calls=%async_computation | async-start | bytes 786432 | tf_op jit(solution)/shard_map/all_to_all | solution.py:677
  13.1 20.6 %collective-permute-start.4 = (bf16[4,2,96,256]{3,2,1,0:T(8,128)(2,1)}, bf16[4,2,96,256]{3,2,1,0:T(8,128)(2,1)S(1)}, u32[]{:S(2)}, u32[]{:S(2)}) collective-permute-start(bf16[4,2,96,256]{3,2,1,0:T(8,128)(2,1)} %get-tuple-element.43.refs_6_.refs_1_), channel_id=1, source_target_pairs={{0,2},{1,3},{2,4},{3,5},{4,6},{5,7},{6,8},{7,9},{8,10},{9,11},{10,... | collective-permute-start | bytes 1179656 | tf_op jit(solution)/shard_map/ppermute | solution.py:26
  14.6 19.1 %collective-permute-start.5 = (bf16[4,2,96,256]{3,2,1,0:T(8,128)(2,1)}, bf16[4,2,96,256]{3,2,1,0:T(8,128)(2,1)S(1)}, u32[]{:S(2)}, u32[]{:S(2)}) collective-permute-start(bf16[4,2,96,256]{3,2,1,0:T(8,128)(2,1)} %get-tuple-element.43.refs_6_.refs_1_), channel_id=1, source_target_pairs={{0,14},{1,15},{2,0},{3,1},{4,2},{5,3},{6,4},{7,5},{8,6},{9,7},{10,... | collective-permute-start | bytes 1179656 | tf_op jit(solution)/shard_map/ppermute | solution.py:26
  22.9 10.8 %collective-permute-start.3 = (bf16[288,512]{1,0:T(8,128)(2,1)S(1)}, bf16[288,512]{1,0:T(8,128)(2,1)S(1)}, u32[]{:S(2)}, u32[]{:S(2)}) collective-permute-start(bf16[288,512]{1,0:T(8,128)(2,1)S(1)} %maximum_maximum_fusion), channel_id=1, source_target_pairs={{0,1},{1,0},{2,3},{3,2},{4,5},{5,4},{6,7},{7,6},{8,9},{9,8},{10,11... | collective-permute-start | bytes 884744 | tf_op jit(solution)/shard_map/ppermute | solution.py:31
  33.7 8.0 %copy-start.5 = (bf16[4,2,96,256]{3,2,1,0:T(8,128)(2,1)}, bf16[4,2,96,256]{3,2,1,0:T(8,128)(2,1)S(1)}, u32[]{:S(2)}) copy-start(bf16[4,2,96,256]{3,2,1,0:T(8,128)(2,1)S(1)} %collective-permute-done.4.refs_3_.refs_2_) | copy-start | bytes 1179652
  33.7 7.9 %copy-start.7 = (bf16[4,2,96,256]{3,2,1,0:T(8,128)(2,1)}, bf16[4,2,96,256]{3,2,1,0:T(8,128)(2,1)S(1)}, u32[]{:S(2)}) copy-start(bf16[4,2,96,256]{3,2,1,0:T(8,128)(2,1)S(1)} %collective-permute-done.5.refs_4_.refs_3_) | copy-start | bytes 1179652
  35.4 23.5 %all-to-all-start.1 = ((bf16[4,288,512]{2,1,0:T(8,128)(2,1)}), bf16[4,288,512]{2,1,0:T(8,128)(2,1)S(1)}, u32[]{:S(2)}, u32[]{:S(2)}) async-start(bf16[4,288,512]{2,1,0:T(8,128)(2,1)} %repeat.2), calls=%async_computation.1 | async-start | bytes 2359296 | tf_op jit(solution)/shard_map/all_to_all | solution.py:697
  40.2 15.4 %collective-permute-start.9 = (bf16[768,384]{1,0:T(8,128)(2,1)S(1)}, bf16[768,384]{1,0:T(8,128)(2,1)S(1)}, u32[]{:S(2)}, u32[]{:S(2)}) collective-permute-start(bf16[768,384]{1,0:T(8,128)(2,1)S(1)} %get-tuple-element.44.refs_2_.refs_10_), channel_id=1, source_target_pairs={{0,1},{1,0},{2,3},{3,2},{4,5},{5,4},{6,7},{7,6},{8,9},{9,8},{10,11... | collective-permute-start | bytes 1769480 | tf_op jit(solution)/shard_map/ppermute | solution.py:31
  41.7 13.9 %collective-permute-start.7 = (bf16[4,2,96,256]{3,2,1,0:T(8,128)(2,1)S(1)}, bf16[4,2,96,256]{3,2,1,0:T(8,128)(2,1)S(1)}, u32[]{:S(2)}, u32[]{:S(2)}) collective-permute-start(bf16[4,2,96,256]{3,2,1,0:T(8,128)(2,1)S(1)} %collective-permute-done.4.refs_3_.refs_2_), channel_id=1, source_target_pairs={{0,2},{1,3},{2,4},{3,5},{4,6},{5,7},{6,8},{7,9},{8,10},{9,11},{10,... | collective-permute-start | bytes 1179656 | tf_op jit(solution)/shard_map/ppermute | solution.py:26
  41.7 13.9 %collective-permute-start.8 = (bf16[4,2,96,256]{3,2,1,0:T(8,128)(2,1)S(1)}, bf16[4,2,96,256]{3,2,1,0:T(8,128)(2,1)S(1)}, u32[]{:S(2)}, u32[]{:S(2)}) collective-permute-start(bf16[4,2,96,256]{3,2,1,0:T(8,128)(2,1)S(1)} %collective-permute-done.5.refs_4_.refs_3_), channel_id=1, source_target_pairs={{0,14},{1,15},{2,0},{3,1},{4,2},{5,3},{6,4},{7,5},{8,6},{9,7},{10,... | collective-permute-start | bytes 1179656 | tf_op jit(solution)/shard_map/ppermute | solution.py:26
  44.9 10.7 %collective-permute-start.6 = (bf16[2,64,768]{2,1,0:T(8,128)(2,1)S(1)}, bf16[2,64,768]{2,1,0:T(8,128)(2,1)S(1)}, u32[]{:S(2)}, u32[]{:S(2)}) collective-permute-start(bf16[2,64,768]{2,1,0:T(8,128)(2,1)S(1)} %get-tuple-element.46), channel_id=1, source_target_pairs={{0,2},{1,3},{2,0},{3,1},{4,6},{5,7},{6,4},{7,5},{8,10},{9,11},{10,... | collective-permute-start | bytes 589832 | tf_op jit(solution)/shard_map/ppermute | solution.py:31
  55.6 29.1 %copy-start.3 = (bf16[768,384]{1,0:T(8,128)(2,1)}, bf16[768,384]{1,0:T(8,128)(2,1)S(1)}, u32[]{:S(2)}) copy-start(bf16[768,384]{1,0:T(8,128)(2,1)S(1)} %collective-permute-done.9.refs_5_.refs_4_.refs_12_) | copy-start | bytes 1769476
  58.9 8.0 %copy-start.12 = (bf16[4,2,96,256]{3,2,1,0:T(8,128)(2,1)S(1)}, bf16[4,2,96,256]{3,2,1,0:T(8,128)(2,1)}, u32[]{:S(2)}) copy-start(bf16[4,2,96,256]{3,2,1,0:T(8,128)(2,1)} %copy-done.11) | copy-start | bytes 1179652
  59.5 19.1 %collective-permute-start.10 = (bf16[4,288,512]{2,1,0:T(8,128)(2,1)S(1)}, bf16[4,288,512]{2,1,0:T(8,128)(2,1)S(1)}, u32[]{:S(2)}, u32[]{:S(2)}) collective-permute-start(bf16[4,288,512]{2,1,0:T(8,128)(2,1)S(1)} %repeat.3.refs_4_), channel_id=1, source_target_pairs={{0,16},{16,0},{32,48},{48,32},{64,80},{80,64},{96,112},{112,96},{1... | collective-permute-start | bytes 3538952 | tf_op jit(solution)/shard_map/ppermute | solution.py:31
  59.9 12.5 %collective-permute-start.15 = (bf16[4,2,96,256]{3,2,1,0:T(8,128)(2,1)S(1)}, bf16[4,2,96,256]{3,2,1,0:T(8,128)(2,1)S(1)}, u32[]{:S(2)}, u32[]{:S(2)}) collective-permute-start(bf16[4,2,96,256]{3,2,1,0:T(8,128)(2,1)S(1)} %copy-done.10), channel_id=1, source_target_pairs={{0,2},{1,3},{2,4},{3,5},{4,6},{5,7},{6,8},{7,9},{8,10},{9,11},{10,... | collective-permute-start | bytes 1179656 | tf_op jit(solution)/shard_map/ppermute | solution.py:26
  60.1 6.8 %collective-permute-start.11 = (bf16[768,128]{1,0:T(8,128)(2,1)S(1)}, bf16[768,128]{1,0:T(8,128)(2,1)S(1)}, u32[]{:S(2)}, u32[]{:S(2)}) collective-permute-start(bf16[768,128]{1,0:T(8,128)(2,1)S(1)} %get-tuple-element.50.refs_3_.refs_11_), channel_id=1, source_target_pairs={{0,1},{1,0},{2,3},{3,2},{4,5},{5,4},{6,7},{7,6},{8,9},{9,8},{10,11... | collective-permute-start | bytes 589832 | tf_op jit(solution)/shard_map/ppermute | solution.py:31
  60.8 35.1 %collective-permute-start.19 = (bf16[768,384]{1,0:T(8,128)(2,1)S(1)}, bf16[768,384]{1,0:T(8,128)(2,1)S(1)}, u32[]{:S(2)}, u32[]{:S(2)}) collective-permute-start(bf16[768,384]{1,0:T(8,128)(2,1)S(1)} %get-tuple-element.44.refs_2_.refs_10_), channel_id=1, source_target_pairs={{0,16},{16,0},{32,48},{48,32},{64,80},{80,64},{96,112},{112,96},{1... | collective-permute-start | bytes 1769480 | tf_op jit(solution)/shard_map/ppermute | solution.py:31
  60.8 38.4 %collective-permute-start.21 = (bf16[768,384]{1,0:T(8,128)(2,1)S(1)}, bf16[768,384]{1,0:T(8,128)(2,1)S(1)}, u32[]{:S(2)}, u32[]{:S(2)}) collective-permute-start(bf16[768,384]{1,0:T(8,128)(2,1)S(1)} %collective-permute-done.9.refs_5_.refs_4_.refs_12_), channel_id=1, source_target_pairs={{0,16},{16,0},{32,48},{48,32},{64,80},{80,64},{96,112},{112,96},{1... | collective-permute-start | bytes 1769480 | tf_op jit(solution)/shard_map/ppermute | solution.py:31
  66.9 25.0 %collective-permute-start.16 = (bf16[4,2,96,256]{3,2,1,0:T(8,128)(2,1)S(1)}, bf16[4,2,96,256]{3,2,1,0:T(8,128)(2,1)S(1)}, u32[]{:S(2)}, u32[]{:S(2)}) collective-permute-start(bf16[4,2,96,256]{3,2,1,0:T(8,128)(2,1)S(1)} %copy-done.12), channel_id=1, source_target_pairs={{0,14},{1,15},{2,0},{3,1},{4,2},{5,3},{6,4},{7,5},{8,6},{9,7},{10,... | collective-permute-start | bytes 1179656 | tf_op jit(solution)/shard_map/ppermute | solution.py:26
  72.3 6.2 %collective-permute-start.12 = (bf16[2,64,768]{2,1,0:T(8,128)(2,1)S(1)}, bf16[2,64,768]{2,1,0:T(8,128)(2,1)S(1)}, u32[]{:S(2)}, u32[]{:S(2)}) collective-permute-start(bf16[2,64,768]{2,1,0:T(8,128)(2,1)S(1)} %get-tuple-element.47.refs_2_.refs_6_), channel_id=1, source_target_pairs={{0,1},{1,0},{2,3},{3,2},{4,5},{5,4},{6,7},{7,6},{8,9},{9,8},{10,11... | collective-permute-start | bytes 589832 | tf_op jit(solution)/shard_map/ppermute | solution.py:31
  78.6 14.1 %collective-permute-start.20 = (bf16[768,128]{1,0:T(8,128)(2,1)S(1)}, bf16[768,128]{1,0:T(8,128)(2,1)S(1)}, u32[]{:S(2)}, u32[]{:S(2)}) collective-permute-start(bf16[768,128]{1,0:T(8,128)(2,1)S(1)} %get-tuple-element.50.refs_3_.refs_11_), channel_id=1, source_target_pairs={{0,16},{16,0},{32,48},{48,32},{64,80},{80,64},{96,112},{112,96},{1... | collective-permute-start | bytes 589832 | tf_op jit(solution)/shard_map/ppermute | solution.py:31
  78.6 17.3 %collective-permute-start.22 = (bf16[768,128]{1,0:T(8,128)(2,1)S(1)}, bf16[768,128]{1,0:T(8,128)(2,1)S(1)}, u32[]{:S(2)}, u32[]{:S(2)}) collective-permute-start(bf16[768,128]{1,0:T(8,128)(2,1)S(1)} %collective-permute-done.11.refs_4_.refs_13_), channel_id=1, source_target_pairs={{0,16},{16,0},{32,48},{48,32},{64,80},{80,64},{96,112},{112,96},{1... | collective-permute-start | bytes 589832 | tf_op jit(solution)/shard_map/ppermute | solution.py:31
  91.9 10.9 %collective-permute-start.13 = (bf16[96,1024]{1,0:T(8,128)(2,1)S(1)}, bf16[96,1024]{1,0:T(8,128)(2,1)S(1)}, u32[]{:S(2)}, u32[]{:S(2)}) collective-permute-start(bf16[96,1024]{1,0:T(8,128)(2,1)S(1)} %get-tuple-element.52.refs_6_), channel_id=1, source_target_pairs={{0,2},{1,3},{2,4},{3,5},{4,6},{5,7},{6,8},{7,9},{8,10},{9,11},{10,... | collective-permute-start | bytes 589832 | tf_op jit(solution)/shard_map/ppermute | solution.py:26
  92.7 10.1 %collective-permute-start.14 = (bf16[96,1024]{1,0:T(8,128)(2,1)S(1)}, bf16[96,1024]{1,0:T(8,128)(2,1)S(1)}, u32[]{:S(2)}, u32[]{:S(2)}) collective-permute-start(bf16[96,1024]{1,0:T(8,128)(2,1)S(1)} %get-tuple-element.53), channel_id=1, source_target_pairs={{0,14},{1,15},{2,0},{3,1},{4,2},{5,3},{6,4},{7,5},{8,6},{9,7},{10,... | collective-permute-start | bytes 589832 | tf_op jit(solution)/shard_map/ppermute | solution.py:26
  95.9 8.3 %collective-permute-start.17 = (bf16[2,2,96,256]{3,2,1,0:T(8,128)(2,1)S(1)}, bf16[2,2,96,256]{3,2,1,0:T(8,128)(2,1)S(1)}, u32[]{:S(2)}, u32[]{:S(2)}) collective-permute-start(bf16[2,2,96,256]{3,2,1,0:T(8,128)(2,1)S(1)} %get-tuple-element.54), channel_id=1, source_target_pairs={{0,2},{1,3},{2,4},{3,5},{4,6},{5,7},{6,8},{7,9},{8,10},{9,11},{10,... | collective-permute-start | bytes 589832 | tf_op jit(solution)/shard_map/ppermute | solution.py:26
  95.9 8.4 %copy-start.4 = (bf16[768,384]{1,0:T(8,128)(2,1)S(1)}, bf16[768,384]{1,0:T(8,128)(2,1)}, u32[]{:S(2)}) copy-start(bf16[768,384]{1,0:T(8,128)(2,1)} %copy-done.3) | copy-start | bytes 1769476
  95.9 8.4 %copy-start.6 = (bf16[4,2,96,256]{3,2,1,0:T(8,128)(2,1)S(1)}, bf16[4,2,96,256]{3,2,1,0:T(8,128)(2,1)}, u32[]{:S(2)}) copy-start(bf16[4,2,96,256]{3,2,1,0:T(8,128)(2,1)} %copy-done.5) | copy-start | bytes 1179652
  95.9 8.3 %copy-start.8 = (bf16[4,2,96,256]{3,2,1,0:T(8,128)(2,1)S(1)}, bf16[4,2,96,256]{3,2,1,0:T(8,128)(2,1)}, u32[]{:S(2)}) copy-start(bf16[4,2,96,256]{3,2,1,0:T(8,128)(2,1)} %copy-done.7) | copy-start | bytes 1179652
  95.9 8.3 %collective-permute-start.18 = (bf16[2,2,96,256]{3,2,1,0:T(8,128)(2,1)S(1)}, bf16[2,2,96,256]{3,2,1,0:T(8,128)(2,1)S(1)}, u32[]{:S(2)}, u32[]{:S(2)}) collective-permute-start(bf16[2,2,96,256]{3,2,1,0:T(8,128)(2,1)S(1)} %get-tuple-element.55), channel_id=1, source_target_pairs={{0,14},{1,15},{2,0},{3,1},{4,2},{5,3},{6,4},{7,5},{8,6},{9,7},{10,... | collective-permute-start | bytes 589832 | tf_op jit(solution)/shard_map/ppermute | solution.py:26
  99.2 5.0 %collective-permute-start.23 = (bf16[768,128]{1,0:T(8,128)(2,1)S(1)}, bf16[768,128]{1,0:T(8,128)(2,1)S(1)}, u32[]{:S(2)}, u32[]{:S(2)}) collective-permute-start(bf16[768,128]{1,0:T(8,128)(2,1)S(1)} %kv_final.1.refs_5_.refs_14_), channel_id=1, source_target_pairs={{0,16},{16,0},{32,48},{48,32},{64,80},{80,64},{96,112},{112,96},{1... | collective-permute-start | bytes 589832 | tf_op jit(solution)/shard_map/ppermute | solution.py:31
  102.8 8.7 %copy-start.20 = (bf16[96,1024]{1,0:T(8,128)(2,1)}, bf16[96,1024]{1,0:T(8,128)(2,1)S(1)}, u32[]{:S(2)}) copy-start(bf16[96,1024]{1,0:T(8,128)(2,1)S(1)} %collective-permute-done.13.refs_21_.refs_1_) | copy-start | bytes 589828
  102.8 8.7 %copy-start.22 = (bf16[96,1024]{1,0:T(8,128)(2,1)}, bf16[96,1024]{1,0:T(8,128)(2,1)S(1)}, u32[]{:S(2)}) copy-start(bf16[96,1024]{1,0:T(8,128)(2,1)S(1)} %collective-permute-done.14.refs_22_.refs_2_) | copy-start | bytes 589828
  112.9 7.3 %copy-start.21 = (bf16[96,1024]{1,0:T(8,128)(2,1)S(1)}, bf16[96,1024]{1,0:T(8,128)(2,1)}, u32[]{:S(2)}) copy-start(bf16[96,1024]{1,0:T(8,128)(2,1)} %copy-done.20) | copy-start | bytes 589828
  112.9 7.3 %copy-start.23 = (bf16[96,1024]{1,0:T(8,128)(2,1)S(1)}, bf16[96,1024]{1,0:T(8,128)(2,1)}, u32[]{:S(2)}) copy-start(bf16[96,1024]{1,0:T(8,128)(2,1)} %copy-done.22) | copy-start | bytes 589828
  112.9 37.1 %all-to-all-start.2 = ((bf16[8,128,1152]{2,1,0:T(8,128)(2,1)}), bf16[8,128,1152]{2,1,0:T(8,128)(2,1)}, u32[]{:S(2)}, u32[]{:S(2)}) async-start(bf16[8,128,1152]{2,1,0:T(8,128)(2,1)} %bitcast.17), calls=%async_computation.2 | async-start | bytes 4718592 | tf_op jit(solution)/shard_map/all_to_all | solution.py:729
  122.6 11.2 %collective-permute-start.24 = (bf16[96,2048]{1,0:T(8,128)(2,1)S(1)}, bf16[96,2048]{1,0:T(8,128)(2,1)S(1)}, u32[]{:S(2)}, u32[]{:S(2)}) collective-permute-start(bf16[96,2048]{1,0:T(8,128)(2,1)S(1)} %get-tuple-element.56), channel_id=1, source_target_pairs={{0,2},{1,3},{2,4},{3,5},{4,6},{5,7},{6,8},{7,9},{8,10},{9,11},{10,... | collective-permute-start | bytes 1179656 | tf_op jit(solution)/shard_map/ppermute | solution.py:26
  124.4 9.4 %collective-permute-start.25 = (bf16[96,2048]{1,0:T(8,128)(2,1)S(1)}, bf16[96,2048]{1,0:T(8,128)(2,1)S(1)}, u32[]{:S(2)}, u32[]{:S(2)}) collective-permute-start(bf16[96,2048]{1,0:T(8,128)(2,1)S(1)} %get-tuple-element.57), channel_id=1, source_target_pairs={{0,14},{1,15},{2,0},{3,1},{4,2},{5,3},{6,4},{7,5},{8,6},{9,7},{10,... | collective-permute-start | bytes 1179656 | tf_op jit(solution)/shard_map/ppermute | solution.py:26
  134.6 10.1 %collective-permute-start.26 = (bf16[96,2048]{1,0:T(8,128)(2,1)S(1)}, bf16[96,2048]{1,0:T(8,128)(2,1)S(1)}, u32[]{:S(2)}, u32[]{:S(2)}) collective-permute-start(bf16[96,2048]{1,0:T(8,128)(2,1)S(1)} %get-tuple-element.58), channel_id=1, source_target_pairs={{0,2},{1,3},{2,4},{3,5},{4,6},{5,7},{6,8},{7,9},{8,10},{9,11},{10,... | collective-permute-start | bytes 1179656 | tf_op jit(solution)/shard_map/ppermute | solution.py:26
  137.0 8.2 %collective-permute-start.27 = (bf16[96,2048]{1,0:T(8,128)(2,1)S(1)}, bf16[96,2048]{1,0:T(8,128)(2,1)S(1)}, u32[]{:S(2)}, u32[]{:S(2)}) collective-permute-start(bf16[96,2048]{1,0:T(8,128)(2,1)S(1)} %get-tuple-element.59), channel_id=1, source_target_pairs={{0,14},{1,15},{2,0},{3,1},{4,2},{5,3},{6,4},{7,5},{8,6},{9,7},{10,... | collective-permute-start | bytes 1179656 | tf_op jit(solution)/shard_map/ppermute | solution.py:26
  146.8 9.2 %collective-permute-start.28 = (bf16[96,2048]{1,0:T(8,128)(2,1)}, bf16[96,2048]{1,0:T(8,128)(2,1)S(1)}, u32[]{:S(2)}, u32[]{:S(2)}) collective-permute-start(bf16[96,2048]{1,0:T(8,128)(2,1)} %get-tuple-element.60.refs_2_), channel_id=1, source_target_pairs={{0,2},{1,3},{2,4},{3,5},{4,6},{5,7},{6,8},{7,9},{8,10},{9,11},{10,... | collective-permute-start | bytes 1179656 | tf_op jit(solution)/shard_map/ppermute | solution.py:26
  148.6 8.0 %collective-permute-start.29 = (bf16[96,2048]{1,0:T(8,128)(2,1)}, bf16[96,2048]{1,0:T(8,128)(2,1)S(1)}, u32[]{:S(2)}, u32[]{:S(2)}) collective-permute-start(bf16[96,2048]{1,0:T(8,128)(2,1)} %get-tuple-element.61), channel_id=1, source_target_pairs={{0,14},{1,15},{2,0},{3,1},{4,2},{5,3},{6,4},{7,5},{8,6},{9,7},{10,... | collective-permute-start | bytes 1179656 | tf_op jit(solution)/shard_map/ppermute | solution.py:26
  158.6 10.8 %collective-permute-start.30 = (bf16[48,2048]{1,0:T(8,128)(2,1)}, bf16[48,2048]{1,0:T(8,128)(2,1)S(1)}, u32[]{:S(2)}, u32[]{:S(2)}) collective-permute-start(bf16[48,2048]{1,0:T(8,128)(2,1)} %get-tuple-element.63), channel_id=1, source_target_pairs={{0,1},{1,0},{2,3},{3,2},{4,5},{5,4},{6,7},{7,6},{8,9},{9,8},{10,11... | collective-permute-start | bytes 589832 | tf_op jit(solution)/shard_map/ppermute | solution.py:31
  159.3 6.9 %collective-permute-start.31 = (bf16[128,640]{1,0:T(8,128)(2,1)}, bf16[128,640]{1,0:T(8,128)(2,1)S(1)}, u32[]{:S(2)}, u32[]{:S(2)}) collective-permute-start(bf16[128,640]{1,0:T(8,128)(2,1)} %get-tuple-element.62.refs_5_), channel_id=1, source_target_pairs={{0,1},{1,0},{2,3},{3,2},{4,5},{5,4},{6,7},{7,6},{8,9},{9,8},{10,11... | collective-permute-start | bytes 491528 | tf_op jit(solution)/shard_map/ppermute | solution.py:31
  (20 other events, 29.4 us)

commit v3 on v2

--- a/solution.py
+++ b/solution.py
@@ -337,23 +337,26 @@
     )
 
 
-def final_kv_kernel(spot, keep, arrived, out):
+def final_kv_kernel(spot, keep, arrived, early, far, out):
     total = keep[...] + arrived[...].astype(F32)
-    out[...] = total.reshape(out.shape[1], out.shape[0]).T.astype(BF)
-
-
-def final_kv(spot, keep, arrived, later, through):
+    start = early.shape[1]
+    deep = start + far.shape[1]
+    out[:, :start] = early[...]
+    out[:, start:deep] = far[...]
+    out[:, deep:] = total.reshape(out.shape[1] - deep, out.shape[0]).T.astype(BF)
+
+
+def final_kv(spot, keep, arrived, early, far, later):
     return call(
         final_kv_kernel,
         "kv_final",
         spot,
-        (keep, arrived),
-        [VMEM] * 2,
-        [shape((keep.shape[2], keep.shape[0] * keep.shape[1]))],
+        (keep, arrived, early, far),
+        [VMEM] * 4,
+        [shape((keep.shape[2], early.shape[1] + far.shape[1] + keep.shape[0] * keep.shape[1]))],
         [VMEM],
         later=later,
-        through=through,
-    )
+    )[0]
 
 
 def offsets(pieces):
@@ -368,7 +371,8 @@
 
 
 def load_rows(aways, z, pieces, held, sems):
-    starts, _ = offsets(pieces)
+    starts, total = offsets(pieces)
+    skip = total - held.shape[1]
     rows = pieces[0].shape[0] // NZ
     copies = []
     for slot, away in enumerate(aways):
@@ -376,8 +380,10 @@
         for index, piece in enumerate(pieces):
             copies.append(
                 pltpu.make_async_copy(
-                    piece.at[pl.ds(row, rows), :],
-                    held.at[pl.ds(slot * rows, rows), pl.ds(starts[index], piece.shape[1])],
+                    piece.at[pl.ds(row, rows), pl.ds(skip, piece.shape[1] - skip)],
+                    held.at[
+                        pl.ds(slot * rows, rows), pl.ds(starts[index], piece.shape[1] - skip)
+                    ],
                     sems.at[slot, index],
                 )
             )
@@ -385,11 +391,15 @@
 
 
 def early_kernel(spot, weights, *rest):
-    pieces, (out, held, sems) = rest[:3], rest[3:]
+    pieces, (out, packed, held, sems) = rest[:3], rest[3:]
+    rows = out.shape[1]
 
     @pl.when(pl.program_id(0) == 0)
     def _():
         run_copies(load_rows(AWAYS, spot[Z], pieces, held, sems))
+        for slot, away in enumerate(AWAYS):
+            row = pl.multiple_of(lax.rem(spot[Z] + away + NZ, NZ) * rows, rows)
+            packed[pl.ds(row, rows), :] = held[slot * rows : (slot + 1) * rows, :]
 
     total = dot(held[...], weights[:, : held.shape[1]], 1, 1)
     out[...] = total.reshape(out.shape)
@@ -406,19 +416,22 @@
         spot,
         (weights, *pieces),
         [pl.BlockSpec((wide, deep), lambda step: (step, 0)), *[ANY] * 3],
-        [shape((NZ, seq // NZ, width), F32)],
-        [pl.BlockSpec((NZ, seq // NZ, wide), lambda step: (0, 0, step))],
+        [shape((NZ, seq // NZ, width), F32), shape((seq, depth))],
+        [
+            pl.BlockSpec((NZ, seq // NZ, wide), lambda step: (0, 0, step)),
+            pl.BlockSpec((seq, depth), lambda step: (0, 0)),
+        ],
         [pltpu.VMEM((seq, depth), BF), pltpu.SemaphoreType.DMA((NZ, 3))],
         grid=(width // wide,),
         work=10**9,
         later=later,
-    )[0]
-
-
-def first_kernel(spot, weights, weights_kv, base, far, kv, up, down, held, sems):
-    run_copies(load_rows(AWAYS[:1], spot[Z], (far, kv), held, sems))
+    )
+
+
+def first_kernel(spot, weights, weights_kv, base, late, up, down, held, sems):
+    run_copies(load_rows(AWAYS[:1], spot[Z], (late,), held, sems))
     wide = up.shape[1]
-    deep = far.shape[1]
+    deep = weights.shape[1]
     for index, out in enumerate((up, down)):
         part = slice(index * wide, (index + 1) * wide)
         total = dot(held[:, :deep], weights[part, :], 1, 1)
@@ -426,60 +439,58 @@
         out[...] = (base[0, :, part] + total).astype(BF)
 
 
-def first_parts(spot, weights, weights_kv, base, far, kv):
+def first_parts(spot, weights, weights_kv, base, late, deep):
     _, rows, width = base.shape
-    depth, deep = far.shape[1] + kv.shape[1], far.shape[1]
+    depth = deep + weights_kv.shape[0]
     last = weights.shape[1] // deep - 1
     out = pl.BlockSpec((rows, width // 2), lambda step: (0, 0))
     return call(
         first_kernel,
         "first_parts",
         spot,
-        (weights, weights_kv, base, far, kv),
+        (weights, weights_kv, base, late),
         [
             pl.BlockSpec((width, deep), lambda step: (0, last)),
             pl.BlockSpec(weights_kv.shape, lambda step: (0, 0)),
             pl.BlockSpec((1, rows, width), lambda step: (0, 0, 0)),
             ANY,
-            ANY,
         ],
         [shape((rows, width // 2))] * 2,
         [out] * 2,
-        [pltpu.VMEM((rows, depth), BF), pltpu.SemaphoreType.DMA((1, 2))],
+        [pltpu.VMEM((rows, depth), BF), pltpu.SemaphoreType.DMA((1, 1))],
         grid=(1,),
     )
 
 
-def rest_kernel(spot, weights, weights_kv, base, far, kv, out, held, sems):
+def rest_kernel(spot, weights, weights_kv, base, late, out, held, sems):
     @pl.when(pl.program_id(0) == 0)
     def _():
-        run_copies(load_rows(AWAYS[1:], spot[Z], (far, kv), held, sems))
-
-    deep = far.shape[1]
+        run_copies(load_rows(AWAYS[1:], spot[Z], (late,), held, sems))
+
+    deep = weights.shape[1]
     total = dot(held[:, :deep], weights[...], 1, 1) + dot(held[:, deep:], weights_kv[...], 1, 0)
     out[...] = (base[1:] + total.reshape(out.shape)).astype(BF)
 
 
-def rest_parts(spot, weights, weights_kv, base, far, kv, later):
+def rest_parts(spot, weights, weights_kv, base, late, deep, later):
     count, rows, width = base.shape
-    depth, deep = far.shape[1] + kv.shape[1], far.shape[1]
+    depth = deep + weights_kv.shape[0]
     last = weights.shape[1] // deep - 1
     wide = 512
     return call(
         rest_kernel,
         "rest_parts",
         spot,
-        (weights, weights_kv, base, far, kv),
+        (weights, weights_kv, base, late),
         [
             pl.BlockSpec((wide, deep), lambda step: (step, last)),
-            pl.BlockSpec((kv.shape[1], wide), lambda step: (0, step)),
+            pl.BlockSpec((depth - deep, wide), lambda step: (0, step)),
             pl.BlockSpec((count, rows, wide), lambda step: (0, 0, step)),
-            ANY,
             ANY,
         ],
         [shape((count - 1, rows, width))],
         [pl.BlockSpec((count - 1, rows, wide), lambda step: (0, 0, step))],
-        [pltpu.VMEM(((count - 1) * rows, depth), BF), pltpu.SemaphoreType.DMA((count - 1, 2))],
+        [pltpu.VMEM(((count - 1) * rows, depth), BF), pltpu.SemaphoreType.DMA((count - 1, 1))],
         grid=(width // wide,),
         work=10**9,
         later=later,
@@ -526,8 +537,7 @@
 
 def wgrad_kernel(spot, *rest):
     blocks, (up, down), rest = rest[: NZ - 1], rest[NZ - 1 : NZ + 1], rest[NZ + 1 :]
-    pieces, (out, held, lefts, sems, left_sems, last_sems) = rest[:10], rest[10:]
-    starts, _ = offsets(pieces[:5])
+    pieces, (out, held, lefts, sems, left_sems, last_sems) = rest[:2], rest[2:]
     z = spot[Z]
     rows = blocks[0].shape[2]
     places = (0, -1, 1, -2, 2, -3, 3)
@@ -538,11 +548,7 @@
             return pl.ds(pl.multiple_of(lax.rem(z + away + NZ, NZ) * rows, rows), rows)
 
         copies = [
-            pltpu.make_async_copy(
-                piece,
-                held.at[index // 5, :, pl.ds(starts[index % 5], piece.shape[1])],
-                sems.at[index],
-            )
+            pltpu.make_async_copy(piece, held.at[index], sems.at[index])
             for index, piece in enumerate(pieces)
         ]
         for index, (block, away) in enumerate(zip(blocks, places)):
@@ -569,21 +575,20 @@
 
 
 def wgrad_parts(spot, blocks, up, down, here, there, later):
-    seq = here[0].shape[0]
-    _, depth = offsets(here)
+    seq, depth = here.shape
     wide = blocks[0].shape[3]
     return call(
         wgrad_kernel,
         "wgrad_parts",
         spot,
-        (*blocks, up, down, *here, *there),
-        [ANY] * (NZ + 11),
+        (*blocks, up, down, here, there),
+        [ANY] * (NZ + 3),
         [shape((NX, wide, depth))],
         [pl.BlockSpec((1, wide, depth), lambda step: (step, 0, 0))],
         [
             pltpu.VMEM((2, seq, depth), BF),
             pltpu.VMEM((NX, 2, seq, wide), BF),
-            pltpu.SemaphoreType.DMA((10,)),
+            pltpu.SemaphoreType.DMA((2,)),
             pltpu.SemaphoreType.DMA((NZ - 1,)),
             pltpu.SemaphoreType.DMA((2,)),
         ],
@@ -617,8 +622,13 @@
     )
 
 
-def wgrad_final_kernel(spot, own, own_kv, arrived, out, out_k, out_v, turned):
+def final_kernel(
+    spot, mine, other, own, own_kv, arrived, out_tokens, out, out_k, out_v, turned
+):
     h = spot[H]
+    wide = mine.shape[1]
+    out_tokens[:, pl.ds(pl.multiple_of(h * wide, wide), wide)] = mine[...]
+    out_tokens[:, pl.ds(pl.multiple_of((1 - h) * wide, wide), wide)] = other[...]
     rows, q_w = own.shape
     kv_w = out_k.shape[0]
     near = pl.ds(pl.multiple_of(h * rows, rows), rows)
@@ -632,16 +642,21 @@
             to[:, cols] = turned[pl.ds(start, kv_w), :]
 
 
-def wgrad_final(spot, own, own_kv, arrived, kv_w):
+def final(spot, mine, other, own, own_kv, arrived, kv_w):
+    n_own, wide = mine.shape
     rows, q_w = own.shape
     return call(
-        wgrad_final_kernel,
-        "wgrad_final",
-        spot,
-        (own, own_kv, arrived),
-        [VMEM] * 3,
-        [shape((2 * rows, q_w), F32)] + [shape((kv_w, 2 * rows), F32)] * 2,
-        [VMEM] * 3,
+        final_kernel,
+        "final",
+        spot,
+        (mine, other, own, own_kv, arrived),
+        [VMEM] * 5,
+        [
+            shape((n_own, 2 * wide)),
+            shape((2 * rows, q_w), F32),
+            *[shape((kv_w, 2 * rows), F32)] * 2,
+        ],
+        [VMEM] * 4,
         [pltpu.VMEM((own_kv.shape[1], rows), F32)],
     )
 
@@ -707,16 +722,15 @@
     weights, weights_kv = gather_weights(
         spot, w_query, w_key, w_value, w_far, w_core, [kv_send]
     )
-    base = early_parts(spot, weights, [own_a, own_b, far_a], [])
+    base, early = early_parts(spot, weights, [own_a, own_b, far_a], [])
     up4, down4 = halves(spot, up3, down3, [base])
     up4, down4 = shift(up4, "tensor", 2), shift(down4, "tensor", -2)
-    (kv_grad,) = final_kv(spot, kv_keep, kv_y, [base, far_b], [])
-    here = [own_a, own_b, far_a, far_b, kv_grad]
-    there = [swap(value, "dp", 1) for value in here]
-
-    up, down = first_parts(spot, weights, weights_kv, base, far_b, kv_grad)
+    here = final_kv(spot, kv_keep, kv_y, early, far_b, [base, up3, down3])
+    there = swap(here, "dp", 1)
+
+    up, down = first_parts(spot, weights, weights_kv, base, here, DH)
     up_next, down_next = shift(up, "tensor", 2), shift(down, "tensor", -2)
-    parts = rest_parts(spot, weights, weights_kv, base, far_b, kv_grad, [up])
+    parts = rest_parts(spot, weights, weights_kv, base, here, DH, [up])
     blocks = [block, up1, down1, up2, down2, up3, down3]
     terms = wgrad_parts(
         spot, blocks, up4, down4, here, there, [parts, up_next, down_next]
@@ -732,12 +746,9 @@
 
     mine, other = ring_step("last", spot, up_next, down_next, parts, (6, 6), [w_send])
     other = swap(other, "tensor", 1)
-    token_grads = jnp.where(
-        h == 1,
-        jnp.concatenate([other, mine], axis=1),
-        jnp.concatenate([mine, other], axis=1),
-    )
-    query_wgrad, key_wgrad, value_wgrad = wgrad_final(spot, w_own, w_own_kv, w_other, kv_w)
+    token_grads, query_wgrad, key_wgrad, value_wgrad = final(
+        spot, mine, other, w_own, w_own_kv, w_other, kv_w
+    )
     return token_grads, query_wgrad, key_wgrad.T, value_wgrad.T
 
 

time: 173 us -> 156 us (0.902)
  waiting for transfers between devices: 49.8 us -> 43 us
  local copies, waits for them, and re-layouts: 20.5 us -> 16.5 us
  starting transfers between devices: 55.4 us -> 52.1 us
    ppermute x13 -> x9, waiting for transfers between devices: 27.3 us -> 16.4 us  [swap(): return lax.ppermute(value, axis, pairs)]
    unnamed x66 -> x48, local copies, waits for them, and re-layouts: 17.9 us -> 14 us
    ppermute x16, waiting for transfers between devices: 22.4 us -> 26.3 us  [shift(): return lax.ppermute(value, axis, pairs)]
    ppermute x16, starting transfers between devices: 29.7 us -> 26.7 us  [shift(): return lax.ppermute(value, axis, pairs)]
    select_n x1 -> x0, other arithmetic: 1.86 us -> none  [body(): jnp.where(h == 1, jnp.concatenate([other, mine], axis=1), jnp.concatenate...]
    ppermute x13 -> x9, starting transfers between devices: 6.74 us -> 6.45 us  [swap(): return lax.ppermute(value, axis, pairs)]
  transfers between devices with their start and end apart: 35 -> 31, of which waited for: 11 -> 12; matrix products, arithmetic and copies ran while one was open for 1% -> 2% of each run, Pallas kernels for 16% -> 16%
where the time goes in v3:
time: 156 us; the launch traced here: 155 us
  starting transfers between devices  52.1 us (33%)
  waiting for transfers between devices  43 us (28%)
  Pallas kernels  39.2 us (25%)
  local copies, waits for them, and re-layouts  16.5 us (11%)
  between operations  2.95 us (2%)
    pallas_call x19, Pallas kernels, call(): pl.pallas_call(whole, grid=grid, in_specs=[SMEM, *specs, *[ANY] * (n_late...  39.2 us
    ppermute x16, starting transfers between devices, shift(): return lax.ppermute(value, axis, pairs)  26.7 us
    ppermute x16, waiting for transfers between devices, shift(): return lax.ppermute(value, axis, pairs)  26.3 us
    ppermute x9, waiting for transfers between devices, swap(): return lax.ppermute(value, axis, pairs)  16.4 us
    unnamed x48, local copies, waits for them, and re-layouts  14 us
    all_to_all x1, starting transfers between devices, body(): lax.all_to_all(terms, 'dp', 0, 0, axis_index_groups=plane, tiled=True)  7.21 us
    ppermute x9, starting transfers between devices, swap(): return lax.ppermute(value, axis, pairs)  6.45 us
    all_to_all x1, starting transfers between devices, body(): lax.all_to_all(w_side, 'dp', 0, 0, axis_index_groups=ring_x, tiled=True)  4.95 us
  transfers between devices with their start and end apart: 31, of which 12 were waited for; matrix products, arithmetic and copies ran while one was open for 2% of the time, Pallas kernels for 16%

profile of v3, /device:TPU:26, one launch (start us, length us, event | category | flops | bytes accessed | tf_op | source)
XLA Modules:
  0.0 154.5 jit_solution(2949185074692206290)
XLA Ops:
  1.3 2.0 %pack.1 = (bf16[4,48,256]{2,1,0:T(8,128)(2,1)}, bf16[4,48,256]{2,1,0:T(8,128)(2,1)}, bf16[4,48,256]{2,1,0:T(8,128)(2,1)}, bf16[4,48,256]{2,1,0:T(8,128)(2,1)}, bf16[4,64,768]{2,1,0:T(8,128)(2,1)}) custom-call(s32[5]{0:T(128)} %stack.23.refs_0_, bf16[48,4096]{1,0:T(8,128)(2,1)} %refs_1_.2, bf16[32,768]{1,0:T(8,128)(2,1)} %bitcast.20, bf16[32,768]{1,0:T(8,128)(2,1)} %bitcast.21), custom_call_target="tpu_custom_call" | custom-call | tf_op jit(solution)/shard_map/pack/pallas_call | solution.py:65
  3.4 0.7 collective-permute-start
  4.1 1.4 collective-permute-start.2
  5.5 4.6 %all-to-all-start = ((bf16[4,64,768]{2,1,0:T(8,128)(2,1)}), bf16[4,64,768]{2,1,0:T(8,128)(2,1)S(1)}, u32[]{:S(2)}, u32[]{:S(2)}) async-start(bf16[4,64,768]{2,1,0:T(8,128)(2,1)} %get-tuple-element.45), calls=%async_computation | async-start | bytes 786432 | tf_op jit(solution)/shard_map/all_to_all | solution.py:692
  10.8 0.9 copy-done.15
  11.7 1.1 token_block.1
  12.8 5.9 %collective-permute-start.5 = (bf16[4,2,96,256]{3,2,1,0:T(8,128)(2,1)S(1)}, bf16[4,2,96,256]{3,2,1,0:T(8,128)(2,1)S(1)}, u32[]{:S(2)}, u32[]{:S(2)}) collective-permute-start(bf16[4,2,96,256]{3,2,1,0:T(8,128)(2,1)S(1)} %get-tuple-element.46.refs_6_.refs_1_), channel_id=1, source_target_pairs={{0,14},{1,15},{2,0},{3,1},{4,2},{5,3},{6,4},{7,5},{8,6},{9,7},{10,... | collective-permute-start | bytes 1179656 | tf_op jit(solution)/shard_map/ppermute | solution.py:26
  20.7 0.8 dynamic-slice_bitcast_fusion
  21.5 1.0 constant_dynamic-slice_fusion
  23.9 1.1 copy-done.17
  25.0 1.1 copy-done.18
  26.8 6.4 %attend.1 = (bf16[768,384]{1,0:T(8,128)(2,1)S(1)}, bf16[768,128]{1,0:T(8,128)(2,1)S(1)}, bf16[2,64,768]{2,1,0:T(8,128)(2,1)S(1)}, f32[2,64,768]{2,1,0:T(8,128)S(1)}) custom-call(s32[5]{0:T(128)S(1)} %copy-done.14, bf16[4,64,768]{2,1,0:T(8,128)(2,1)S(1)} %all-to-all-done.refs_1_, bf16[768,512]{1,0:T(8,128)(2,1)S(1)} %copy-done.16, ...), custom_call_target="tpu_custom_call" | custom-call | flops 1000000000 | tf_op jit(solution)/shard_map/attend/pallas_call | solution.py:65
  34.7 1.7 %repeat.2 = bf16[4,288,512]{2,1,0:T(8,128)(2,1)} custom-call(s32[5]{0:T(128)S(1)} %copy-done.14, bf16[288,512]{1,0:T(8,128)(2,1)S(1)} %collective-permute-done.3.refs_1_, bf16[768,384]{1,0:T(8,128)(2,1)S(1)} %get-tuple-element.47.refs_2_, bf16[4,2,96,256]{3,2,1,0:T(8,128)(2,1)S(1)} %collective-permute-done.4.refs_3_.refs_2_, ...), custom_call_target="tpu_custom_call" | custom-call | tf_op jit(solution)/shard_map/repeat/pallas_call | solution.py:65
  36.4 5.0 %all-to-all-start.1 = ((bf16[4,288,512]{2,1,0:T(8,128)(2,1)}), bf16[4,288,512]{2,1,0:T(8,128)(2,1)S(1)}, u32[]{:S(2)}, u32[]{:S(2)}) async-start(bf16[4,288,512]{2,1,0:T(8,128)(2,1)} %repeat.2), calls=%async_computation.1 | async-start | bytes 2359296 | tf_op jit(solution)/shard_map/all_to_all | solution.py:712
  41.3 1.5 collective-permute-start.9
  42.8 3.2 %collective-permute-start.8 = (bf16[4,2,96,256]{3,2,1,0:T(8,128)(2,1)S(1)}, bf16[4,2,96,256]{3,2,1,0:T(8,128)(2,1)S(1)}, u32[]{:S(2)}, u32[]{:S(2)}) collective-permute-start(bf16[4,2,96,256]{3,2,1,0:T(8,128)(2,1)S(1)} %collective-permute-done.5.refs_4_.refs_3_), channel_id=1, source_target_pairs={{0,14},{1,15},{2,0},{3,1},{4,2},{5,3},{6,4},{7,5},{8,6},{9,7},{10,... | collective-permute-start | bytes 1179656 | tf_op jit(solution)/shard_map/ppermute | solution.py:26
  46.1 10.9 %collective-permute-done.6.refs_2_ = bf16[2,64,768]{2,1,0:T(8,128)(2,1)S(1)} collective-permute-done((bf16[2,64,768]{2,1,0:T(8,128)(2,1)S(1)}, bf16[2,64,768]{2,1,0:T(8,128)(2,1)S(1)}, u32[]{:S(2)}, u32[]{:S(2)}) %collective-permute-start.6) | collective-permute-done | bytes 196640 | tf_op jit(solution)/shard_map/ppermute | solution.py:31
  57.1 1.0 copy-done.10
  61.2 2.5 %collective-permute-start.14 = (bf16[4,2,96,256]{3,2,1,0:T(8,128)(2,1)S(1)}, bf16[4,2,96,256]{3,2,1,0:T(8,128)(2,1)S(1)}, u32[]{:S(2)}, u32[]{:S(2)}) collective-permute-start(bf16[4,2,96,256]{3,2,1,0:T(8,128)(2,1)S(1)} %copy-done.6), channel_id=1, source_target_pairs={{0,14},{1,15},{2,0},{3,1},{4,2},{5,3},{6,4},{7,5},{8,6},{9,7},{10,... | collective-permute-start | bytes 1179656 | tf_op jit(solution)/shard_map/ppermute | solution.py:26
  63.8 0.7 collective-permute-start.12
  64.5 1.3 collective-permute-start.11
  65.8 2.2 %copy-done.2 = bf16[4096,512]{1,0:T(8,128)(2,1)S(1)} copy-done((bf16[4096,512]{1,0:T(8,128)(2,1)S(1)}, bf16[4096,512]{1,0:T(8,128)(2,1)}, u32[]{:S(2)}) %copy-start.2) | copy-done | bytes 4194328
  68.0 1.5 gather_weights.1
  69.5 5.6 %early_parts.1 = (f32[8,96,2048]{2,1,0:T(8,128)S(1)}, bf16[768,896]{1,0:T(8,128)(2,1)S(1)}) custom-call(s32[5]{0:T(128)S(1)} %copy-done.14, bf16[2048,1024]{1,0:T(8,128)(2,1)S(1)} %get-tuple-element.51.refs_1_, bf16[768,384]{1,0:T(8,128)(2,1)S(1)} %get-tuple-element.47.refs_2_, bf16[768,128]{1,0:T(8,128)(2,1)S(1)} %get-tuple-element.53.refs_3_, ...), custom_call_target="tpu_custom_call" | custom-call | flops 1000000000 | tf_op jit(solution)/shard_map/early_parts/pallas_call | solution.py:65
  76.7 1.0 first_parts.1
  78.3 1.3 collective-permute-start.17
  79.6 2.0 %collective-permute-start.18 = (bf16[2,2,96,256]{3,2,1,0:T(8,128)(2,1)S(1)}, bf16[2,2,96,256]{3,2,1,0:T(8,128)(2,1)S(1)}, u32[]{:S(2)}, u32[]{:S(2)}) collective-permute-start(bf16[2,2,96,256]{3,2,1,0:T(8,128)(2,1)S(1)} %get-tuple-element.60), channel_id=1, source_target_pairs={{0,14},{1,15},{2,0},{3,1},{4,2},{5,3},{6,4},{7,5},{8,6},{9,7},{10,... | collective-permute-start | bytes 589832 | tf_op jit(solution)/shard_map/ppermute | solution.py:26
  81.6 1.2 collective-permute-start.16
  82.9 0.8 collective-permute-start.15
  83.6 3.4 %rest_parts.1.refs_12_.refs_3_.refs_4_ = bf16[7,96,2048]{2,1,0:T(8,128)(2,1)S(1)} custom-call(s32[5]{0:T(128)S(1)} %copy-done.14, bf16[2048,1024]{1,0:T(8,128)(2,1)S(1)} %get-tuple-element.51.refs_1_, bf16[128,2048]{1,0:T(8,128)(2,1)S(1)} %get-tuple-element.52.refs_2_, f32[8,96,2048]{2,1,0:T(8,128)S(1)} %get-tuple-element.54.refs_5_.refs_3_, ...), custom_call_target="tpu_custom_call" | custom-call | flops 1000000000 | tf_op jit(solution)/shard_map/rest_parts/pallas_call | solution.py:65
  87.4 3.5 %collective-permute-done.16.refs_14_.refs_2_ = bf16[96,1024]{1,0:T(8,128)(2,1)S(1)} collective-permute-done((bf16[96,1024]{1,0:T(8,128)(2,1)S(1)}, bf16[96,1024]{1,0:T(8,128)(2,1)S(1)}, u32[]{:S(2)}, u32[]{:S(2)}) %collective-permute-start.16) | collective-permute-done | bytes 196640 | tf_op jit(solution)/shard_map/ppermute | solution.py:26
  91.1 6.9 %wgrad_parts.1.refs_5_ = bf16[4,256,1152]{2,1,0:T(8,128)(2,1)S(1)} custom-call(s32[5]{0:T(128)S(1)} %copy-done.14, bf16[4,2,96,256]{3,2,1,0:T(8,128)(2,1)S(1)} %copy-done.20, bf16[4,2,96,256]{3,2,1,0:T(8,128)(2,1)S(1)} %copy-done.4, bf16[4,2,96,256]{3,2,1,0:T(8,128)(2,1)S(1)} %collective-permute-done.5.refs_4_.refs_3_, ...), custom_call_target="tpu_custom_call" | custom-call | flops 10000000000 | tf_op jit(solution)/shard_map/wgrad_parts/pallas_call | solution.py:65
  98.0 1.4 copy-done
  99.4 7.2 %all-to-all-start.2 = ((bf16[8,128,1152]{2,1,0:T(8,128)(2,1)}), bf16[8,128,1152]{2,1,0:T(8,128)(2,1)}, u32[]{:S(2)}, u32[]{:S(2)}) async-start(bf16[8,128,1152]{2,1,0:T(8,128)(2,1)} %bitcast.17), calls=%async_computation.2 | async-start | bytes 4718592 | tf_op jit(solution)/shard_map/all_to_all | solution.py:743
  106.6 1.7 %copy-done.1 = bf16[4,256,1152]{2,1,0:T(8,128)(2,1)S(1)} copy-done((bf16[4,256,1152]{2,1,0:T(8,128)(2,1)S(1)}, bf16[4,256,1152]{2,1,0:T(8,128)(2,1)}, u32[]{:S(2)}) %copy-start.1) | copy-done | bytes 2359320
  109.2 3.1 %collective-permute-start.21 = (bf16[96,2048]{1,0:T(8,128)(2,1)S(1)}, bf16[96,2048]{1,0:T(8,128)(2,1)S(1)}, u32[]{:S(2)}, u32[]{:S(2)}) collective-permute-start(bf16[96,2048]{1,0:T(8,128)(2,1)S(1)} %get-tuple-element.62), channel_id=1, source_target_pairs={{0,14},{1,15},{2,0},{3,1},{4,2},{5,3},{6,4},{7,5},{8,6},{9,7},{10,... | collective-permute-start | bytes 1179656 | tf_op jit(solution)/shard_map/ppermute | solution.py:26
  112.3 7.8 %collective-permute-done.20.refs_1_ = bf16[96,2048]{1,0:T(8,128)(2,1)S(1)} collective-permute-done((bf16[96,2048]{1,0:T(8,128)(2,1)S(1)}, bf16[96,2048]{1,0:T(8,128)(2,1)S(1)}, u32[]{:S(2)}, u32[]{:S(2)}) %collective-permute-start.20) | collective-permute-done | bytes 393248 | tf_op jit(solution)/shard_map/ppermute | solution.py:26
  120.9 3.2 %collective-permute-start.23 = (bf16[96,2048]{1,0:T(8,128)(2,1)S(1)}, bf16[96,2048]{1,0:T(8,128)(2,1)S(1)}, u32[]{:S(2)}, u32[]{:S(2)}) collective-permute-start(bf16[96,2048]{1,0:T(8,128)(2,1)S(1)} %get-tuple-element.64), channel_id=1, source_target_pairs={{0,14},{1,15},{2,0},{3,1},{4,2},{5,3},{6,4},{7,5},{8,6},{9,7},{10,... | collective-permute-start | bytes 1179656 | tf_op jit(solution)/shard_map/ppermute | solution.py:26
  124.1 7.0 %collective-permute-done.22.refs_1_ = bf16[96,2048]{1,0:T(8,128)(2,1)S(1)} collective-permute-done((bf16[96,2048]{1,0:T(8,128)(2,1)S(1)}, bf16[96,2048]{1,0:T(8,128)(2,1)S(1)}, u32[]{:S(2)}, u32[]{:S(2)}) %collective-permute-start.22) | collective-permute-done | bytes 393248 | tf_op jit(solution)/shard_map/ppermute | solution.py:26
  131.1 1.5 ring_step.6
  132.6 3.0 %collective-permute-start.25 = (bf16[96,2048]{1,0:T(8,128)(2,1)}, bf16[96,2048]{1,0:T(8,128)(2,1)S(1)}, u32[]{:S(2)}, u32[]{:S(2)}) collective-permute-start(bf16[96,2048]{1,0:T(8,128)(2,1)} %get-tuple-element.66), channel_id=1, source_target_pairs={{0,14},{1,15},{2,0},{3,1},{4,2},{5,3},{6,4},{7,5},{8,6},{9,7},{10,... | collective-permute-start | bytes 1179656 | tf_op jit(solution)/shard_map/ppermute | solution.py:26
  136.0 2.0 %wgrad_sum.1 = (f32[128,512]{1,0:T(8,128)S(1)}, f32[128,128]{1,0:T(8,128)S(1)}, bf16[128,640]{1,0:T(8,128)(2,1)S(1)}) custom-call(s32[5]{0:T(128)S(1)} %copy-done.14, bf16[8,128,1152]{2,1,0:T(8,128)(2,1)} %all-to-all-done.2.refs_1_, bf16[96,2048]{1,0:T(8,128)(2,1)} %get-tuple-element.65.refs_2_), custom_call_target="tpu_custom_call" | custom-call | tf_op jit(solution)/shard_map/wgrad_sum/pallas_call | solution.py:65
  137.9 3.4 %collective-permute-done.25.refs_2_ = bf16[96,2048]{1,0:T(8,128)(2,1)S(1)} collective-permute-done((bf16[96,2048]{1,0:T(8,128)(2,1)}, bf16[96,2048]{1,0:T(8,128)(2,1)S(1)}, u32[]{:S(2)}, u32[]{:S(2)}) %collective-permute-start.25) | collective-permute-done | bytes 393248 | tf_op jit(solution)/shard_map/ppermute | solution.py:26
  141.3 3.5 %collective-permute-done.24.refs_1_ = bf16[96,2048]{1,0:T(8,128)(2,1)S(1)} collective-permute-done((bf16[96,2048]{1,0:T(8,128)(2,1)}, bf16[96,2048]{1,0:T(8,128)(2,1)S(1)}, u32[]{:S(2)}, u32[]{:S(2)}) %collective-permute-start.24) | collective-permute-done | bytes 393248 | tf_op jit(solution)/shard_map/ppermute | solution.py:26
  145.5 0.9 collective-permute-start.26
  146.4 1.2 collective-permute-start.27
  147.6 5.4 %collective-permute-done.27.refs_5_ = bf16[128,640]{1,0:T(8,128)(2,1)S(1)} collective-permute-done((bf16[128,640]{1,0:T(8,128)(2,1)S(1)}, bf16[128,640]{1,0:T(8,128)(2,1)S(1)}, u32[]{:S(2)}, u32[]{:S(2)}) %collective-permute-start.27) | collective-permute-done | bytes 163872 | tf_op jit(solution)/shard_map/ppermute | solution.py:31
  153.0 1.5 final.1
  (85 shorter events, 13.4 us)
Async XLA Ops:
  3.4 20.5 %copy-start.14 = (s32[5]{0:T(128)S(1)}, s32[5]{0:T(128)}, u32[]{:S(2)}) copy-start(s32[5]{0:T(128)} %stack.23.refs_0_) | copy-start | bytes 64
  3.4 20.5 %copy-start.16 = (bf16[768,512]{1,0:T(8,128)(2,1)S(1)}, bf16[768,512]{1,0:T(8,128)(2,1)}, u32[]{:S(2)}) copy-start(bf16[768,512]{1,0:T(8,128)(2,1)} %refs_2_.1) | copy-start | bytes 2359300
  3.4 6.8 %collective-permute-start = (bf16[4,48,256]{2,1,0:T(8,128)(2,1)}, bf16[4,48,256]{2,1,0:T(8,128)(2,1)S(1)}, u32[]{:S(2)}, u32[]{:S(2)}) collective-permute-start(bf16[4,48,256]{2,1,0:T(8,128)(2,1)} %get-tuple-element.41), channel_id=1, source_target_pairs={{0,1},{1,0},{2,3},{3,2},{4,5},{5,4},{6,7},{7,6},{8,9},{9,8},{10,11... | collective-permute-start | bytes 294920 | tf_op jit(solution)/shard_map/ppermute | solution.py:39
  4.1 6.1 %collective-permute-start.1 = (bf16[4,48,256]{2,1,0:T(8,128)(2,1)}, bf16[4,48,256]{2,1,0:T(8,128)(2,1)S(1)}, u32[]{:S(2)}, u32[]{:S(2)}) collective-permute-start(bf16[4,48,256]{2,1,0:T(8,128)(2,1)} %get-tuple-element.42), channel_id=1, source_target_pairs={{0,16},{1,17},{2,18},{3,19},{4,20},{5,21},{6,22},{7,23},{8,24},{9,... | collective-permute-start | bytes 294920 | tf_op jit(solution)/shard_map/ppermute | solution.py:39
  4.1 6.1 %collective-permute-start.2 = (bf16[4,48,256]{2,1,0:T(8,128)(2,1)}, bf16[4,48,256]{2,1,0:T(8,128)(2,1)S(1)}, u32[]{:S(2)}, u32[]{:S(2)}) collective-permute-start(bf16[4,48,256]{2,1,0:T(8,128)(2,1)} %get-tuple-element.43), channel_id=1, source_target_pairs={{0,17},{1,16},{2,19},{3,18},{4,21},{5,20},{6,23},{7,22},{8,25},{9,... | collective-permute-start | bytes 294920 | tf_op jit(solution)/shard_map/ppermute | solution.py:39
  5.5 18.3 %all-to-all-start = ((bf16[4,64,768]{2,1,0:T(8,128)(2,1)}), bf16[4,64,768]{2,1,0:T(8,128)(2,1)S(1)}, u32[]{:S(2)}, u32[]{:S(2)}) async-start(bf16[4,64,768]{2,1,0:T(8,128)(2,1)} %get-tuple-element.45), calls=%async_computation | async-start | bytes 786432 | tf_op jit(solution)/shard_map/all_to_all | solution.py:692
  12.8 20.4 %copy-start.19 = (bf16[4,2,96,256]{3,2,1,0:T(8,128)(2,1)}, bf16[4,2,96,256]{3,2,1,0:T(8,128)(2,1)S(1)}, u32[]{:S(2)}) copy-start(bf16[4,2,96,256]{3,2,1,0:T(8,128)(2,1)S(1)} %get-tuple-element.46.refs_6_.refs_1_) | copy-start | bytes 1179652
  12.8 21.9 %collective-permute-start.5 = (bf16[4,2,96,256]{3,2,1,0:T(8,128)(2,1)S(1)}, bf16[4,2,96,256]{3,2,1,0:T(8,128)(2,1)S(1)}, u32[]{:S(2)}, u32[]{:S(2)}) collective-permute-start(bf16[4,2,96,256]{3,2,1,0:T(8,128)(2,1)S(1)} %get-tuple-element.46.refs_6_.refs_1_), channel_id=1, source_target_pairs={{0,14},{1,15},{2,0},{3,1},{4,2},{5,3},{6,4},{7,5},{8,6},{9,7},{10,... | collective-permute-start | bytes 1179656 | tf_op jit(solution)/shard_map/ppermute | solution.py:26
  18.7 16.0 %collective-permute-start.4 = (bf16[4,2,96,256]{3,2,1,0:T(8,128)(2,1)S(1)}, bf16[4,2,96,256]{3,2,1,0:T(8,128)(2,1)S(1)}, u32[]{:S(2)}, u32[]{:S(2)}) collective-permute-start(bf16[4,2,96,256]{3,2,1,0:T(8,128)(2,1)S(1)} %get-tuple-element.46.refs_6_.refs_1_), channel_id=1, source_target_pairs={{0,2},{1,3},{2,4},{3,5},{4,6},{5,7},{6,8},{7,9},{8,10},{9,11},{10,... | collective-permute-start | bytes 1179656 | tf_op jit(solution)/shard_map/ppermute | solution.py:26
  23.3 11.4 %collective-permute-start.3 = (bf16[288,512]{1,0:T(8,128)(2,1)}, bf16[288,512]{1,0:T(8,128)(2,1)S(1)}, u32[]{:S(2)}, u32[]{:S(2)}) collective-permute-start(bf16[288,512]{1,0:T(8,128)(2,1)} %maximum_maximum_fusion), channel_id=1, source_target_pairs={{0,1},{1,0},{2,3},{3,2},{4,5},{5,4},{6,7},{7,6},{8,9},{9,8},{10,11... | collective-permute-start | bytes 884744 | tf_op jit(solution)/shard_map/ppermute | solution.py:31
  23.8 1.1 copy-start.17
  25.0 1.1 copy-start.18
  34.7 11.3 %copy-start.3 = (bf16[4,2,96,256]{3,2,1,0:T(8,128)(2,1)}, bf16[4,2,96,256]{3,2,1,0:T(8,128)(2,1)S(1)}, u32[]{:S(2)}) copy-start(bf16[4,2,96,256]{3,2,1,0:T(8,128)(2,1)S(1)} %collective-permute-done.4.refs_3_.refs_2_) | copy-start | bytes 1179652
  36.4 9.7 %copy-start.22 = (bf16[2,64,768]{2,1,0:T(8,128)(2,1)S(1)}, bf16[2,64,768]{2,1,0:T(8,128)(2,1)}, u32[]{:S(2)}) copy-start(bf16[2,64,768]{2,1,0:T(8,128)(2,1)} %copy-done.21) | copy-start | bytes 589828
  36.4 23.8 %all-to-all-start.1 = ((bf16[4,288,512]{2,1,0:T(8,128)(2,1)}), bf16[4,288,512]{2,1,0:T(8,128)(2,1)S(1)}, u32[]{:S(2)}, u32[]{:S(2)}) async-start(bf16[4,288,512]{2,1,0:T(8,128)(2,1)} %repeat.2), calls=%async_computation.1 | async-start | bytes 2359296 | tf_op jit(solution)/shard_map/all_to_all | solution.py:712
  41.3 15.8 %collective-permute-start.9 = (bf16[768,384]{1,0:T(8,128)(2,1)S(1)}, bf16[768,384]{1,0:T(8,128)(2,1)S(1)}, u32[]{:S(2)}, u32[]{:S(2)}) collective-permute-start(bf16[768,384]{1,0:T(8,128)(2,1)S(1)} %get-tuple-element.47.refs_2_), channel_id=1, source_target_pairs={{0,1},{1,0},{2,3},{3,2},{4,5},{5,4},{6,7},{7,6},{8,9},{9,8},{10,11... | collective-permute-start | bytes 1769480 | tf_op jit(solution)/shard_map/ppermute | solution.py:31
  42.8 14.3 %collective-permute-start.8 = (bf16[4,2,96,256]{3,2,1,0:T(8,128)(2,1)S(1)}, bf16[4,2,96,256]{3,2,1,0:T(8,128)(2,1)S(1)}, u32[]{:S(2)}, u32[]{:S(2)}) collective-permute-start(bf16[4,2,96,256]{3,2,1,0:T(8,128)(2,1)S(1)} %collective-permute-done.5.refs_4_.refs_3_), channel_id=1, source_target_pairs={{0,14},{1,15},{2,0},{3,1},{4,2},{5,3},{6,4},{7,5},{8,6},{9,7},{10,... | collective-permute-start | bytes 1179656 | tf_op jit(solution)/shard_map/ppermute | solution.py:26
  46.0 11.1 %collective-permute-start.7 = (bf16[4,2,96,256]{3,2,1,0:T(8,128)(2,1)S(1)}, bf16[4,2,96,256]{3,2,1,0:T(8,128)(2,1)S(1)}, u32[]{:S(2)}, u32[]{:S(2)}) collective-permute-start(bf16[4,2,96,256]{3,2,1,0:T(8,128)(2,1)S(1)} %collective-permute-done.4.refs_3_.refs_2_), channel_id=1, source_target_pairs={{0,2},{1,3},{2,4},{3,5},{4,6},{5,7},{6,8},{7,9},{8,10},{9,11},{10,... | collective-permute-start | bytes 1179656 | tf_op jit(solution)/shard_map/ppermute | solution.py:26
  46.0 11.0 %collective-permute-start.6 = (bf16[2,64,768]{2,1,0:T(8,128)(2,1)S(1)}, bf16[2,64,768]{2,1,0:T(8,128)(2,1)S(1)}, u32[]{:S(2)}, u32[]{:S(2)}) collective-permute-start(bf16[2,64,768]{2,1,0:T(8,128)(2,1)S(1)} %copy-done.22), channel_id=1, source_target_pairs={{0,2},{1,3},{2,0},{3,1},{4,6},{5,7},{6,4},{7,5},{8,10},{9,11},{10,... | collective-permute-start | bytes 589832 | tf_op jit(solution)/shard_map/ppermute | solution.py:31
  57.1 1.0 copy-start.10
  60.2 1.0 copy-start.6
  60.2 3.5 %copy-start.8 = (bf16[4,2,96,256]{3,2,1,0:T(8,128)(2,1)S(1)}, bf16[4,2,96,256]{3,2,1,0:T(8,128)(2,1)}, u32[]{:S(2)}) copy-start(bf16[4,2,96,256]{3,2,1,0:T(8,128)(2,1)} %copy-done.7) | copy-start | bytes 1179652
  60.2 5.6 %copy-start.11 = (bf16[4096,32]{0,1:T(8,128)(2,1)S(1)}, bf16[4096,32]{0,1:T(8,128)(2,1)}, u32[]{:S(2)}) copy-start(bf16[4096,32]{0,1:T(8,128)(2,1)} %param.18) | copy-start | bytes 786436
  60.2 5.6 %copy-start.12 = (bf16[4096,32]{0,1:T(8,128)(2,1)S(1)}, bf16[4096,32]{0,1:T(8,128)(2,1)}, u32[]{:S(2)}) copy-start(bf16[4096,32]{0,1:T(8,128)(2,1)} %param.19) | copy-start | bytes 786436
  60.8 5.0 %collective-permute-start.10 = (bf16[4,288,512]{2,1,0:T(8,128)(2,1)S(1)}, bf16[4,288,512]{2,1,0:T(8,128)(2,1)S(1)}, u32[]{:S(2)}, u32[]{:S(2)}) collective-permute-start(bf16[4,288,512]{2,1,0:T(8,128)(2,1)S(1)} %repeat.3.refs_4_), channel_id=1, source_target_pairs={{0,16},{16,0},{32,48},{48,32},{64,80},{80,64},{96,112},{112,96},{1... | collective-permute-start | bytes 3538952 | tf_op jit(solution)/shard_map/ppermute | solution.py:31
  61.2 14.0 %collective-permute-start.14 = (bf16[4,2,96,256]{3,2,1,0:T(8,128)(2,1)S(1)}, bf16[4,2,96,256]{3,2,1,0:T(8,128)(2,1)S(1)}, u32[]{:S(2)}, u32[]{:S(2)}) collective-permute-start(bf16[4,2,96,256]{3,2,1,0:T(8,128)(2,1)S(1)} %copy-done.6), channel_id=1, source_target_pairs={{0,14},{1,15},{2,0},{3,1},{4,2},{5,3},{6,4},{7,5},{8,6},{9,7},{10,... | collective-permute-start | bytes 1179656 | tf_op jit(solution)/shard_map/ppermute | solution.py:26
  63.7 12.2 %collective-permute-start.13 = (bf16[4,2,96,256]{3,2,1,0:T(8,128)(2,1)S(1)}, bf16[4,2,96,256]{3,2,1,0:T(8,128)(2,1)S(1)}, u32[]{:S(2)}, u32[]{:S(2)}) collective-permute-start(bf16[4,2,96,256]{3,2,1,0:T(8,128)(2,1)S(1)} %copy-done.8), channel_id=1, source_target_pairs={{0,2},{1,3},{2,4},{3,5},{4,6},{5,7},{6,8},{7,9},{8,10},{9,11},{10,... | collective-permute-start | bytes 1179656 | tf_op jit(solution)/shard_map/ppermute | solution.py:26
  63.8 11.4 %collective-permute-start.12 = (bf16[768,128]{1,0:T(8,128)(2,1)S(1)}, bf16[768,128]{1,0:T(8,128)(2,1)S(1)}, u32[]{:S(2)}, u32[]{:S(2)}) collective-permute-start(bf16[768,128]{1,0:T(8,128)(2,1)S(1)} %get-tuple-element.53.refs_3_), channel_id=1, source_target_pairs={{0,1},{1,0},{2,3},{3,2},{4,5},{5,4},{6,7},{7,6},{8,9},{9,8},{10,11... | collective-permute-start | bytes 589832 | tf_op jit(solution)/shard_map/ppermute | solution.py:31
  64.5 11.3 %collective-permute-start.11 = (bf16[2,64,768]{2,1,0:T(8,128)(2,1)S(1)}, bf16[2,64,768]{2,1,0:T(8,128)(2,1)S(1)}, u32[]{:S(2)}, u32[]{:S(2)}) collective-permute-start(bf16[2,64,768]{2,1,0:T(8,128)(2,1)S(1)} %get-tuple-element.50.refs_2_.refs_6_), channel_id=1, source_target_pairs={{0,1},{1,0},{2,3},{3,2},{4,5},{5,4},{6,7},{7,6},{8,9},{9,8},{10,11... | collective-permute-start | bytes 589832 | tf_op jit(solution)/shard_map/ppermute | solution.py:31
  65.8 2.2 %copy-start.2 = (bf16[4096,512]{1,0:T(8,128)(2,1)S(1)}, bf16[4096,512]{1,0:T(8,128)(2,1)}, u32[]{:S(2)}) copy-start(bf16[4096,512]{1,0:T(8,128)(2,1)} %refs_1_.3) | copy-start | bytes 12582916
  76.6 14.5 %collective-permute-start.19 = (bf16[768,1152]{1,0:T(8,128)(2,1)S(1)}, bf16[768,1152]{1,0:T(8,128)(2,1)S(1)}, u32[]{:S(2)}, u32[]{:S(2)}) collective-permute-start(bf16[768,1152]{1,0:T(8,128)(2,1)S(1)} %kv_final.1.refs_4_.refs_10_), channel_id=1, source_target_pairs={{0,16},{16,0},{32,48},{48,32},{64,80},{80,64},{96,112},{112,96},{1... | collective-permute-start | bytes 5308424 | tf_op jit(solution)/shard_map/ppermute | solution.py:31
  78.3 9.0 %collective-permute-start.17 = (bf16[2,2,96,256]{3,2,1,0:T(8,128)(2,1)S(1)}, bf16[2,2,96,256]{3,2,1,0:T(8,128)(2,1)S(1)}, u32[]{:S(2)}, u32[]{:S(2)}) collective-permute-start(bf16[2,2,96,256]{3,2,1,0:T(8,128)(2,1)S(1)} %get-tuple-element.59), channel_id=1, source_target_pairs={{0,2},{1,3},{2,4},{3,5},{4,6},{5,7},{6,8},{7,9},{8,10},{9,11},{10,... | collective-permute-start | bytes 589832 | tf_op jit(solution)/shard_map/ppermute | solution.py:26
  79.6 7.7 %collective-permute-start.18 = (bf16[2,2,96,256]{3,2,1,0:T(8,128)(2,1)S(1)}, bf16[2,2,96,256]{3,2,1,0:T(8,128)(2,1)S(1)}, u32[]{:S(2)}, u32[]{:S(2)}) collective-permute-start(bf16[2,2,96,256]{3,2,1,0:T(8,128)(2,1)S(1)} %get-tuple-element.60), channel_id=1, source_target_pairs={{0,14},{1,15},{2,0},{3,1},{4,2},{5,3},{6,4},{7,5},{8,6},{9,7},{10,... | collective-permute-start | bytes 589832 | tf_op jit(solution)/shard_map/ppermute | solution.py:26
  81.6 9.2 %collective-permute-start.16 = (bf16[96,1024]{1,0:T(8,128)(2,1)S(1)}, bf16[96,1024]{1,0:T(8,128)(2,1)S(1)}, u32[]{:S(2)}, u32[]{:S(2)}) collective-permute-start(bf16[96,1024]{1,0:T(8,128)(2,1)S(1)} %get-tuple-element.58), channel_id=1, source_target_pairs={{0,14},{1,15},{2,0},{3,1},{4,2},{5,3},{6,4},{7,5},{8,6},{9,7},{10,... | collective-permute-start | bytes 589832 | tf_op jit(solution)/shard_map/ppermute | solution.py:26
  82.9 8.2 %copy-start.4 = (bf16[4,2,96,256]{3,2,1,0:T(8,128)(2,1)S(1)}, bf16[4,2,96,256]{3,2,1,0:T(8,128)(2,1)}, u32[]{:S(2)}) copy-start(bf16[4,2,96,256]{3,2,1,0:T(8,128)(2,1)} %copy-done.3) | copy-start | bytes 1179652
  82.9 8.2 %copy-start.20 = (bf16[4,2,96,256]{3,2,1,0:T(8,128)(2,1)S(1)}, bf16[4,2,96,256]{3,2,1,0:T(8,128)(2,1)}, u32[]{:S(2)}) copy-start(bf16[4,2,96,256]{3,2,1,0:T(8,128)(2,1)} %copy-done.19) | copy-start | bytes 1179652
  82.9 8.2 %collective-permute-start.15 = (bf16[96,1024]{1,0:T(8,128)(2,1)S(1)}, bf16[96,1024]{1,0:T(8,128)(2,1)S(1)}, u32[]{:S(2)}, u32[]{:S(2)}) collective-permute-start(bf16[96,1024]{1,0:T(8,128)(2,1)S(1)} %get-tuple-element.57.refs_5_), channel_id=1, source_target_pairs={{0,2},{1,3},{2,4},{3,5},{4,6},{5,7},{6,8},{7,9},{8,10},{9,11},{10,... | collective-permute-start | bytes 589832 | tf_op jit(solution)/shard_map/ppermute | solution.py:26
  98.0 1.4 copy-start
  99.4 36.5 %all-to-all-start.2 = ((bf16[8,128,1152]{2,1,0:T(8,128)(2,1)}), bf16[8,128,1152]{2,1,0:T(8,128)(2,1)}, u32[]{:S(2)}, u32[]{:S(2)}) async-start(bf16[8,128,1152]{2,1,0:T(8,128)(2,1)} %bitcast.17), calls=%async_computation.2 | async-start | bytes 4718592 | tf_op jit(solution)/shard_map/all_to_all | solution.py:743
  106.6 1.7 %copy-start.1 = (bf16[4,256,1152]{2,1,0:T(8,128)(2,1)S(1)}, bf16[4,256,1152]{2,1,0:T(8,128)(2,1)}, u32[]{:S(2)}) copy-start(bf16[4,256,1152]{2,1,0:T(8,128)(2,1)} %copy-done) | copy-start | bytes 7077892
  109.0 11.1 %collective-permute-start.20 = (bf16[96,2048]{1,0:T(8,128)(2,1)S(1)}, bf16[96,2048]{1,0:T(8,128)(2,1)S(1)}, u32[]{:S(2)}, u32[]{:S(2)}) collective-permute-start(bf16[96,2048]{1,0:T(8,128)(2,1)S(1)} %get-tuple-element.61), channel_id=1, source_target_pairs={{0,2},{1,3},{2,4},{3,5},{4,6},{5,7},{6,8},{7,9},{8,10},{9,11},{10,... | collective-permute-start | bytes 1179656 | tf_op jit(solution)/shard_map/ppermute | solution.py:26
  109.2 10.9 %collective-permute-start.21 = (bf16[96,2048]{1,0:T(8,128)(2,1)S(1)}, bf16[96,2048]{1,0:T(8,128)(2,1)S(1)}, u32[]{:S(2)}, u32[]{:S(2)}) collective-permute-start(bf16[96,2048]{1,0:T(8,128)(2,1)S(1)} %get-tuple-element.62), channel_id=1, source_target_pairs={{0,14},{1,15},{2,0},{3,1},{4,2},{5,3},{6,4},{7,5},{8,6},{9,7},{10,... | collective-permute-start | bytes 1179656 | tf_op jit(solution)/shard_map/ppermute | solution.py:26
  120.8 10.3 %collective-permute-start.22 = (bf16[96,2048]{1,0:T(8,128)(2,1)S(1)}, bf16[96,2048]{1,0:T(8,128)(2,1)S(1)}, u32[]{:S(2)}, u32[]{:S(2)}) collective-permute-start(bf16[96,2048]{1,0:T(8,128)(2,1)S(1)} %get-tuple-element.63), channel_id=1, source_target_pairs={{0,2},{1,3},{2,4},{3,5},{4,6},{5,7},{6,8},{7,9},{8,10},{9,11},{10,... | collective-permute-start | bytes 1179656 | tf_op jit(solution)/shard_map/ppermute | solution.py:26
  120.9 10.2 %collective-permute-start.23 = (bf16[96,2048]{1,0:T(8,128)(2,1)S(1)}, bf16[96,2048]{1,0:T(8,128)(2,1)S(1)}, u32[]{:S(2)}, u32[]{:S(2)}) collective-permute-start(bf16[96,2048]{1,0:T(8,128)(2,1)S(1)} %get-tuple-element.64), channel_id=1, source_target_pairs={{0,14},{1,15},{2,0},{3,1},{4,2},{5,3},{6,4},{7,5},{8,6},{9,7},{10,... | collective-permute-start | bytes 1179656 | tf_op jit(solution)/shard_map/ppermute | solution.py:26
  132.6 8.7 %collective-permute-start.25 = (bf16[96,2048]{1,0:T(8,128)(2,1)}, bf16[96,2048]{1,0:T(8,128)(2,1)S(1)}, u32[]{:S(2)}, u32[]{:S(2)}) collective-permute-start(bf16[96,2048]{1,0:T(8,128)(2,1)} %get-tuple-element.66), channel_id=1, source_target_pairs={{0,14},{1,15},{2,0},{3,1},{4,2},{5,3},{6,4},{7,5},{8,6},{9,7},{10,... | collective-permute-start | bytes 1179656 | tf_op jit(solution)/shard_map/ppermute | solution.py:26
  135.6 9.2 %collective-permute-start.24 = (bf16[96,2048]{1,0:T(8,128)(2,1)}, bf16[96,2048]{1,0:T(8,128)(2,1)S(1)}, u32[]{:S(2)}, u32[]{:S(2)}) collective-permute-start(bf16[96,2048]{1,0:T(8,128)(2,1)} %get-tuple-element.65.refs_2_), channel_id=1, source_target_pairs={{0,2},{1,3},{2,4},{3,5},{4,6},{5,7},{6,8},{7,9},{8,10},{9,11},{10,... | collective-permute-start | bytes 1179656 | tf_op jit(solution)/shard_map/ppermute | solution.py:26
  145.5 7.5 %collective-permute-start.26 = (bf16[48,2048]{1,0:T(8,128)(2,1)S(1)}, bf16[48,2048]{1,0:T(8,128)(2,1)S(1)}, u32[]{:S(2)}, u32[]{:S(2)}) collective-permute-start(bf16[48,2048]{1,0:T(8,128)(2,1)S(1)} %get-tuple-element.69), channel_id=1, source_target_pairs={{0,1},{1,0},{2,3},{3,2},{4,5},{5,4},{6,7},{7,6},{8,9},{9,8},{10,11... | collective-permute-start | bytes 589832 | tf_op jit(solution)/shard_map/ppermute | solution.py:31
  146.4 6.6 %collective-permute-start.27 = (bf16[128,640]{1,0:T(8,128)(2,1)S(1)}, bf16[128,640]{1,0:T(8,128)(2,1)S(1)}, u32[]{:S(2)}, u32[]{:S(2)}) collective-permute-start(bf16[128,640]{1,0:T(8,128)(2,1)S(1)} %get-tuple-element.67.refs_5_), channel_id=1, source_target_pairs={{0,1},{1,0},{2,3},{3,2},{4,5},{5,4},{6,7},{7,6},{8,9},{9,8},{10,11... | collective-permute-start | bytes 491528 | tf_op jit(solution)/shard_map/ppermute | solution.py:31
  (7 other events, 5.2 us)

commit v4 on v3

--- a/solution.py
+++ b/solution.py
@@ -113,7 +113,7 @@
 
 
 def block_kernel(quarter, spot, own, side, core, both, out, start):
-    start[0] = ((1 - spot[H]) * 2 + spot[C]) * quarter + spot[X] * (quarter // NX)
+    start[0] = ((1 - spot[H]) * 2 + spot[C]) * quarter + lax.rem(spot[X], 2) * (quarter // 2)
     h = spot[H]
     rows = own.shape[1]
     near = pl.ds(pl.multiple_of(h * rows, rows), rows)
@@ -138,6 +138,16 @@
     )
 
 
+def again_kernel(spot, value, out):
+    out[...] = value[...]
+
+
+def again(spot, value, later):
+    return call(
+        again_kernel, "again", spot, (value,), [VMEM], [shape(value.shape)], [VMEM], later=later
+    )[0]
+
+
 def halves_kernel(spot, up, down, out_up, out_down):
     out_up[...] = up[...]
     out_down[...] = down[...]
@@ -160,32 +170,12 @@
     )
 
 
-def repeat_kernel(spot, value, out):
-    if len(value.shape) == len(out.shape):
-        out[...] = value[...]
-    else:
-        for index in range(out.shape[0]):
-            out[index] = value[...]
-
-
-def repeat(spot, value, times, later):
-    return call(
-        repeat_kernel,
-        "repeat",
-        spot,
-        (value,),
-        [VMEM],
-        [shape((times, *value.shape) if times else value.shape)],
-        [VMEM],
-        later=later,
-    )[0]
-
-
-def weights_kernel(spot, w_query, w_key, w_value, far_own, far_core, out, out_kv, sems):
-    h, c = spot[H], spot[C]
+def weights_kernel(spot, w_query, w_key, w_value, *rest):
+    parts, (out, out_kv, sems) = rest[:4], rest[4:]
+    h, c, side = spot[H], spot[C], lax.rem(spot[X], 2)
     half, q2 = out.shape
     q_w, kv_w = q2 // 2, w_key.shape[0]
-    piece = far_own.shape[1] - kv_w
+    piece = parts[0].shape[0] - 2 * kv_w
     start = pl.multiple_of(h * half, half)
     near = [pl.ds(pl.multiple_of(kind * 2 * kv_w + h * kv_w, kv_w), kv_w) for kind in (0, 1)]
     far = [pl.ds(pl.multiple_of(kind * 2 * kv_w + (1 - h) * kv_w, kv_w), kv_w) for kind in (0, 1)]
@@ -194,19 +184,17 @@
         (w_key.at[:, pl.ds(start, half)], out_kv.at[near[0], :]),
         (w_value.at[:, pl.ds(start, half)], out_kv.at[near[1], :]),
     ]
-    for ref, place in ((far_own, c), (far_core, 1 - c)):
-        for index in range(NX):
-            row = pl.multiple_of(place * (half // 2) + index * piece, piece)
+    places = ((c, side), (c, 1 - side), (1 - c, side), (1 - c, 1 - side))
+    for ref, (core, part) in zip(parts, places):
+        row = pl.multiple_of(core * (half // 2) + part * piece, piece)
+        pairs.append((ref.at[pl.ds(0, piece), :], out.at[pl.ds(row, piece), pl.ds(q_w, q_w)]))
+        for kind in (0, 1):
             pairs.append(
-                (ref.at[index, pl.ds(0, piece), :], out.at[pl.ds(row, piece), pl.ds(q_w, q_w)])
+                (
+                    ref.at[pl.ds(piece + kind * kv_w, kv_w), :],
+                    out_kv.at[far[kind], pl.ds(row, piece)],
+                )
             )
-            for kind in (0, 1):
-                pairs.append(
-                    (
-                        ref.at[index, pl.ds(piece, kv_w), pl.ds(kind * piece, piece)],
-                        out_kv.at[far[kind], pl.ds(row, piece)],
-                    )
-                )
     run_copies(
         [
             pltpu.make_async_copy(source, target, sems.at[index])
@@ -215,17 +203,17 @@
     )
 
 
-def gather_weights(spot, w_query, w_key, w_value, far_own, far_core, later):
+def gather_weights(spot, w_query, w_key, w_value, parts, later):
     width, q_w = w_query.shape
     return call(
         weights_kernel,
         "gather_weights",
         spot,
-        (w_query, w_key, w_value, far_own, far_core),
-        [ANY] * 5,
+        (w_query, w_key, w_value, *parts),
+        [ANY] * 7,
         [shape((width // 2, 2 * q_w)), shape((4 * w_key.shape[0], width // 2))],
         [ANY] * 2,
-        [pltpu.SemaphoreType.DMA((3 + 6 * NX,))],
+        [pltpu.SemaphoreType.DMA((15,))],
         later=later,
     )
 
@@ -266,13 +254,16 @@
         total[0, :, :width] += dot(query_t, dscores, 0, 0)
         total[1, :, :width] += dot(grad_t, probs.astype(BF), 0, 0)
 
-    @pl.when(head < heads - 1)
+    @pl.when(head < heads // 2)
     def _():
         out_a[...] = grads[...]
 
+    @pl.when(head >= heads // 2)
+    def _():
+        out_b[...] = grads[...]
+
     @pl.when(head == heads - 1)
     def _():
-        out_b[...] = grads[...]
         half = DH // 2
         mine = spot[ZB]
         near = pl.ds(pl.multiple_of(mine * half, half), half)
@@ -288,8 +279,8 @@
     cols = pl.BlockSpec((seq, DH), lambda head: (0, head))
     full = lambda a: pl.BlockSpec(a.shape, lambda head: (0,) * len(a.shape))
     outs = [
-        shape((seq, (heads - 1) * DH)),
-        shape((seq, DH)),
+        shape((seq, heads // 2 * DH)),
+        shape((seq, heads // 2 * DH)),
         shape((2, DH // 2, seq)),
         shape((2, DH // 2, seq), F32),
     ]
@@ -301,8 +292,9 @@
         [full(kv), cols, cols, cols, full(norms)],
         outs,
         [
-            pl.BlockSpec((seq, DH), lambda head: (0, jnp.minimum(head, heads - 2))),
-            *[full(out) for out in outs[1:]],
+            pl.BlockSpec((seq, DH), lambda head: (0, jnp.minimum(head, heads // 2 - 1))),
+            pl.BlockSpec((seq, DH), lambda head: (0, jnp.maximum(head - heads // 2, 0))),
+            *[full(out) for out in outs[2:]],
         ],
         [
             pltpu.VMEM((DH, seq), BF),
@@ -537,7 +529,7 @@
 
 def wgrad_kernel(spot, *rest):
     blocks, (up, down), rest = rest[: NZ - 1], rest[NZ - 1 : NZ + 1], rest[NZ + 1 :]
-    pieces, (out, held, lefts, sems, left_sems, last_sems) = rest[:2], rest[2:]
+    pieces, (out, done, held, lefts, sems, left_sems, last_sems) = rest[:2], rest[2:]
     z = spot[Z]
     rows = blocks[0].shape[2]
     places = (0, -1, 1, -2, 2, -3, 3)
@@ -568,6 +560,7 @@
             )
         run_copies(copies)
 
+    done[...] = jnp.zeros_like(done)
     left = lefts[pl.program_id(0)]
     left = left.reshape(left.shape[0] * left.shape[1], left.shape[2])
     right = held[...].reshape(left.shape[0], held.shape[2])
@@ -583,8 +576,11 @@
         spot,
         (*blocks, up, down, here, there),
         [ANY] * (NZ + 3),
-        [shape((NX, wide, depth))],
-        [pl.BlockSpec((1, wide, depth), lambda step: (step, 0, 0))],
+        [shape((NX, wide, depth)), shape((8, DH), F32)],
+        [
+            pl.BlockSpec((1, wide, depth), lambda step: (step, 0, 0)),
+            pl.BlockSpec((8, DH), lambda step: (0, 0)),
+        ],
         [
             pltpu.VMEM((2, seq, depth), BF),
             pltpu.VMEM((NX, 2, seq, wide), BF),
@@ -595,7 +591,7 @@
         grid=(NX,),
         work=10**10,
         later=later,
-    )[0]
+    )
 
 
 def wgrad_sum_kernel(spot, terms, own, own_kv, send):
@@ -693,14 +689,12 @@
     quarter = tokens.shape[1] // 4
     block, start = token_block(spot, (own, side, core, both), quarter, [])
     up1, down1 = shift(block, "tensor", 2), shift(block, "tensor", -2)
-    piece = quarter // NX
+    piece = quarter // 2
     row = start[0]
     w_send = jnp.concatenate(
         [
             lax.dynamic_slice_in_dim(w_query, row, piece, 0),
-            jnp.concatenate(
-                [lax.dynamic_slice_in_dim(w, row, piece, 1) for w in (w_key, w_value)], axis=1
-            ),
+            *[lax.dynamic_slice_in_dim(w, row, piece, 1) for w in (w_key, w_value)],
         ]
     )
     w_side = swap(w_send, "tensor", 1)
@@ -708,35 +702,32 @@
     own_a, own_b, kv_send, kv_keep = attend(
         spot, kv, queries, out_grads, outputs, log_norms, [block]
     )
-    w_side = repeat(spot, w_side, NX, [own_a, up1, down1])
-    w_far = lax.all_to_all(w_side, "dp", 0, 0, axis_index_groups=ring_x, tiled=True)
+    w_side = again(spot, w_side, [up1, down1, own_a])
     far_a = swap(own_a, "tensor", 1)
     kv_z = swap(kv_send, "tensor", 2)
     up2, down2 = shift(up1, "tensor", 2), shift(down1, "tensor", -2)
-    kv_keep, kv_send = middle(spot, kv_keep, kv_z, [up2, down2, far_a], [])
+    w_x = swap(w_side, "dp", 4)
+    kv_keep, kv_send = middle(spot, kv_keep, kv_z, [up2, down2, far_a, w_x], [])
     kv_y = swap(kv_send, "tensor", 1)
     far_b = swap(own_b, "tensor", 1)
     up3, down3 = shift(up2, "tensor", 2), shift(down2, "tensor", -2)
-    w_far = repeat(spot, w_far, 0, [kv_send])
-    w_core = swap(w_far, "dp", 1)
-    weights, weights_kv = gather_weights(
-        spot, w_query, w_key, w_value, w_far, w_core, [kv_send]
-    )
+    w_parts = [w_side, w_x] + [swap(value, "dp", 1) for value in (w_side, w_x)]
+    weights, weights_kv = gather_weights(spot, w_query, w_key, w_value, w_parts, [kv_send])
     base, early = early_parts(spot, weights, [own_a, own_b, far_a], [])
     up4, down4 = halves(spot, up3, down3, [base])
     up4, down4 = shift(up4, "tensor", 2), shift(down4, "tensor", -2)
     here = final_kv(spot, kv_keep, kv_y, early, far_b, [base, up3, down3])
     there = swap(here, "dp", 1)
 
-    up, down = first_parts(spot, weights, weights_kv, base, here, DH)
+    up, down = first_parts(spot, weights, weights_kv, base, here, 2 * DH)
     up_next, down_next = shift(up, "tensor", 2), shift(down, "tensor", -2)
-    parts = rest_parts(spot, weights, weights_kv, base, here, DH, [up])
+    parts = rest_parts(spot, weights, weights_kv, base, here, 2 * DH, [up])
     blocks = [block, up1, down1, up2, down2, up3, down3]
-    terms = wgrad_parts(
+    terms, done = wgrad_parts(
         spot, blocks, up4, down4, here, there, [parts, up_next, down_next]
     )
     for kind, slots in (("first", (0, 1)), ("next", (2, 3)), ("next", (4, 5))):
-        up, down = ring_step(kind, spot, up_next, down_next, parts, slots, [terms])
+        up, down = ring_step(kind, spot, up_next, down_next, parts, slots, [done])
         up_next, down_next = shift(up, "tensor", 2), shift(down, "tensor", -2)
 
     terms = terms.reshape(8, DH, terms.shape[2])

time: 156 us -> 146 us (0.936)
  local copies, waits for them, and re-layouts: 16.5 us -> 7.28 us
  waiting for transfers between devices: 43 us -> 49.2 us
  starting transfers between devices: 52.1 us -> 47.2 us
  Pallas kernels: 39.2 us -> 37.6 us
    unnamed x48 -> x30, local copies, waits for them, and re-layouts: 14 us -> 5.33 us
    ppermute x16, waiting for transfers between devices: 26.3 us -> 33.7 us  [shift(): return lax.ppermute(value, axis, pairs)]
    all_to_all x1 -> x0, starting transfers between devices: 4.95 us -> none  [body(): lax.all_to_all(w_side, 'dp', 0, 0, axis_index_groups=ring_x, tiled=True)]
    ppermute x9 -> x11, waiting for transfers between devices: 16.4 us -> 14.1 us  [swap(): return lax.ppermute(value, axis, pairs)]
    pallas_call x19 -> x18, Pallas kernels: 39.2 us -> 37.6 us  [call(): pl.pallas_call(whole, grid=grid, in_specs=[SMEM, *specs, *[ANY] * (n_late...]
    ppermute x9 -> x11, starting transfers between devices: 6.45 us -> 6.2 us  [swap(): return lax.ppermute(value, axis, pairs)]
  transfers between devices with their start and end apart: 31 -> 32, of which waited for: 12 -> 17; matrix products, arithmetic and copies ran while one was open for 2% -> 1% of each run, Pallas kernels for 16% -> 17%
where the time goes in v4:
time: 146 us; the launch traced here: 145 us
  waiting for transfers between devices  49.2 us (34%)
  starting transfers between devices  47.2 us (32%)
  Pallas kernels  37.6 us (26%)
  local copies, waits for them, and re-layouts  7.28 us (5%)
  between operations  2.91 us (2%)
    pallas_call x18, Pallas kernels, call(): pl.pallas_call(whole, grid=grid, in_specs=[SMEM, *specs, *[ANY] * (n_late...  37.6 us
    ppermute x16, waiting for transfers between devices, shift(): return lax.ppermute(value, axis, pairs)  33.7 us
    ppermute x16, starting transfers between devices, shift(): return lax.ppermute(value, axis, pairs)  26.7 us
    ppermute x11, waiting for transfers between devices, swap(): return lax.ppermute(value, axis, pairs)  14.1 us
    all_to_all x1, starting transfers between devices, body(): lax.all_to_all(terms, 'dp', 0, 0, axis_index_groups=plane, tiled=True)  7.34 us
    ppermute x11, starting transfers between devices, swap(): return lax.ppermute(value, axis, pairs)  6.2 us
    unnamed x30, local copies, waits for them, and re-layouts  5.33 us
    all_to_all x1, starting transfers between devices, body(): lax.all_to_all(kv, 'tensor', 0, 0, axis_index_groups=heads4, tiled=True)  4.78 us
  transfers between devices with their start and end apart: 32, of which 17 were waited for; matrix products, arithmetic and copies ran while one was open for 1% of the time, Pallas kernels for 17%

profile of v4, /device:TPU:26, one launch (start us, length us, event | category | flops | bytes accessed | tf_op | source)
XLA Modules:
  0.0 145.0 jit_solution(3943393631140248250)
XLA Ops:
  1.4 2.0 %pack.1 = (bf16[4,48,256]{2,1,0:T(8,128)(2,1)}, bf16[4,48,256]{2,1,0:T(8,128)(2,1)}, bf16[4,48,256]{2,1,0:T(8,128)(2,1)}, bf16[4,48,256]{2,1,0:T(8,128)(2,1)}, bf16[4,64,768]{2,1,0:T(8,128)(2,1)}) custom-call(s32[5]{0:T(128)} %stack.23.refs_0_, bf16[48,4096]{1,0:T(8,128)(2,1)} %refs_1_.2, bf16[32,768]{1,0:T(8,128)(2,1)} %bitcast.20, bf16[32,768]{1,0:T(8,128)(2,1)} %bitcast.21), custom_call_target="tpu_custom_call" | custom-call | tf_op jit(solution)/shard_map/pack/pallas_call | solution.py:65
  3.4 0.8 collective-permute-start
  4.1 1.4 collective-permute-start.2
  5.5 4.8 %all-to-all-start = ((bf16[4,64,768]{2,1,0:T(8,128)(2,1)}), bf16[4,64,768]{2,1,0:T(8,128)(2,1)S(1)}, u32[]{:S(2)}, u32[]{:S(2)}) async-start(bf16[4,64,768]{2,1,0:T(8,128)(2,1)} %get-tuple-element.48), calls=%async_computation | async-start | bytes 786432 | tf_op jit(solution)/shard_map/all_to_all | solution.py:688
  11.0 0.9 copy-done.10
  11.9 1.3 token_block.1
  15.2 1.2 constant_dynamic-slice_fusion
  16.5 0.9 pad_maximum_fusion
  17.7 6.0 %collective-permute-start.5 = (bf16[4,2,96,256]{3,2,1,0:T(8,128)(2,1)}, bf16[4,2,96,256]{3,2,1,0:T(8,128)(2,1)S(1)}, u32[]{:S(2)}, u32[]{:S(2)}) collective-permute-start(bf16[4,2,96,256]{3,2,1,0:T(8,128)(2,1)} %get-tuple-element.47.refs_6_.refs_1_), channel_id=1, source_target_pairs={{0,14},{1,15},{2,0},{3,1},{4,2},{5,3},{6,4},{7,5},{8,6},{9,7},{10,... | collective-permute-start | bytes 1179656 | tf_op jit(solution)/shard_map/ppermute | solution.py:26
  23.8 1.1 copy-done.12
  24.9 1.1 copy-done.13
  26.1 6.5 %attend.1 = (bf16[768,256]{1,0:T(8,128)(2,1)S(1)}, bf16[768,256]{1,0:T(8,128)(2,1)S(1)}, bf16[2,64,768]{2,1,0:T(8,128)(2,1)S(1)}, f32[2,64,768]{2,1,0:T(8,128)S(1)}) custom-call(s32[5]{0:T(128)S(1)} %copy-done.9, bf16[4,64,768]{2,1,0:T(8,128)(2,1)S(1)} %all-to-all-done.refs_1_, bf16[768,512]{1,0:T(8,128)(2,1)S(1)} %copy-done.11, ...), custom_call_target="tpu_custom_call" | custom-call | flops 1000000000 | tf_op jit(solution)/shard_map/attend/pallas_call | solution.py:65
  32.6 3.1 %collective-permute-done.4.refs_2_ = bf16[4,2,96,256]{3,2,1,0:T(8,128)(2,1)S(1)} collective-permute-done((bf16[4,2,96,256]{3,2,1,0:T(8,128)(2,1)}, bf16[4,2,96,256]{3,2,1,0:T(8,128)(2,1)S(1)}, u32[]{:S(2)}, u32[]{:S(2)}) %collective-permute-start.4) | collective-permute-done | bytes 393248 | tf_op jit(solution)/shard_map/ppermute | solution.py:26
  36.9 3.8 %collective-permute-start.11 = (bf16[4,2,96,256]{3,2,1,0:T(8,128)(2,1)S(1)}, bf16[4,2,96,256]{3,2,1,0:T(8,128)(2,1)S(1)}, u32[]{:S(2)}, u32[]{:S(2)}) collective-permute-start(bf16[4,2,96,256]{3,2,1,0:T(8,128)(2,1)S(1)} %collective-permute-done.5.refs_3_), channel_id=1, source_target_pairs={{0,14},{1,15},{2,0},{3,1},{4,2},{5,3},{6,4},{7,5},{8,6},{9,7},{10,... | collective-permute-start | bytes 1179656 | tf_op jit(solution)/shard_map/ppermute | solution.py:26
  40.7 0.7 collective-permute-start.12
  41.4 3.3 %collective-permute-done.9.refs_2_ = bf16[2,64,768]{2,1,0:T(8,128)(2,1)S(1)} collective-permute-done((bf16[2,64,768]{2,1,0:T(8,128)(2,1)S(1)}, bf16[2,64,768]{2,1,0:T(8,128)(2,1)S(1)}, u32[]{:S(2)}, u32[]{:S(2)}) %collective-permute-start.9) | collective-permute-done | bytes 196640 | tf_op jit(solution)/shard_map/ppermute | solution.py:31
  44.7 5.4 %collective-permute-done.6.refs_6_.refs_5_ = bf16[576,512]{1,0:T(8,128)(2,1)S(1)} collective-permute-done((bf16[576,512]{1,0:T(8,128)(2,1)S(1)}, bf16[576,512]{1,0:T(8,128)(2,1)S(1)}, u32[]{:S(2)}, u32[]{:S(2)}) %collective-permute-start.6) | collective-permute-done | bytes 589856 | tf_op jit(solution)/shard_map/ppermute | solution.py:31
  50.4 1.1 collective-permute-start.14
  51.6 2.7 %collective-permute-start.16 = (bf16[4,2,96,256]{3,2,1,0:T(8,128)(2,1)S(1)}, bf16[4,2,96,256]{3,2,1,0:T(8,128)(2,1)S(1)}, u32[]{:S(2)}, u32[]{:S(2)}) collective-permute-start(bf16[4,2,96,256]{3,2,1,0:T(8,128)(2,1)S(1)} %collective-permute-done.11.refs_4_.refs_5_), channel_id=1, source_target_pairs={{0,14},{1,15},{2,0},{3,1},{4,2},{5,3},{6,4},{7,5},{8,6},{9,7},{10,... | collective-permute-start | bytes 1179656 | tf_op jit(solution)/shard_map/ppermute | solution.py:26
  54.9 1.2 collective-permute-start.13
  56.1 1.5 %gather_weights.1 = (bf16[2048,1024]{1,0:T(8,128)(2,1)S(1)}, bf16[128,2048]{1,0:T(8,128)(2,1)S(1)}) custom-call(s32[5]{0:T(128)S(1)} %copy-done.9, bf16[4096,512]{1,0:T(8,128)(2,1)S(1)} %copy-done, bf16[32,4096]{1,0:T(8,128)(2,1)S(1)} %bitcast.18, bf16[32,4096]{1,0:T(8,128)(2,1)S(1)} %bitcast.19, bf16[576,512]{1,0:T(8,128)(2,1)S(1)} %again.1.refs_4_, ...), custom_call_target="tpu_custom_call" | custom-call | tf_op jit(solution)/shard_map/gather_weights/pallas_call | solution.py:65
  57.6 4.7 %early_parts.1 = (f32[8,96,2048]{2,1,0:T(8,128)S(1)}, bf16[768,768]{1,0:T(8,128)(2,1)S(1)}) custom-call(s32[5]{0:T(128)S(1)} %copy-done.9, bf16[2048,1024]{1,0:T(8,128)(2,1)S(1)} %get-tuple-element.53.refs_1_, bf16[768,256]{1,0:T(8,128)(2,1)S(1)} %get-tuple-element.49.refs_4_.refs_2_, bf16[768,256]{1,0:T(8,128)(2,1)S(1)} %get-tuple-element.55.refs_3_, ...), custom_call_target="tpu_custom_call" | custom-call | flops 1000000000 | tf_op jit(solution)/shard_map/early_parts/pallas_call | solution.py:65
  62.3 0.7 collective-permute-done.16.refs_7_.refs_2_
  63.1 3.4 %collective-permute-done.15.refs_6_.refs_1_ = bf16[4,2,96,256]{3,2,1,0:T(8,128)(2,1)S(1)} collective-permute-done((bf16[4,2,96,256]{3,2,1,0:T(8,128)(2,1)S(1)}, bf16[4,2,96,256]{3,2,1,0:T(8,128)(2,1)S(1)}, u32[]{:S(2)}, u32[]{:S(2)}) %collective-permute-start.15) | collective-permute-done | bytes 393248 | tf_op jit(solution)/shard_map/ppermute | solution.py:26
  67.3 1.2 first_parts.1
  69.2 3.2 %collective-permute-start.20 = (bf16[2,2,96,256]{3,2,1,0:T(8,128)(2,1)S(1)}, bf16[2,2,96,256]{3,2,1,0:T(8,128)(2,1)S(1)}, u32[]{:S(2)}, u32[]{:S(2)}) collective-permute-start(bf16[2,2,96,256]{3,2,1,0:T(8,128)(2,1)S(1)} %get-tuple-element.62), channel_id=1, source_target_pairs={{0,14},{1,15},{2,0},{3,1},{4,2},{5,3},{6,4},{7,5},{8,6},{9,7},{10,... | collective-permute-start | bytes 589832 | tf_op jit(solution)/shard_map/ppermute | solution.py:26
  72.4 1.4 collective-permute-start.18
  74.4 3.5 %rest_parts.1.refs_12_.refs_3_.refs_4_ = bf16[7,96,2048]{2,1,0:T(8,128)(2,1)S(1)} custom-call(s32[5]{0:T(128)S(1)} %copy-done.9, bf16[2048,1024]{1,0:T(8,128)(2,1)S(1)} %get-tuple-element.53.refs_1_, bf16[128,2048]{1,0:T(8,128)(2,1)S(1)} %get-tuple-element.54.refs_2_, f32[8,96,2048]{2,1,0:T(8,128)S(1)} %get-tuple-element.56.refs_5_.refs_3_, ...), custom_call_target="tpu_custom_call" | custom-call | flops 1000000000 | tf_op jit(solution)/shard_map/rest_parts/pallas_call | solution.py:65
  78.0 3.1 %collective-permute-done.18.refs_14_.refs_2_ = bf16[96,1024]{1,0:T(8,128)(2,1)S(1)} collective-permute-done((bf16[96,1024]{1,0:T(8,128)(2,1)S(1)}, bf16[96,1024]{1,0:T(8,128)(2,1)S(1)}, u32[]{:S(2)}, u32[]{:S(2)}) %collective-permute-start.18) | collective-permute-done | bytes 196640 | tf_op jit(solution)/shard_map/ppermute | solution.py:26
  81.1 0.7 collective-permute-done.17.refs_13_.refs_1_
  81.9 7.4 %wgrad_parts.1 = (bf16[4,256,1152]{2,1,0:T(8,128)(2,1)S(1)}, f32[8,128]{1,0:T(8,128)S(1)}) custom-call(s32[5]{0:T(128)S(1)} %copy-done.9, bf16[4,2,96,256]{3,2,1,0:T(8,128)(2,1)} %get-tuple-element.47.refs_6_.refs_1_, bf16[4,2,96,256]{3,2,1,0:T(8,128)(2,1)S(1)} %collective-permute-done.4.refs_2_, bf16[4,2,96,256]{3,2,1,0:T(8,128)(2,1)S(1)} %collective-permute-done.5.refs_3_, ...), custom_call_target="tpu_custom_call" | custom-call | flops 10000000000 | tf_op jit(solution)/shard_map/wgrad_parts/pallas_call | solution.py:65
  89.3 1.5 %copy-done.1 = bf16[4,256,1152]{2,1,0:T(8,128)(2,1)} copy-done((bf16[4,256,1152]{2,1,0:T(8,128)(2,1)}, bf16[4,256,1152]{2,1,0:T(8,128)(2,1)S(1)}, u32[]{:S(2)}) %copy-start.1) | copy-done | bytes 2359320
  90.8 7.3 %all-to-all-start.1 = ((bf16[8,128,1152]{2,1,0:T(8,128)(2,1)}), bf16[8,128,1152]{2,1,0:T(8,128)(2,1)}, u32[]{:S(2)}, u32[]{:S(2)}) async-start(bf16[8,128,1152]{2,1,0:T(8,128)(2,1)} %bitcast.17), calls=%async_computation.1 | async-start | bytes 4718592 | tf_op jit(solution)/shard_map/all_to_all | solution.py:734
  98.9 3.2 %collective-permute-start.23 = (bf16[96,2048]{1,0:T(8,128)(2,1)S(1)}, bf16[96,2048]{1,0:T(8,128)(2,1)S(1)}, u32[]{:S(2)}, u32[]{:S(2)}) collective-permute-start(bf16[96,2048]{1,0:T(8,128)(2,1)S(1)} %get-tuple-element.65), channel_id=1, source_target_pairs={{0,14},{1,15},{2,0},{3,1},{4,2},{5,3},{6,4},{7,5},{8,6},{9,7},{10,... | collective-permute-start | bytes 1179656 | tf_op jit(solution)/shard_map/ppermute | solution.py:26
  102.1 7.9 %collective-permute-done.22.refs_1_ = bf16[96,2048]{1,0:T(8,128)(2,1)S(1)} collective-permute-done((bf16[96,2048]{1,0:T(8,128)(2,1)S(1)}, bf16[96,2048]{1,0:T(8,128)(2,1)S(1)}, u32[]{:S(2)}, u32[]{:S(2)}) %collective-permute-start.22) | collective-permute-done | bytes 393248 | tf_op jit(solution)/shard_map/ppermute | solution.py:26
  110.0 0.7 ring_step.5
  110.7 2.7 %collective-permute-start.24 = (bf16[96,2048]{1,0:T(8,128)(2,1)S(1)}, bf16[96,2048]{1,0:T(8,128)(2,1)S(1)}, u32[]{:S(2)}, u32[]{:S(2)}) collective-permute-start(bf16[96,2048]{1,0:T(8,128)(2,1)S(1)} %get-tuple-element.66), channel_id=1, source_target_pairs={{0,2},{1,3},{2,4},{3,5},{4,6},{5,7},{6,8},{7,9},{8,10},{9,11},{10,... | collective-permute-start | bytes 1179656 | tf_op jit(solution)/shard_map/ppermute | solution.py:26
  114.0 7.3 %collective-permute-done.24.refs_1_ = bf16[96,2048]{1,0:T(8,128)(2,1)S(1)} collective-permute-done((bf16[96,2048]{1,0:T(8,128)(2,1)S(1)}, bf16[96,2048]{1,0:T(8,128)(2,1)S(1)}, u32[]{:S(2)}, u32[]{:S(2)}) %collective-permute-start.24) | collective-permute-done | bytes 393248 | tf_op jit(solution)/shard_map/ppermute | solution.py:26
  121.4 0.8 collective-permute-done.25.refs_2_
  122.2 1.5 %ring_step.6 = (bf16[96,2048]{1,0:T(8,128)(2,1)}, bf16[96,2048]{1,0:T(8,128)(2,1)}) custom-call(s32[5]{0:T(128)S(1)} %copy-done.9, bf16[96,2048]{1,0:T(8,128)(2,1)S(1)} %collective-permute-done.24.refs_1_, bf16[96,2048]{1,0:T(8,128)(2,1)S(1)} %collective-permute-done.25.refs_2_, bf16[7,96,2048]{2,1,0:T(8,128)(2,1)S(1)} %rest_parts.1.refs_12_.refs_3_.refs_4_, ...), custom_call_target="tpu_custom_call" | custom-call | tf_op jit(solution)/shard_map/ring_step/pallas_call | solution.py:65
  123.7 2.1 %collective-permute-start.27 = (bf16[96,2048]{1,0:T(8,128)(2,1)}, bf16[96,2048]{1,0:T(8,128)(2,1)S(1)}, u32[]{:S(2)}, u32[]{:S(2)}) collective-permute-start(bf16[96,2048]{1,0:T(8,128)(2,1)} %get-tuple-element.69), channel_id=1, source_target_pairs={{0,14},{1,15},{2,0},{3,1},{4,2},{5,3},{6,4},{7,5},{8,6},{9,7},{10,... | collective-permute-start | bytes 1179656 | tf_op jit(solution)/shard_map/ppermute | solution.py:26
  125.9 1.4 all-to-all-done.1.refs_1_
  127.2 2.0 %wgrad_sum.1 = (f32[128,512]{1,0:T(8,128)S(1)}, f32[128,128]{1,0:T(8,128)S(1)}, bf16[128,640]{1,0:T(8,128)(2,1)S(1)}) custom-call(s32[5]{0:T(128)S(1)} %copy-done.9, bf16[8,128,1152]{2,1,0:T(8,128)(2,1)} %all-to-all-done.1.refs_1_, bf16[96,2048]{1,0:T(8,128)(2,1)} %get-tuple-element.68.refs_2_), custom_call_target="tpu_custom_call" | custom-call | tf_op jit(solution)/shard_map/wgrad_sum/pallas_call | solution.py:65
  129.2 2.8 %collective-permute-done.27.refs_2_ = bf16[96,2048]{1,0:T(8,128)(2,1)S(1)} collective-permute-done((bf16[96,2048]{1,0:T(8,128)(2,1)}, bf16[96,2048]{1,0:T(8,128)(2,1)S(1)}, u32[]{:S(2)}, u32[]{:S(2)}) %collective-permute-start.27) | collective-permute-done | bytes 393248 | tf_op jit(solution)/shard_map/ppermute | solution.py:26
  131.9 3.3 %collective-permute-done.26.refs_1_ = bf16[96,2048]{1,0:T(8,128)(2,1)S(1)} collective-permute-done((bf16[96,2048]{1,0:T(8,128)(2,1)}, bf16[96,2048]{1,0:T(8,128)(2,1)S(1)}, u32[]{:S(2)}, u32[]{:S(2)}) %collective-permute-start.26) | collective-permute-done | bytes 393248 | tf_op jit(solution)/shard_map/ppermute | solution.py:26
  136.6 1.4 collective-permute-start.29
  138.1 5.4 %collective-permute-done.29.refs_5_ = bf16[128,640]{1,0:T(8,128)(2,1)S(1)} collective-permute-done((bf16[128,640]{1,0:T(8,128)(2,1)S(1)}, bf16[128,640]{1,0:T(8,128)(2,1)S(1)}, u32[]{:S(2)}, u32[]{:S(2)}) %collective-permute-start.29) | collective-permute-done | bytes 163872 | tf_op jit(solution)/shard_map/ppermute | solution.py:31
  143.5 1.5 %final.1 = (bf16[48,4096]{1,0:T(8,128)(2,1)}, f32[256,512]{1,0:T(8,128)}, f32[32,256]{1,0:T(8,128)}, f32[32,256]{1,0:T(8,128)}) custom-call(s32[5]{0:T(128)S(1)} %copy-done.9, bf16[48,2048]{1,0:T(8,128)(2,1)S(1)} %get-tuple-element.72.refs_1_, bf16[48,2048]{1,0:T(8,128)(2,1)S(1)} %collective-permute-done.28.refs_2_, ...), custom_call_target="tpu_custom_call" | custom-call | tf_op jit(solution)/shard_map/final/pallas_call | solution.py:65
  (68 shorter events, 9.0 us)
Async XLA Ops:
  3.4 13.0 %copy-start.2 = (bf16[4096,32]{0,1:T(8,128)(2,1)S(1)}, bf16[4096,32]{0,1:T(8,128)(2,1)}, u32[]{:S(2)}) copy-start(bf16[4096,32]{0,1:T(8,128)(2,1)} %param.18) | copy-start | bytes 786436
  3.4 13.0 %copy-start.3 = (bf16[4096,32]{0,1:T(8,128)(2,1)S(1)}, bf16[4096,32]{0,1:T(8,128)(2,1)}, u32[]{:S(2)}) copy-start(bf16[4096,32]{0,1:T(8,128)(2,1)} %param.19) | copy-start | bytes 786436
  3.4 6.9 %collective-permute-start = (bf16[4,48,256]{2,1,0:T(8,128)(2,1)}, bf16[4,48,256]{2,1,0:T(8,128)(2,1)S(1)}, u32[]{:S(2)}, u32[]{:S(2)}) collective-permute-start(bf16[4,48,256]{2,1,0:T(8,128)(2,1)} %get-tuple-element.43), channel_id=1, source_target_pairs={{0,1},{1,0},{2,3},{3,2},{4,5},{5,4},{6,7},{7,6},{8,9},{9,8},{10,11... | collective-permute-start | bytes 294920 | tf_op jit(solution)/shard_map/ppermute | solution.py:39
  4.1 6.2 %collective-permute-start.1 = (bf16[4,48,256]{2,1,0:T(8,128)(2,1)}, bf16[4,48,256]{2,1,0:T(8,128)(2,1)S(1)}, u32[]{:S(2)}, u32[]{:S(2)}) collective-permute-start(bf16[4,48,256]{2,1,0:T(8,128)(2,1)} %get-tuple-element.44), channel_id=1, source_target_pairs={{0,16},{1,17},{2,18},{3,19},{4,20},{5,21},{6,22},{7,23},{8,24},{9,... | collective-permute-start | bytes 294920 | tf_op jit(solution)/shard_map/ppermute | solution.py:39
  4.1 6.2 %collective-permute-start.2 = (bf16[4,48,256]{2,1,0:T(8,128)(2,1)}, bf16[4,48,256]{2,1,0:T(8,128)(2,1)S(1)}, u32[]{:S(2)}, u32[]{:S(2)}) collective-permute-start(bf16[4,48,256]{2,1,0:T(8,128)(2,1)} %get-tuple-element.45), channel_id=1, source_target_pairs={{0,17},{1,16},{2,19},{3,18},{4,21},{5,20},{6,23},{7,22},{8,25},{9,... | collective-permute-start | bytes 294920 | tf_op jit(solution)/shard_map/ppermute | solution.py:39
  5.5 18.2 %copy-start.9 = (s32[5]{0:T(128)S(1)}, s32[5]{0:T(128)}, u32[]{:S(2)}) copy-start(s32[5]{0:T(128)} %stack.23.refs_0_) | copy-start | bytes 64
  5.5 18.2 %copy-start.14 = (f32[4,768]{1,0:T(4,128)S(1)}, f32[4,768]{1,0:T(4,128)}, u32[]{:S(2)}) copy-start(f32[4,768]{1,0:T(4,128)} %refs_5_.1) | copy-start | bytes 36868
  5.5 18.2 %all-to-all-start = ((bf16[4,64,768]{2,1,0:T(8,128)(2,1)}), bf16[4,64,768]{2,1,0:T(8,128)(2,1)S(1)}, u32[]{:S(2)}, u32[]{:S(2)}) async-start(bf16[4,64,768]{2,1,0:T(8,128)(2,1)} %get-tuple-element.48), calls=%async_computation | async-start | bytes 786432 | tf_op jit(solution)/shard_map/all_to_all | solution.py:688
  10.3 0.7 copy-start.8
  11.0 0.9 copy-start.10
  11.9 11.9 %copy-start.11 = (bf16[768,512]{1,0:T(8,128)(2,1)S(1)}, bf16[768,512]{1,0:T(8,128)(2,1)}, u32[]{:S(2)}) copy-start(bf16[768,512]{1,0:T(8,128)(2,1)} %refs_2_.1) | copy-start | bytes 2359300
  17.4 18.3 %collective-permute-start.3 = (bf16[576,512]{1,0:T(8,128)(2,1)}, bf16[576,512]{1,0:T(8,128)(2,1)S(1)}, u32[]{:S(2)}, u32[]{:S(2)}) collective-permute-start(bf16[576,512]{1,0:T(8,128)(2,1)} %pad_maximum_fusion), channel_id=1, source_target_pairs={{0,1},{1,0},{2,3},{3,2},{4,5},{5,4},{6,7},{7,6},{8,9},{9,8},{10,11... | collective-permute-start | bytes 1769480 | tf_op jit(solution)/shard_map/ppermute | solution.py:31
  17.7 14.8 %collective-permute-start.5 = (bf16[4,2,96,256]{3,2,1,0:T(8,128)(2,1)}, bf16[4,2,96,256]{3,2,1,0:T(8,128)(2,1)S(1)}, u32[]{:S(2)}, u32[]{:S(2)}) collective-permute-start(bf16[4,2,96,256]{3,2,1,0:T(8,128)(2,1)} %get-tuple-element.47.refs_6_.refs_1_), channel_id=1, source_target_pairs={{0,14},{1,15},{2,0},{3,1},{4,2},{5,3},{6,4},{7,5},{8,6},{9,7},{10,... | collective-permute-start | bytes 1179656 | tf_op jit(solution)/shard_map/ppermute | solution.py:26
  23.8 11.9 %collective-permute-start.4 = (bf16[4,2,96,256]{3,2,1,0:T(8,128)(2,1)}, bf16[4,2,96,256]{3,2,1,0:T(8,128)(2,1)S(1)}, u32[]{:S(2)}, u32[]{:S(2)}) collective-permute-start(bf16[4,2,96,256]{3,2,1,0:T(8,128)(2,1)} %get-tuple-element.47.refs_6_.refs_1_), channel_id=1, source_target_pairs={{0,2},{1,3},{2,4},{3,5},{4,6},{5,7},{6,8},{7,9},{8,10},{9,11},{10,... | collective-permute-start | bytes 1179656 | tf_op jit(solution)/shard_map/ppermute | solution.py:26
  23.8 1.1 copy-start.12
  24.9 1.1 copy-start.13
  35.7 20.4 %copy-start = (bf16[4096,512]{1,0:T(8,128)(2,1)S(1)}, bf16[4096,512]{1,0:T(8,128)(2,1)}, u32[]{:S(2)}) copy-start(bf16[4096,512]{1,0:T(8,128)(2,1)} %refs_1_.3) | copy-start | bytes 12582916
  36.2 13.9 %collective-permute-start.6 = (bf16[576,512]{1,0:T(8,128)(2,1)S(1)}, bf16[576,512]{1,0:T(8,128)(2,1)S(1)}, u32[]{:S(2)}, u32[]{:S(2)}) collective-permute-start(bf16[576,512]{1,0:T(8,128)(2,1)S(1)} %again.1.refs_4_), channel_id=1, source_target_pairs={{0,64},{16,80},{32,96},{48,112},{64,0},{80,16},{96,32},{112,48},{1... | collective-permute-start | bytes 1769480 | tf_op jit(solution)/shard_map/ppermute | solution.py:31
  36.9 7.8 %collective-permute-start.9 = (bf16[2,64,768]{2,1,0:T(8,128)(2,1)S(1)}, bf16[2,64,768]{2,1,0:T(8,128)(2,1)S(1)}, u32[]{:S(2)}, u32[]{:S(2)}) collective-permute-start(bf16[2,64,768]{2,1,0:T(8,128)(2,1)S(1)} %get-tuple-element.51), channel_id=1, source_target_pairs={{0,2},{1,3},{2,0},{3,1},{4,6},{5,7},{6,4},{7,5},{8,10},{9,11},{10,... | collective-permute-start | bytes 589832 | tf_op jit(solution)/shard_map/ppermute | solution.py:31
  36.9 13.5 %collective-permute-start.11 = (bf16[4,2,96,256]{3,2,1,0:T(8,128)(2,1)S(1)}, bf16[4,2,96,256]{3,2,1,0:T(8,128)(2,1)S(1)}, u32[]{:S(2)}, u32[]{:S(2)}) collective-permute-start(bf16[4,2,96,256]{3,2,1,0:T(8,128)(2,1)S(1)} %collective-permute-done.5.refs_3_), channel_id=1, source_target_pairs={{0,14},{1,15},{2,0},{3,1},{4,2},{5,3},{6,4},{7,5},{8,6},{9,7},{10,... | collective-permute-start | bytes 1179656 | tf_op jit(solution)/shard_map/ppermute | solution.py:26
  40.7 10.9 %collective-permute-start.10 = (bf16[4,2,96,256]{3,2,1,0:T(8,128)(2,1)S(1)}, bf16[4,2,96,256]{3,2,1,0:T(8,128)(2,1)S(1)}, u32[]{:S(2)}, u32[]{:S(2)}) collective-permute-start(bf16[4,2,96,256]{3,2,1,0:T(8,128)(2,1)S(1)} %collective-permute-done.4.refs_2_), channel_id=1, source_target_pairs={{0,2},{1,3},{2,4},{3,5},{4,6},{5,7},{6,8},{7,9},{8,10},{9,11},{10,... | collective-permute-start | bytes 1179656 | tf_op jit(solution)/shard_map/ppermute | solution.py:26
  40.7 13.6 %collective-permute-start.12 = (bf16[768,256]{1,0:T(8,128)(2,1)S(1)}, bf16[768,256]{1,0:T(8,128)(2,1)S(1)}, u32[]{:S(2)}, u32[]{:S(2)}) collective-permute-start(bf16[768,256]{1,0:T(8,128)(2,1)S(1)} %get-tuple-element.49.refs_4_.refs_2_), channel_id=1, source_target_pairs={{0,1},{1,0},{2,3},{3,2},{4,5},{5,4},{6,7},{7,6},{8,9},{9,8},{10,11... | collective-permute-start | bytes 1179656 | tf_op jit(solution)/shard_map/ppermute | solution.py:31
  44.7 10.2 %collective-permute-start.7 = (bf16[576,512]{1,0:T(8,128)(2,1)S(1)}, bf16[576,512]{1,0:T(8,128)(2,1)S(1)}, u32[]{:S(2)}, u32[]{:S(2)}) collective-permute-start(bf16[576,512]{1,0:T(8,128)(2,1)S(1)} %again.1.refs_4_), channel_id=1, source_target_pairs={{0,16},{16,0},{32,48},{48,32},{64,80},{80,64},{96,112},{112,96},{1... | collective-permute-start | bytes 1769480 | tf_op jit(solution)/shard_map/ppermute | solution.py:31
  50.1 6.0 %collective-permute-start.8 = (bf16[576,512]{1,0:T(8,128)(2,1)S(1)}, bf16[576,512]{1,0:T(8,128)(2,1)S(1)}, u32[]{:S(2)}, u32[]{:S(2)}) collective-permute-start(bf16[576,512]{1,0:T(8,128)(2,1)S(1)} %collective-permute-done.6.refs_6_.refs_5_), channel_id=1, source_target_pairs={{0,16},{16,0},{32,48},{48,32},{64,80},{80,64},{96,112},{112,96},{1... | collective-permute-start | bytes 1769480 | tf_op jit(solution)/shard_map/ppermute | solution.py:31
  50.4 12.0 %collective-permute-start.14 = (bf16[768,256]{1,0:T(8,128)(2,1)S(1)}, bf16[768,256]{1,0:T(8,128)(2,1)S(1)}, u32[]{:S(2)}, u32[]{:S(2)}) collective-permute-start(bf16[768,256]{1,0:T(8,128)(2,1)S(1)} %get-tuple-element.55.refs_3_), channel_id=1, source_target_pairs={{0,1},{1,0},{2,3},{3,2},{4,5},{5,4},{6,7},{7,6},{8,9},{9,8},{10,11... | collective-permute-start | bytes 1179656 | tf_op jit(solution)/shard_map/ppermute | solution.py:31
  51.6 11.5 %collective-permute-start.16 = (bf16[4,2,96,256]{3,2,1,0:T(8,128)(2,1)S(1)}, bf16[4,2,96,256]{3,2,1,0:T(8,128)(2,1)S(1)}, u32[]{:S(2)}, u32[]{:S(2)}) collective-permute-start(bf16[4,2,96,256]{3,2,1,0:T(8,128)(2,1)S(1)} %collective-permute-done.11.refs_4_.refs_5_), channel_id=1, source_target_pairs={{0,14},{1,15},{2,0},{3,1},{4,2},{5,3},{6,4},{7,5},{8,6},{9,7},{10,... | collective-permute-start | bytes 1179656 | tf_op jit(solution)/shard_map/ppermute | solution.py:26
  54.3 12.2 %collective-permute-start.15 = (bf16[4,2,96,256]{3,2,1,0:T(8,128)(2,1)S(1)}, bf16[4,2,96,256]{3,2,1,0:T(8,128)(2,1)S(1)}, u32[]{:S(2)}, u32[]{:S(2)}) collective-permute-start(bf16[4,2,96,256]{3,2,1,0:T(8,128)(2,1)S(1)} %collective-permute-done.10.refs_3_.refs_4_), channel_id=1, source_target_pairs={{0,2},{1,3},{2,4},{3,5},{4,6},{5,7},{6,8},{7,9},{8,10},{9,11},{10,... | collective-permute-start | bytes 1179656 | tf_op jit(solution)/shard_map/ppermute | solution.py:26
  54.9 11.6 %collective-permute-start.13 = (bf16[2,64,768]{2,1,0:T(8,128)(2,1)S(1)}, bf16[2,64,768]{2,1,0:T(8,128)(2,1)S(1)}, u32[]{:S(2)}, u32[]{:S(2)}) collective-permute-start(bf16[2,64,768]{2,1,0:T(8,128)(2,1)S(1)} %get-tuple-element.52.refs_8_), channel_id=1, source_target_pairs={{0,1},{1,0},{2,3},{3,2},{4,5},{5,4},{6,7},{7,6},{8,9},{9,8},{10,11... | collective-permute-start | bytes 589832 | tf_op jit(solution)/shard_map/ppermute | solution.py:31
  67.2 14.6 %collective-permute-start.21 = (bf16[768,1152]{1,0:T(8,128)(2,1)S(1)}, bf16[768,1152]{1,0:T(8,128)(2,1)S(1)}, u32[]{:S(2)}, u32[]{:S(2)}) collective-permute-start(bf16[768,1152]{1,0:T(8,128)(2,1)S(1)} %kv_final.1.refs_4_.refs_10_), channel_id=1, source_target_pairs={{0,16},{16,0},{32,48},{48,32},{64,80},{80,64},{96,112},{112,96},{1... | collective-permute-start | bytes 5308424 | tf_op jit(solution)/shard_map/ppermute | solution.py:31
  69.1 9.0 %collective-permute-start.19 = (bf16[2,2,96,256]{3,2,1,0:T(8,128)(2,1)S(1)}, bf16[2,2,96,256]{3,2,1,0:T(8,128)(2,1)S(1)}, u32[]{:S(2)}, u32[]{:S(2)}) collective-permute-start(bf16[2,2,96,256]{3,2,1,0:T(8,128)(2,1)S(1)} %get-tuple-element.61), channel_id=1, source_target_pairs={{0,2},{1,3},{2,4},{3,5},{4,6},{5,7},{6,8},{7,9},{8,10},{9,11},{10,... | collective-permute-start | bytes 589832 | tf_op jit(solution)/shard_map/ppermute | solution.py:26
  69.2 8.9 %collective-permute-start.20 = (bf16[2,2,96,256]{3,2,1,0:T(8,128)(2,1)S(1)}, bf16[2,2,96,256]{3,2,1,0:T(8,128)(2,1)S(1)}, u32[]{:S(2)}, u32[]{:S(2)}) collective-permute-start(bf16[2,2,96,256]{3,2,1,0:T(8,128)(2,1)S(1)} %get-tuple-element.62), channel_id=1, source_target_pairs={{0,14},{1,15},{2,0},{3,1},{4,2},{5,3},{6,4},{7,5},{8,6},{9,7},{10,... | collective-permute-start | bytes 589832 | tf_op jit(solution)/shard_map/ppermute | solution.py:26
  72.4 8.8 %collective-permute-start.18 = (bf16[96,1024]{1,0:T(8,128)(2,1)S(1)}, bf16[96,1024]{1,0:T(8,128)(2,1)S(1)}, u32[]{:S(2)}, u32[]{:S(2)}) collective-permute-start(bf16[96,1024]{1,0:T(8,128)(2,1)S(1)} %get-tuple-element.60), channel_id=1, source_target_pairs={{0,14},{1,15},{2,0},{3,1},{4,2},{5,3},{6,4},{7,5},{8,6},{9,7},{10,... | collective-permute-start | bytes 589832 | tf_op jit(solution)/shard_map/ppermute | solution.py:26
  73.8 8.1 %collective-permute-start.17 = (bf16[96,1024]{1,0:T(8,128)(2,1)S(1)}, bf16[96,1024]{1,0:T(8,128)(2,1)S(1)}, u32[]{:S(2)}, u32[]{:S(2)}) collective-permute-start(bf16[96,1024]{1,0:T(8,128)(2,1)S(1)} %get-tuple-element.59.refs_5_), channel_id=1, source_target_pairs={{0,2},{1,3},{2,4},{3,5},{4,6},{5,7},{6,8},{7,9},{8,10},{9,11},{10,... | collective-permute-start | bytes 589832 | tf_op jit(solution)/shard_map/ppermute | solution.py:26
  81.1 8.2 %copy-start.4 = (bf16[96,1024]{1,0:T(8,128)(2,1)}, bf16[96,1024]{1,0:T(8,128)(2,1)S(1)}, u32[]{:S(2)}) copy-start(bf16[96,1024]{1,0:T(8,128)(2,1)S(1)} %collective-permute-done.18.refs_14_.refs_2_) | copy-start | bytes 589828
  81.9 7.4 %copy-start.6 = (bf16[96,1024]{1,0:T(8,128)(2,1)}, bf16[96,1024]{1,0:T(8,128)(2,1)S(1)}, u32[]{:S(2)}) copy-start(bf16[96,1024]{1,0:T(8,128)(2,1)S(1)} %collective-permute-done.17.refs_13_.refs_1_) | copy-start | bytes 589828
  89.3 1.5 %copy-start.1 = (bf16[4,256,1152]{2,1,0:T(8,128)(2,1)}, bf16[4,256,1152]{2,1,0:T(8,128)(2,1)S(1)}, u32[]{:S(2)}) copy-start(bf16[4,256,1152]{2,1,0:T(8,128)(2,1)S(1)} %get-tuple-element.70) | copy-start | bytes 7077892
  90.8 7.3 %copy-start.5 = (bf16[96,1024]{1,0:T(8,128)(2,1)S(1)}, bf16[96,1024]{1,0:T(8,128)(2,1)}, u32[]{:S(2)}) copy-start(bf16[96,1024]{1,0:T(8,128)(2,1)} %copy-done.4) | copy-start | bytes 589828
  90.8 7.3 %copy-start.7 = (bf16[96,1024]{1,0:T(8,128)(2,1)S(1)}, bf16[96,1024]{1,0:T(8,128)(2,1)}, u32[]{:S(2)}) copy-start(bf16[96,1024]{1,0:T(8,128)(2,1)} %copy-done.6) | copy-start | bytes 589828
  90.8 36.4 %all-to-all-start.1 = ((bf16[8,128,1152]{2,1,0:T(8,128)(2,1)}), bf16[8,128,1152]{2,1,0:T(8,128)(2,1)}, u32[]{:S(2)}, u32[]{:S(2)}) async-start(bf16[8,128,1152]{2,1,0:T(8,128)(2,1)} %bitcast.17), calls=%async_computation.1 | async-start | bytes 4718592 | tf_op jit(solution)/shard_map/all_to_all | solution.py:734
  98.8 11.2 %collective-permute-start.22 = (bf16[96,2048]{1,0:T(8,128)(2,1)S(1)}, bf16[96,2048]{1,0:T(8,128)(2,1)S(1)}, u32[]{:S(2)}, u32[]{:S(2)}) collective-permute-start(bf16[96,2048]{1,0:T(8,128)(2,1)S(1)} %get-tuple-element.64), channel_id=1, source_target_pairs={{0,2},{1,3},{2,4},{3,5},{4,6},{5,7},{6,8},{7,9},{8,10},{9,11},{10,... | collective-permute-start | bytes 1179656 | tf_op jit(solution)/shard_map/ppermute | solution.py:26
  98.9 11.1 %collective-permute-start.23 = (bf16[96,2048]{1,0:T(8,128)(2,1)S(1)}, bf16[96,2048]{1,0:T(8,128)(2,1)S(1)}, u32[]{:S(2)}, u32[]{:S(2)}) collective-permute-start(bf16[96,2048]{1,0:T(8,128)(2,1)S(1)} %get-tuple-element.65), channel_id=1, source_target_pairs={{0,14},{1,15},{2,0},{3,1},{4,2},{5,3},{6,4},{7,5},{8,6},{9,7},{10,... | collective-permute-start | bytes 1179656 | tf_op jit(solution)/shard_map/ppermute | solution.py:26
  110.7 10.6 %collective-permute-start.24 = (bf16[96,2048]{1,0:T(8,128)(2,1)S(1)}, bf16[96,2048]{1,0:T(8,128)(2,1)S(1)}, u32[]{:S(2)}, u32[]{:S(2)}) collective-permute-start(bf16[96,2048]{1,0:T(8,128)(2,1)S(1)} %get-tuple-element.66), channel_id=1, source_target_pairs={{0,2},{1,3},{2,4},{3,5},{4,6},{5,7},{6,8},{7,9},{8,10},{9,11},{10,... | collective-permute-start | bytes 1179656 | tf_op jit(solution)/shard_map/ppermute | solution.py:26
  113.4 8.8 %collective-permute-start.25 = (bf16[96,2048]{1,0:T(8,128)(2,1)S(1)}, bf16[96,2048]{1,0:T(8,128)(2,1)S(1)}, u32[]{:S(2)}, u32[]{:S(2)}) collective-permute-start(bf16[96,2048]{1,0:T(8,128)(2,1)S(1)} %get-tuple-element.67), channel_id=1, source_target_pairs={{0,14},{1,15},{2,0},{3,1},{4,2},{5,3},{6,4},{7,5},{8,6},{9,7},{10,... | collective-permute-start | bytes 1179656 | tf_op jit(solution)/shard_map/ppermute | solution.py:26
  123.7 8.2 %collective-permute-start.27 = (bf16[96,2048]{1,0:T(8,128)(2,1)}, bf16[96,2048]{1,0:T(8,128)(2,1)S(1)}, u32[]{:S(2)}, u32[]{:S(2)}) collective-permute-start(bf16[96,2048]{1,0:T(8,128)(2,1)} %get-tuple-element.69), channel_id=1, source_target_pairs={{0,14},{1,15},{2,0},{3,1},{4,2},{5,3},{6,4},{7,5},{8,6},{9,7},{10,... | collective-permute-start | bytes 1179656 | tf_op jit(solution)/shard_map/ppermute | solution.py:26
  125.9 9.4 %collective-permute-start.26 = (bf16[96,2048]{1,0:T(8,128)(2,1)}, bf16[96,2048]{1,0:T(8,128)(2,1)S(1)}, u32[]{:S(2)}, u32[]{:S(2)}) collective-permute-start(bf16[96,2048]{1,0:T(8,128)(2,1)} %get-tuple-element.68.refs_2_), channel_id=1, source_target_pairs={{0,2},{1,3},{2,4},{3,5},{4,6},{5,7},{6,8},{7,9},{8,10},{9,11},{10,... | collective-permute-start | bytes 1179656 | tf_op jit(solution)/shard_map/ppermute | solution.py:26
  135.9 7.5 %collective-permute-start.28 = (bf16[48,2048]{1,0:T(8,128)(2,1)S(1)}, bf16[48,2048]{1,0:T(8,128)(2,1)S(1)}, u32[]{:S(2)}, u32[]{:S(2)}) collective-permute-start(bf16[48,2048]{1,0:T(8,128)(2,1)S(1)} %get-tuple-element.73), channel_id=1, source_target_pairs={{0,1},{1,0},{2,3},{3,2},{4,5},{5,4},{6,7},{7,6},{8,9},{9,8},{10,11... | collective-permute-start | bytes 589832 | tf_op jit(solution)/shard_map/ppermute | solution.py:31
  136.6 6.8 %collective-permute-start.29 = (bf16[128,640]{1,0:T(8,128)(2,1)S(1)}, bf16[128,640]{1,0:T(8,128)(2,1)S(1)}, u32[]{:S(2)}, u32[]{:S(2)}) collective-permute-start(bf16[128,640]{1,0:T(8,128)(2,1)S(1)} %get-tuple-element.71.refs_5_), channel_id=1, source_target_pairs={{0,1},{1,0},{2,3},{3,2},{4,5},{5,4},{6,7},{7,6},{8,9},{9,8},{10,11... | collective-permute-start | bytes 491528 | tf_op jit(solution)/shard_map/ppermute | solution.py:31

commit v5 on v4

--- a/solution.py
+++ b/solution.py
@@ -112,29 +112,48 @@
     )
 
 
-def block_kernel(quarter, spot, own, side, core, both, out, start):
-    start[0] = ((1 - spot[H]) * 2 + spot[C]) * quarter + lax.rem(spot[X], 2) * (quarter // 2)
+def block_kernel(spot, own, side, core, both, w_query, w_key, w_value, out, w_send, sems):
     h = spot[H]
     rows = own.shape[1]
+    kv_w = w_key.shape[0]
+    piece = w_send.shape[0] - 2 * kv_w
+    row = ((1 - h) * 2 + spot[C]) * (2 * piece) + lax.rem(spot[X], 2) * piece
+    part = pl.ds(pl.multiple_of(row, piece), piece)
+    copies = [
+        pltpu.make_async_copy(source, w_send.at[pl.ds(start, size), :], sems.at[index])
+        for index, (source, start, size) in enumerate(
+            (
+                (w_query.at[part, :], 0, piece),
+                (w_key.at[:, part], piece, kv_w),
+                (w_value.at[:, part], piece + kv_w, kv_w),
+            )
+        )
+    ]
+    for copy in copies:
+        copy.start()
     near = pl.ds(pl.multiple_of(h * rows, rows), rows)
     far = pl.ds(pl.multiple_of((1 - h) * rows, rows), rows)
     out[:, 0, near, :] = own[...]
     out[:, 0, far, :] = side[...]
     out[:, 1, near, :] = core[...]
     out[:, 1, far, :] = both[...]
-
-
-def token_block(spot, parts, quarter, later):
+    for copy in copies:
+        copy.wait()
+
+
+def token_block(spot, parts, w_query, w_key, w_value):
     part, rows, wide = parts[0].shape
-    return call(
-        functools.partial(block_kernel, quarter),
+    w_rows = w_query.shape[0] // 8 + 2 * w_key.shape[0]
+    return call(
+        block_kernel,
         "token_block",
         spot,
-        parts,
-        [VMEM] * 4,
-        [shape((part, 2, 2 * rows, wide)), shape((1,), jnp.int32)],
-        [VMEM, SMEM],
-        later=later,
+        (*parts, w_query, w_key, w_value),
+        [VMEM] * 4 + [ANY] * 3,
+        [shape((part, 2, 2 * rows, wide)), shape((w_rows, w_query.shape[1]))],
+        [VMEM, VMEM],
+        [pltpu.SemaphoreType.DMA((3,))],
+        vmem=64,
     )
 
 
@@ -686,19 +705,9 @@
     core = swap_quad(core, 1, 0)
     both = swap_quad(both, 1, 1)
     kv = lax.all_to_all(kv, "tensor", 0, 0, axis_index_groups=heads4, tiled=True)
-    quarter = tokens.shape[1] // 4
-    block, start = token_block(spot, (own, side, core, both), quarter, [])
+    block, w_send = token_block(spot, (own, side, core, both), w_query, w_key, w_value)
+    w_side = swap(w_send, "tensor", 1)
     up1, down1 = shift(block, "tensor", 2), shift(block, "tensor", -2)
-    piece = quarter // 2
-    row = start[0]
-    w_send = jnp.concatenate(
-        [
-            lax.dynamic_slice_in_dim(w_query, row, piece, 0),
-            *[lax.dynamic_slice_in_dim(w, row, piece, 1) for w in (w_key, w_value)],
-        ]
-    )
-    w_side = swap(w_send, "tensor", 1)
-
     own_a, own_b, kv_send, kv_keep = attend(
         spot, kv, queries, out_grads, outputs, log_norms, [block]
     )

time: 146 us -> 144 us (0.986)
  waiting for transfers between devices: 49.2 us -> 46.4 us
  between operations: 2.91 us -> 0.98 us
  Pallas kernels: 37.6 us -> 39.4 us
    ppermute x16, waiting for transfers between devices: 33.7 us -> 28.9 us  [shift(): return lax.ppermute(value, axis, pairs)]
    unnamed x30 -> x32, local copies, waits for them, and re-layouts: 5.33 us -> 7.19 us
    pallas_call x18, Pallas kernels: 37.6 us -> 39.4 us  [call(): pl.pallas_call(whole, grid=grid, in_specs=[SMEM, *specs, *[ANY] * (n_late...]
  transfers between devices with their start and end apart: 32 -> 32, of which waited for: 17 -> 15; matrix products, arithmetic and copies ran while one was open for 1% -> 0% of each run, Pallas kernels for 17% -> 19%
where the time goes in v5:
time: 144 us; the launch traced here: 143 us
  starting transfers between devices  48.5 us (34%)
  waiting for transfers between devices  46.4 us (32%)
  Pallas kernels  39.4 us (27%)
  local copies, waits for them, and re-layouts  7.78 us (5%)
    pallas_call x18, Pallas kernels, call(): pl.pallas_call(whole, grid=grid, in_specs=[SMEM, *specs, *[ANY] * (n_late...  39.4 us
    ppermute x16, waiting for transfers between devices, shift(): return lax.ppermute(value, axis, pairs)  28.9 us
    ppermute x16, starting transfers between devices, shift(): return lax.ppermute(value, axis, pairs)  27.5 us
    ppermute x11, waiting for transfers between devices, swap(): return lax.ppermute(value, axis, pairs)  14.8 us
    all_to_all x1, starting transfers between devices, body(): lax.all_to_all(terms, 'dp', 0, 0, axis_index_groups=plane, tiled=True)  7.36 us
    unnamed x32, local copies, waits for them, and re-layouts  7.19 us
    ppermute x11, starting transfers between devices, swap(): return lax.ppermute(value, axis, pairs)  6.69 us
    all_to_all x1, starting transfers between devices, body(): lax.all_to_all(kv, 'tensor', 0, 0, axis_index_groups=heads4, tiled=True)  4.81 us
  transfers between devices with their start and end apart: 32, of which 15 were waited for; matrix products, arithmetic and copies ran while one was open for 0% of the time, Pallas kernels for 19%

profile of v5, /device:TPU:26, one launch (start us, length us, event | category | flops | bytes accessed | tf_op | source)
XLA Modules:
  0.0 143.0 jit_solution(14162146464257179352)
XLA Ops:
  1.3 2.0 %pack.1 = (bf16[4,48,256]{2,1,0:T(8,128)(2,1)}, bf16[4,48,256]{2,1,0:T(8,128)(2,1)}, bf16[4,48,256]{2,1,0:T(8,128)(2,1)}, bf16[4,48,256]{2,1,0:T(8,128)(2,1)}, bf16[4,64,768]{2,1,0:T(8,128)(2,1)}) custom-call(s32[5]{0:T(128)} %stack.23.refs_0_, bf16[48,4096]{1,0:T(8,128)(2,1)} %refs_1_.2, bf16[32,768]{1,0:T(8,128)(2,1)} %bitcast.17, bf16[32,768]{1,0:T(8,128)(2,1)} %bitcast.18), custom_call_target="tpu_custom_call" | custom-call | tf_op jit(solution)/shard_map/pack/pallas_call | solution.py:65
  3.3 0.7 collective-permute-start
  4.0 1.4 collective-permute-start.2
  5.4 4.8 %all-to-all-start = ((bf16[4,64,768]{2,1,0:T(8,128)(2,1)}), bf16[4,64,768]{2,1,0:T(8,128)(2,1)}, u32[]{:S(2)}, u32[]{:S(2)}) async-start(bf16[4,64,768]{2,1,0:T(8,128)(2,1)} %get-tuple-element.48), calls=%async_computation | async-start | bytes 786432 | tf_op jit(solution)/shard_map/all_to_all | solution.py:707
  10.3 3.1 %token_block.1 = (bf16[4,2,96,256]{3,2,1,0:T(8,128)(2,1)}, bf16[576,512]{1,0:T(8,128)(2,1)}) custom-call(s32[5]{0:T(128)} %stack.23.refs_0_, bf16[4,48,256]{2,1,0:T(8,128)(2,1)} %get-tuple-element.42.refs_1_, bf16[4,48,256]{2,1,0:T(8,128)(2,1)} %collective-permute-done.refs_2_, bf16[4,48,256]{2,1,0:T(8,128)(2,1)} %collective-permute-done.1.refs_3_, ...), custom_call_target="tpu_custom_call" | custom-call | tf_op jit(solution)/shard_map/token_block/pallas_call | solution.py:65
  13.9 6.4 %collective-permute-start.5 = (bf16[4,2,96,256]{3,2,1,0:T(8,128)(2,1)}, bf16[4,2,96,256]{3,2,1,0:T(8,128)(2,1)S(1)}, u32[]{:S(2)}, u32[]{:S(2)}) collective-permute-start(bf16[4,2,96,256]{3,2,1,0:T(8,128)(2,1)} %get-tuple-element.47.refs_6_.refs_1_), channel_id=1, source_target_pairs={{0,14},{1,15},{2,0},{3,1},{4,2},{5,3},{6,4},{7,5},{8,6},{9,7},{10,... | collective-permute-start | bytes 1179656 | tf_op jit(solution)/shard_map/ppermute | solution.py:26
  20.9 1.1 copy-done.10
  22.1 1.1 copy-done.11
  23.2 1.1 copy-done.12
  24.3 1.0 copy-done.13
  25.3 0.7 copy-done.15
  26.0 7.0 %attend.1 = (bf16[768,256]{1,0:T(8,128)(2,1)S(1)}, bf16[768,256]{1,0:T(8,128)(2,1)S(1)}, bf16[2,64,768]{2,1,0:T(8,128)(2,1)S(1)}, f32[2,64,768]{2,1,0:T(8,128)S(1)}) custom-call(s32[5]{0:T(128)S(1)} %copy-done.8, bf16[4,64,768]{2,1,0:T(8,128)(2,1)} %all-to-all-done.refs_1_, bf16[768,512]{1,0:T(8,128)(2,1)S(1)} %copy-done.10, ...), custom_call_target="tpu_custom_call" | custom-call | flops 1000000000 | tf_op jit(solution)/shard_map/attend/pallas_call | solution.py:65
  34.3 3.5 %collective-permute-start.11 = (bf16[4,2,96,256]{3,2,1,0:T(8,128)(2,1)S(1)}, bf16[4,2,96,256]{3,2,1,0:T(8,128)(2,1)S(1)}, u32[]{:S(2)}, u32[]{:S(2)}) collective-permute-start(bf16[4,2,96,256]{3,2,1,0:T(8,128)(2,1)S(1)} %collective-permute-done.5.refs_3_), channel_id=1, source_target_pairs={{0,14},{1,15},{2,0},{3,1},{4,2},{5,3},{6,4},{7,5},{8,6},{9,7},{10,... | collective-permute-start | bytes 1179656 | tf_op jit(solution)/shard_map/ppermute | solution.py:26
  37.8 1.2 collective-permute-start.12
  39.0 3.1 %collective-permute-done.9.refs_2_ = bf16[2,64,768]{2,1,0:T(8,128)(2,1)S(1)} collective-permute-done((bf16[2,64,768]{2,1,0:T(8,128)(2,1)S(1)}, bf16[2,64,768]{2,1,0:T(8,128)(2,1)S(1)}, u32[]{:S(2)}, u32[]{:S(2)}) %collective-permute-start.9) | collective-permute-done | bytes 196640 | tf_op jit(solution)/shard_map/ppermute | solution.py:31
  42.1 6.0 %collective-permute-done.6.refs_6_.refs_5_ = bf16[576,512]{1,0:T(8,128)(2,1)S(1)} collective-permute-done((bf16[576,512]{1,0:T(8,128)(2,1)S(1)}, bf16[576,512]{1,0:T(8,128)(2,1)S(1)}, u32[]{:S(2)}, u32[]{:S(2)}) %collective-permute-start.6) | collective-permute-done | bytes 589856 | tf_op jit(solution)/shard_map/ppermute | solution.py:31
  48.4 1.5 %collective-permute-start.14 = (bf16[768,256]{1,0:T(8,128)(2,1)S(1)}, bf16[768,256]{1,0:T(8,128)(2,1)S(1)}, u32[]{:S(2)}, u32[]{:S(2)}) collective-permute-start(bf16[768,256]{1,0:T(8,128)(2,1)S(1)} %get-tuple-element.55.refs_3_), channel_id=1, source_target_pairs={{0,1},{1,0},{2,3},{3,2},{4,5},{5,4},{6,7},{7,6},{8,9},{9,8},{10,11... | collective-permute-start | bytes 1179656 | tf_op jit(solution)/shard_map/ppermute | solution.py:31
  49.9 2.7 %collective-permute-start.16 = (bf16[4,2,96,256]{3,2,1,0:T(8,128)(2,1)S(1)}, bf16[4,2,96,256]{3,2,1,0:T(8,128)(2,1)S(1)}, u32[]{:S(2)}, u32[]{:S(2)}) collective-permute-start(bf16[4,2,96,256]{3,2,1,0:T(8,128)(2,1)S(1)} %collective-permute-done.11.refs_4_.refs_5_), channel_id=1, source_target_pairs={{0,14},{1,15},{2,0},{3,1},{4,2},{5,3},{6,4},{7,5},{8,6},{9,7},{10,... | collective-permute-start | bytes 1179656 | tf_op jit(solution)/shard_map/ppermute | solution.py:26
  53.9 1.5 %gather_weights.1 = (bf16[2048,1024]{1,0:T(8,128)(2,1)S(1)}, bf16[128,2048]{1,0:T(8,128)(2,1)S(1)}) custom-call(s32[5]{0:T(128)S(1)} %copy-done.9, bf16[4096,512]{1,0:T(8,128)(2,1)S(1)} %copy-done, bf16[32,4096]{1,0:T(8,128)(2,1)S(1)} %bitcast.14, bf16[32,4096]{1,0:T(8,128)(2,1)S(1)} %bitcast.16, bf16[576,512]{1,0:T(8,128)(2,1)S(1)} %again.1.refs_4_, ...), custom_call_target="tpu_custom_call" | custom-call | tf_op jit(solution)/shard_map/gather_weights/pallas_call | solution.py:65
  55.3 4.7 %early_parts.1 = (f32[8,96,2048]{2,1,0:T(8,128)S(1)}, bf16[768,768]{1,0:T(8,128)(2,1)S(1)}) custom-call(s32[5]{0:T(128)S(1)} %copy-done.9, bf16[2048,1024]{1,0:T(8,128)(2,1)S(1)} %get-tuple-element.53.refs_1_, bf16[768,256]{1,0:T(8,128)(2,1)S(1)} %get-tuple-element.49.refs_4_.refs_2_, bf16[768,256]{1,0:T(8,128)(2,1)S(1)} %get-tuple-element.55.refs_3_, ...), custom_call_target="tpu_custom_call" | custom-call | flops 1000000000 | tf_op jit(solution)/shard_map/early_parts/pallas_call | solution.py:65
  60.4 1.0 collective-permute-done.16.refs_7_.refs_2_
  61.4 3.4 %collective-permute-done.15.refs_6_.refs_1_ = bf16[4,2,96,256]{3,2,1,0:T(8,128)(2,1)S(1)} collective-permute-done((bf16[4,2,96,256]{3,2,1,0:T(8,128)(2,1)S(1)}, bf16[4,2,96,256]{3,2,1,0:T(8,128)(2,1)S(1)}, u32[]{:S(2)}, u32[]{:S(2)}) %collective-permute-start.15) | collective-permute-done | bytes 393248 | tf_op jit(solution)/shard_map/ppermute | solution.py:26
  64.8 0.7 kv_final.1.refs_4_.refs_10_
  65.6 1.2 first_parts.1
  67.4 3.2 %collective-permute-start.20 = (bf16[2,2,96,256]{3,2,1,0:T(8,128)(2,1)S(1)}, bf16[2,2,96,256]{3,2,1,0:T(8,128)(2,1)S(1)}, u32[]{:S(2)}, u32[]{:S(2)}) collective-permute-start(bf16[2,2,96,256]{3,2,1,0:T(8,128)(2,1)S(1)} %get-tuple-element.62), channel_id=1, source_target_pairs={{0,14},{1,15},{2,0},{3,1},{4,2},{5,3},{6,4},{7,5},{8,6},{9,7},{10,... | collective-permute-start | bytes 589832 | tf_op jit(solution)/shard_map/ppermute | solution.py:26
  70.7 0.9 collective-permute-start.18
  71.5 1.1 collective-permute-start.17
  72.7 3.5 %rest_parts.1.refs_12_.refs_3_.refs_4_ = bf16[7,96,2048]{2,1,0:T(8,128)(2,1)S(1)} custom-call(s32[5]{0:T(128)S(1)} %copy-done.9, bf16[2048,1024]{1,0:T(8,128)(2,1)S(1)} %get-tuple-element.53.refs_1_, bf16[128,2048]{1,0:T(8,128)(2,1)S(1)} %get-tuple-element.54.refs_2_, f32[8,96,2048]{2,1,0:T(8,128)S(1)} %get-tuple-element.56.refs_5_.refs_3_, ...), custom_call_target="tpu_custom_call" | custom-call | flops 1000000000 | tf_op jit(solution)/shard_map/rest_parts/pallas_call | solution.py:65
  76.3 3.1 %collective-permute-done.18.refs_14_.refs_2_ = bf16[96,1024]{1,0:T(8,128)(2,1)S(1)} collective-permute-done((bf16[96,1024]{1,0:T(8,128)(2,1)S(1)}, bf16[96,1024]{1,0:T(8,128)(2,1)S(1)}, u32[]{:S(2)}, u32[]{:S(2)}) %collective-permute-start.18) | collective-permute-done | bytes 196640 | tf_op jit(solution)/shard_map/ppermute | solution.py:26
  79.4 0.7 collective-permute-done.17.refs_13_.refs_1_
  80.1 6.9 %wgrad_parts.1 = (bf16[4,256,1152]{2,1,0:T(8,128)(2,1)S(1)}, f32[8,128]{1,0:T(8,128)S(1)}) custom-call(s32[5]{0:T(128)S(1)} %copy-done.9, bf16[4,2,96,256]{3,2,1,0:T(8,128)(2,1)S(1)} %copy-done.14, bf16[4,2,96,256]{3,2,1,0:T(8,128)(2,1)S(1)} %collective-permute-done.4.refs_2_, bf16[4,2,96,256]{3,2,1,0:T(8,128)(2,1)S(1)} %collective-permute-done.5.refs_3_, ...), custom_call_target="tpu_custom_call" | custom-call | flops 10000000000 | tf_op jit(solution)/shard_map/wgrad_parts/pallas_call | solution.py:65
  87.1 1.5 %copy-done.1 = bf16[4,256,1152]{2,1,0:T(8,128)(2,1)} copy-done((bf16[4,256,1152]{2,1,0:T(8,128)(2,1)}, bf16[4,256,1152]{2,1,0:T(8,128)(2,1)S(1)}, u32[]{:S(2)}) %copy-start.1) | copy-done | bytes 2359320
  88.5 7.4 %all-to-all-start.1 = ((bf16[8,128,1152]{2,1,0:T(8,128)(2,1)}), bf16[8,128,1152]{2,1,0:T(8,128)(2,1)}, u32[]{:S(2)}, u32[]{:S(2)}) async-start(bf16[8,128,1152]{2,1,0:T(8,128)(2,1)} %bitcast.12), calls=%async_computation.1 | async-start | bytes 4718592 | tf_op jit(solution)/shard_map/all_to_all | solution.py:743
  96.7 3.2 %collective-permute-start.23 = (bf16[96,2048]{1,0:T(8,128)(2,1)S(1)}, bf16[96,2048]{1,0:T(8,128)(2,1)S(1)}, u32[]{:S(2)}, u32[]{:S(2)}) collective-permute-start(bf16[96,2048]{1,0:T(8,128)(2,1)S(1)} %get-tuple-element.65), channel_id=1, source_target_pairs={{0,14},{1,15},{2,0},{3,1},{4,2},{5,3},{6,4},{7,5},{8,6},{9,7},{10,... | collective-permute-start | bytes 1179656 | tf_op jit(solution)/shard_map/ppermute | solution.py:26
  99.9 8.1 %collective-permute-done.22.refs_1_ = bf16[96,2048]{1,0:T(8,128)(2,1)S(1)} collective-permute-done((bf16[96,2048]{1,0:T(8,128)(2,1)S(1)}, bf16[96,2048]{1,0:T(8,128)(2,1)S(1)}, u32[]{:S(2)}, u32[]{:S(2)}) %collective-permute-start.22) | collective-permute-done | bytes 393248 | tf_op jit(solution)/shard_map/ppermute | solution.py:26
  108.0 0.7 ring_step.5
  108.8 0.8 collective-permute-start.24
  109.5 2.6 %collective-permute-start.25 = (bf16[96,2048]{1,0:T(8,128)(2,1)S(1)}, bf16[96,2048]{1,0:T(8,128)(2,1)S(1)}, u32[]{:S(2)}, u32[]{:S(2)}) collective-permute-start(bf16[96,2048]{1,0:T(8,128)(2,1)S(1)} %get-tuple-element.67), channel_id=1, source_target_pairs={{0,14},{1,15},{2,0},{3,1},{4,2},{5,3},{6,4},{7,5},{8,6},{9,7},{10,... | collective-permute-start | bytes 1179656 | tf_op jit(solution)/shard_map/ppermute | solution.py:26
  112.1 7.3 %collective-permute-done.24.refs_1_ = bf16[96,2048]{1,0:T(8,128)(2,1)S(1)} collective-permute-done((bf16[96,2048]{1,0:T(8,128)(2,1)S(1)}, bf16[96,2048]{1,0:T(8,128)(2,1)S(1)}, u32[]{:S(2)}, u32[]{:S(2)}) %collective-permute-start.24) | collective-permute-done | bytes 393248 | tf_op jit(solution)/shard_map/ppermute | solution.py:26
  119.4 1.5 %ring_step.6 = (bf16[96,2048]{1,0:T(8,128)(2,1)}, bf16[96,2048]{1,0:T(8,128)(2,1)}) custom-call(s32[5]{0:T(128)S(1)} %copy-done.9, bf16[96,2048]{1,0:T(8,128)(2,1)S(1)} %collective-permute-done.24.refs_1_, bf16[96,2048]{1,0:T(8,128)(2,1)S(1)} %collective-permute-done.25.refs_2_, bf16[7,96,2048]{2,1,0:T(8,128)(2,1)S(1)} %rest_parts.1.refs_12_.refs_3_.refs_4_, ...), custom_call_target="tpu_custom_call" | custom-call | tf_op jit(solution)/shard_map/ring_step/pallas_call | solution.py:65
  120.9 3.0 %collective-permute-start.27 = (bf16[96,2048]{1,0:T(8,128)(2,1)}, bf16[96,2048]{1,0:T(8,128)(2,1)S(1)}, u32[]{:S(2)}, u32[]{:S(2)}) collective-permute-start(bf16[96,2048]{1,0:T(8,128)(2,1)} %get-tuple-element.69), channel_id=1, source_target_pairs={{0,14},{1,15},{2,0},{3,1},{4,2},{5,3},{6,4},{7,5},{8,6},{9,7},{10,... | collective-permute-start | bytes 1179656 | tf_op jit(solution)/shard_map/ppermute | solution.py:26
  123.9 2.6 %all-to-all-done.1.refs_1_ = bf16[8,128,1152]{2,1,0:T(8,128)(2,1)} async-done(((bf16[8,128,1152]{2,1,0:T(8,128)(2,1)}), bf16[8,128,1152]{2,1,0:T(8,128)(2,1)}, u32[]{:S(2)}, u32[]{:S(2)}) %all-to-all-start.1) | async-done | bytes 2359328 | tf_op jit(solution)/shard_map/all_to_all | solution.py:743
  126.5 2.0 %wgrad_sum.1 = (f32[128,512]{1,0:T(8,128)S(1)}, f32[128,128]{1,0:T(8,128)S(1)}, bf16[128,640]{1,0:T(8,128)(2,1)S(1)}) custom-call(s32[5]{0:T(128)S(1)} %copy-done.9, bf16[8,128,1152]{2,1,0:T(8,128)(2,1)} %all-to-all-done.1.refs_1_, bf16[96,2048]{1,0:T(8,128)(2,1)} %get-tuple-element.68.refs_2_), custom_call_target="tpu_custom_call" | custom-call | tf_op jit(solution)/shard_map/wgrad_sum/pallas_call | solution.py:65
  128.5 1.5 %collective-permute-done.27.refs_2_ = bf16[96,2048]{1,0:T(8,128)(2,1)S(1)} collective-permute-done((bf16[96,2048]{1,0:T(8,128)(2,1)}, bf16[96,2048]{1,0:T(8,128)(2,1)S(1)}, u32[]{:S(2)}, u32[]{:S(2)}) %collective-permute-start.27) | collective-permute-done | bytes 393248 | tf_op jit(solution)/shard_map/ppermute | solution.py:26
  130.0 3.3 %collective-permute-done.26.refs_1_ = bf16[96,2048]{1,0:T(8,128)(2,1)S(1)} collective-permute-done((bf16[96,2048]{1,0:T(8,128)(2,1)}, bf16[96,2048]{1,0:T(8,128)(2,1)S(1)}, u32[]{:S(2)}, u32[]{:S(2)}) %collective-permute-start.26) | collective-permute-done | bytes 393248 | tf_op jit(solution)/shard_map/ppermute | solution.py:26
  134.2 1.9 %collective-permute-start.29 = (bf16[128,640]{1,0:T(8,128)(2,1)S(1)}, bf16[128,640]{1,0:T(8,128)(2,1)S(1)}, u32[]{:S(2)}, u32[]{:S(2)}) collective-permute-start(bf16[128,640]{1,0:T(8,128)(2,1)S(1)} %get-tuple-element.71.refs_5_), channel_id=1, source_target_pairs={{0,1},{1,0},{2,3},{3,2},{4,5},{5,4},{6,7},{7,6},{8,9},{9,8},{10,11... | collective-permute-start | bytes 491528 | tf_op jit(solution)/shard_map/ppermute | solution.py:31
  136.1 5.4 %collective-permute-done.29.refs_5_ = bf16[128,640]{1,0:T(8,128)(2,1)S(1)} collective-permute-done((bf16[128,640]{1,0:T(8,128)(2,1)S(1)}, bf16[128,640]{1,0:T(8,128)(2,1)S(1)}, u32[]{:S(2)}, u32[]{:S(2)}) %collective-permute-start.29) | collective-permute-done | bytes 163872 | tf_op jit(solution)/shard_map/ppermute | solution.py:31
  141.5 1.5 %final.1 = (bf16[48,4096]{1,0:T(8,128)(2,1)}, f32[256,512]{1,0:T(8,128)}, f32[32,256]{1,0:T(8,128)}, f32[32,256]{1,0:T(8,128)}) custom-call(s32[5]{0:T(128)S(1)} %copy-done.9, bf16[48,2048]{1,0:T(8,128)(2,1)S(1)} %get-tuple-element.72.refs_1_, bf16[48,2048]{1,0:T(8,128)(2,1)S(1)} %collective-permute-done.28.refs_2_, ...), custom_call_target="tpu_custom_call" | custom-call | tf_op jit(solution)/shard_map/final/pallas_call | solution.py:65
  (67 shorter events, 7.3 us)
Async XLA Ops:
  3.3 7.0 %collective-permute-start = (bf16[4,48,256]{2,1,0:T(8,128)(2,1)}, bf16[4,48,256]{2,1,0:T(8,128)(2,1)}, u32[]{:S(2)}, u32[]{:S(2)}) collective-permute-start(bf16[4,48,256]{2,1,0:T(8,128)(2,1)} %get-tuple-element.43), channel_id=1, source_target_pairs={{0,1},{1,0},{2,3},{3,2},{4,5},{5,4},{6,7},{7,6},{8,9},{9,8},{10,11... | collective-permute-start | bytes 294920 | tf_op jit(solution)/shard_map/ppermute | solution.py:39
  4.0 6.2 %collective-permute-start.1 = (bf16[4,48,256]{2,1,0:T(8,128)(2,1)}, bf16[4,48,256]{2,1,0:T(8,128)(2,1)}, u32[]{:S(2)}, u32[]{:S(2)}) collective-permute-start(bf16[4,48,256]{2,1,0:T(8,128)(2,1)} %get-tuple-element.44), channel_id=1, source_target_pairs={{0,16},{1,17},{2,18},{3,19},{4,20},{5,21},{6,22},{7,23},{8,24},{9,... | collective-permute-start | bytes 294920 | tf_op jit(solution)/shard_map/ppermute | solution.py:39
  4.0 6.2 %collective-permute-start.2 = (bf16[4,48,256]{2,1,0:T(8,128)(2,1)}, bf16[4,48,256]{2,1,0:T(8,128)(2,1)}, u32[]{:S(2)}, u32[]{:S(2)}) collective-permute-start(bf16[4,48,256]{2,1,0:T(8,128)(2,1)} %get-tuple-element.45), channel_id=1, source_target_pairs={{0,17},{1,16},{2,19},{3,18},{4,21},{5,20},{6,23},{7,22},{8,25},{9,... | collective-permute-start | bytes 294920 | tf_op jit(solution)/shard_map/ppermute | solution.py:39
  5.4 14.9 %all-to-all-start = ((bf16[4,64,768]{2,1,0:T(8,128)(2,1)}), bf16[4,64,768]{2,1,0:T(8,128)(2,1)}, u32[]{:S(2)}, u32[]{:S(2)}) async-start(bf16[4,64,768]{2,1,0:T(8,128)(2,1)} %get-tuple-element.48), calls=%async_computation | async-start | bytes 786432 | tf_op jit(solution)/shard_map/all_to_all | solution.py:707
  13.4 19.7 %copy-start.9 = (s32[5]{0:T(128)S(1)}, s32[5]{0:T(128)}, u32[]{:S(2)}) copy-start(s32[5]{0:T(128)} %stack.23.refs_0_) | copy-start | bytes 64
  13.4 19.7 %collective-permute-start.3 = (bf16[576,512]{1,0:T(8,128)(2,1)}, bf16[576,512]{1,0:T(8,128)(2,1)S(1)}, u32[]{:S(2)}, u32[]{:S(2)}) collective-permute-start(bf16[576,512]{1,0:T(8,128)(2,1)} %get-tuple-element.46), channel_id=1, source_target_pairs={{0,1},{1,0},{2,3},{3,2},{4,5},{5,4},{6,7},{7,6},{8,9},{9,8},{10,11... | collective-permute-start | bytes 1769480 | tf_op jit(solution)/shard_map/ppermute | solution.py:31
  13.9 19.1 %collective-permute-start.5 = (bf16[4,2,96,256]{3,2,1,0:T(8,128)(2,1)}, bf16[4,2,96,256]{3,2,1,0:T(8,128)(2,1)S(1)}, u32[]{:S(2)}, u32[]{:S(2)}) collective-permute-start(bf16[4,2,96,256]{3,2,1,0:T(8,128)(2,1)} %get-tuple-element.47.refs_6_.refs_1_), channel_id=1, source_target_pairs={{0,14},{1,15},{2,0},{3,1},{4,2},{5,3},{6,4},{7,5},{8,6},{9,7},{10,... | collective-permute-start | bytes 1179656 | tf_op jit(solution)/shard_map/ppermute | solution.py:26
  20.3 12.7 %collective-permute-start.4 = (bf16[4,2,96,256]{3,2,1,0:T(8,128)(2,1)}, bf16[4,2,96,256]{3,2,1,0:T(8,128)(2,1)S(1)}, u32[]{:S(2)}, u32[]{:S(2)}) collective-permute-start(bf16[4,2,96,256]{3,2,1,0:T(8,128)(2,1)} %get-tuple-element.47.refs_6_.refs_1_), channel_id=1, source_target_pairs={{0,2},{1,3},{2,4},{3,5},{4,6},{5,7},{6,8},{7,9},{8,10},{9,11},{10,... | collective-permute-start | bytes 1179656 | tf_op jit(solution)/shard_map/ppermute | solution.py:26
  20.3 0.6 copy-start.8
  20.9 1.1 copy-start.10
  22.1 1.1 copy-start.11
  23.2 1.1 copy-start.12
  24.3 1.0 copy-start.13
  25.3 0.7 copy-start.15
  33.1 20.8 %copy-start = (bf16[4096,512]{1,0:T(8,128)(2,1)S(1)}, bf16[4096,512]{1,0:T(8,128)(2,1)}, u32[]{:S(2)}) copy-start(bf16[4096,512]{1,0:T(8,128)(2,1)} %refs_1_.3) | copy-start | bytes 12582916
  33.1 20.8 %copy-start.2 = (bf16[4096,32]{0,1:T(8,128)(2,1)S(1)}, bf16[4096,32]{0,1:T(8,128)(2,1)}, u32[]{:S(2)}) copy-start(bf16[4096,32]{0,1:T(8,128)(2,1)} %param.18) | copy-start | bytes 786436
  33.1 20.8 %copy-start.3 = (bf16[4096,32]{0,1:T(8,128)(2,1)S(1)}, bf16[4096,32]{0,1:T(8,128)(2,1)}, u32[]{:S(2)}) copy-start(bf16[4096,32]{0,1:T(8,128)(2,1)} %param.19) | copy-start | bytes 786436
  33.7 14.5 %collective-permute-start.6 = (bf16[576,512]{1,0:T(8,128)(2,1)S(1)}, bf16[576,512]{1,0:T(8,128)(2,1)S(1)}, u32[]{:S(2)}, u32[]{:S(2)}) collective-permute-start(bf16[576,512]{1,0:T(8,128)(2,1)S(1)} %again.1.refs_4_), channel_id=1, source_target_pairs={{0,64},{16,80},{32,96},{48,112},{64,0},{80,16},{96,32},{112,48},{1... | collective-permute-start | bytes 1769480 | tf_op jit(solution)/shard_map/ppermute | solution.py:31
  34.3 7.8 %collective-permute-start.9 = (bf16[2,64,768]{2,1,0:T(8,128)(2,1)S(1)}, bf16[2,64,768]{2,1,0:T(8,128)(2,1)S(1)}, u32[]{:S(2)}, u32[]{:S(2)}) collective-permute-start(bf16[2,64,768]{2,1,0:T(8,128)(2,1)S(1)} %get-tuple-element.51), channel_id=1, source_target_pairs={{0,2},{1,3},{2,0},{3,1},{4,6},{5,7},{6,4},{7,5},{8,10},{9,11},{10,... | collective-permute-start | bytes 589832 | tf_op jit(solution)/shard_map/ppermute | solution.py:31
  34.3 14.1 %collective-permute-start.11 = (bf16[4,2,96,256]{3,2,1,0:T(8,128)(2,1)S(1)}, bf16[4,2,96,256]{3,2,1,0:T(8,128)(2,1)S(1)}, u32[]{:S(2)}, u32[]{:S(2)}) collective-permute-start(bf16[4,2,96,256]{3,2,1,0:T(8,128)(2,1)S(1)} %collective-permute-done.5.refs_3_), channel_id=1, source_target_pairs={{0,14},{1,15},{2,0},{3,1},{4,2},{5,3},{6,4},{7,5},{8,6},{9,7},{10,... | collective-permute-start | bytes 1179656 | tf_op jit(solution)/shard_map/ppermute | solution.py:26
  37.8 12.1 %collective-permute-start.10 = (bf16[4,2,96,256]{3,2,1,0:T(8,128)(2,1)S(1)}, bf16[4,2,96,256]{3,2,1,0:T(8,128)(2,1)S(1)}, u32[]{:S(2)}, u32[]{:S(2)}) collective-permute-start(bf16[4,2,96,256]{3,2,1,0:T(8,128)(2,1)S(1)} %collective-permute-done.4.refs_2_), channel_id=1, source_target_pairs={{0,2},{1,3},{2,4},{3,5},{4,6},{5,7},{6,8},{7,9},{8,10},{9,11},{10,... | collective-permute-start | bytes 1179656 | tf_op jit(solution)/shard_map/ppermute | solution.py:26
  37.8 14.8 %collective-permute-start.12 = (bf16[768,256]{1,0:T(8,128)(2,1)S(1)}, bf16[768,256]{1,0:T(8,128)(2,1)S(1)}, u32[]{:S(2)}, u32[]{:S(2)}) collective-permute-start(bf16[768,256]{1,0:T(8,128)(2,1)S(1)} %get-tuple-element.49.refs_4_.refs_2_), channel_id=1, source_target_pairs={{0,1},{1,0},{2,3},{3,2},{4,5},{5,4},{6,7},{7,6},{8,9},{9,8},{10,11... | collective-permute-start | bytes 1179656 | tf_op jit(solution)/shard_map/ppermute | solution.py:31
  42.1 11.1 %collective-permute-start.7 = (bf16[576,512]{1,0:T(8,128)(2,1)S(1)}, bf16[576,512]{1,0:T(8,128)(2,1)S(1)}, u32[]{:S(2)}, u32[]{:S(2)}) collective-permute-start(bf16[576,512]{1,0:T(8,128)(2,1)S(1)} %again.1.refs_4_), channel_id=1, source_target_pairs={{0,16},{16,0},{32,48},{48,32},{64,80},{80,64},{96,112},{112,96},{1... | collective-permute-start | bytes 1769480 | tf_op jit(solution)/shard_map/ppermute | solution.py:31
  48.2 5.7 %collective-permute-start.8 = (bf16[576,512]{1,0:T(8,128)(2,1)S(1)}, bf16[576,512]{1,0:T(8,128)(2,1)S(1)}, u32[]{:S(2)}, u32[]{:S(2)}) collective-permute-start(bf16[576,512]{1,0:T(8,128)(2,1)S(1)} %collective-permute-done.6.refs_6_.refs_5_), channel_id=1, source_target_pairs={{0,16},{16,0},{32,48},{48,32},{64,80},{80,64},{96,112},{112,96},{1... | collective-permute-start | bytes 1769480 | tf_op jit(solution)/shard_map/ppermute | solution.py:31
  48.4 11.9 %collective-permute-start.14 = (bf16[768,256]{1,0:T(8,128)(2,1)S(1)}, bf16[768,256]{1,0:T(8,128)(2,1)S(1)}, u32[]{:S(2)}, u32[]{:S(2)}) collective-permute-start(bf16[768,256]{1,0:T(8,128)(2,1)S(1)} %get-tuple-element.55.refs_3_), channel_id=1, source_target_pairs={{0,1},{1,0},{2,3},{3,2},{4,5},{5,4},{6,7},{7,6},{8,9},{9,8},{10,11... | collective-permute-start | bytes 1179656 | tf_op jit(solution)/shard_map/ppermute | solution.py:31
  49.9 11.5 %collective-permute-start.16 = (bf16[4,2,96,256]{3,2,1,0:T(8,128)(2,1)S(1)}, bf16[4,2,96,256]{3,2,1,0:T(8,128)(2,1)S(1)}, u32[]{:S(2)}, u32[]{:S(2)}) collective-permute-start(bf16[4,2,96,256]{3,2,1,0:T(8,128)(2,1)S(1)} %collective-permute-done.11.refs_4_.refs_5_), channel_id=1, source_target_pairs={{0,14},{1,15},{2,0},{3,1},{4,2},{5,3},{6,4},{7,5},{8,6},{9,7},{10,... | collective-permute-start | bytes 1179656 | tf_op jit(solution)/shard_map/ppermute | solution.py:26
  52.6 12.2 %collective-permute-start.15 = (bf16[4,2,96,256]{3,2,1,0:T(8,128)(2,1)S(1)}, bf16[4,2,96,256]{3,2,1,0:T(8,128)(2,1)S(1)}, u32[]{:S(2)}, u32[]{:S(2)}) collective-permute-start(bf16[4,2,96,256]{3,2,1,0:T(8,128)(2,1)S(1)} %collective-permute-done.10.refs_3_.refs_4_), channel_id=1, source_target_pairs={{0,2},{1,3},{2,4},{3,5},{4,6},{5,7},{6,8},{7,9},{8,10},{9,11},{10,... | collective-permute-start | bytes 1179656 | tf_op jit(solution)/shard_map/ppermute | solution.py:26
  53.2 11.6 %collective-permute-start.13 = (bf16[2,64,768]{2,1,0:T(8,128)(2,1)S(1)}, bf16[2,64,768]{2,1,0:T(8,128)(2,1)S(1)}, u32[]{:S(2)}, u32[]{:S(2)}) collective-permute-start(bf16[2,64,768]{2,1,0:T(8,128)(2,1)S(1)} %get-tuple-element.52.refs_8_), channel_id=1, source_target_pairs={{0,1},{1,0},{2,3},{3,2},{4,5},{5,4},{6,7},{7,6},{8,9},{9,8},{10,11... | collective-permute-start | bytes 589832 | tf_op jit(solution)/shard_map/ppermute | solution.py:31
  65.5 14.6 %collective-permute-start.21 = (bf16[768,1152]{1,0:T(8,128)(2,1)S(1)}, bf16[768,1152]{1,0:T(8,128)(2,1)S(1)}, u32[]{:S(2)}, u32[]{:S(2)}) collective-permute-start(bf16[768,1152]{1,0:T(8,128)(2,1)S(1)} %kv_final.1.refs_4_.refs_10_), channel_id=1, source_target_pairs={{0,16},{16,0},{32,48},{48,32},{64,80},{80,64},{96,112},{112,96},{1... | collective-permute-start | bytes 5308424 | tf_op jit(solution)/shard_map/ppermute | solution.py:31
  67.3 9.0 %collective-permute-start.19 = (bf16[2,2,96,256]{3,2,1,0:T(8,128)(2,1)S(1)}, bf16[2,2,96,256]{3,2,1,0:T(8,128)(2,1)S(1)}, u32[]{:S(2)}, u32[]{:S(2)}) collective-permute-start(bf16[2,2,96,256]{3,2,1,0:T(8,128)(2,1)S(1)} %get-tuple-element.61), channel_id=1, source_target_pairs={{0,2},{1,3},{2,4},{3,5},{4,6},{5,7},{6,8},{7,9},{8,10},{9,11},{10,... | collective-permute-start | bytes 589832 | tf_op jit(solution)/shard_map/ppermute | solution.py:26
  67.4 8.9 %collective-permute-start.20 = (bf16[2,2,96,256]{3,2,1,0:T(8,128)(2,1)S(1)}, bf16[2,2,96,256]{3,2,1,0:T(8,128)(2,1)S(1)}, u32[]{:S(2)}, u32[]{:S(2)}) collective-permute-start(bf16[2,2,96,256]{3,2,1,0:T(8,128)(2,1)S(1)} %get-tuple-element.62), channel_id=1, source_target_pairs={{0,14},{1,15},{2,0},{3,1},{4,2},{5,3},{6,4},{7,5},{8,6},{9,7},{10,... | collective-permute-start | bytes 589832 | tf_op jit(solution)/shard_map/ppermute | solution.py:26
  70.7 8.8 %collective-permute-start.18 = (bf16[96,1024]{1,0:T(8,128)(2,1)S(1)}, bf16[96,1024]{1,0:T(8,128)(2,1)S(1)}, u32[]{:S(2)}, u32[]{:S(2)}) collective-permute-start(bf16[96,1024]{1,0:T(8,128)(2,1)S(1)} %get-tuple-element.60), channel_id=1, source_target_pairs={{0,14},{1,15},{2,0},{3,1},{4,2},{5,3},{6,4},{7,5},{8,6},{9,7},{10,... | collective-permute-start | bytes 589832 | tf_op jit(solution)/shard_map/ppermute | solution.py:26
  71.5 8.6 %copy-start.14 = (bf16[4,2,96,256]{3,2,1,0:T(8,128)(2,1)S(1)}, bf16[4,2,96,256]{3,2,1,0:T(8,128)(2,1)}, u32[]{:S(2)}) copy-start(bf16[4,2,96,256]{3,2,1,0:T(8,128)(2,1)} %get-tuple-element.47.refs_6_.refs_1_) | copy-start | bytes 1179652
  71.5 8.6 %collective-permute-start.17 = (bf16[96,1024]{1,0:T(8,128)(2,1)S(1)}, bf16[96,1024]{1,0:T(8,128)(2,1)S(1)}, u32[]{:S(2)}, u32[]{:S(2)}) collective-permute-start(bf16[96,1024]{1,0:T(8,128)(2,1)S(1)} %get-tuple-element.59.refs_5_), channel_id=1, source_target_pairs={{0,2},{1,3},{2,4},{3,5},{4,6},{5,7},{6,8},{7,9},{8,10},{9,11},{10,... | collective-permute-start | bytes 589832 | tf_op jit(solution)/shard_map/ppermute | solution.py:26
  79.4 7.7 %copy-start.4 = (bf16[96,1024]{1,0:T(8,128)(2,1)}, bf16[96,1024]{1,0:T(8,128)(2,1)S(1)}, u32[]{:S(2)}) copy-start(bf16[96,1024]{1,0:T(8,128)(2,1)S(1)} %collective-permute-done.18.refs_14_.refs_2_) | copy-start | bytes 589828
  80.1 6.9 %copy-start.6 = (bf16[96,1024]{1,0:T(8,128)(2,1)}, bf16[96,1024]{1,0:T(8,128)(2,1)S(1)}, u32[]{:S(2)}) copy-start(bf16[96,1024]{1,0:T(8,128)(2,1)S(1)} %collective-permute-done.17.refs_13_.refs_1_) | copy-start | bytes 589828
  87.1 1.5 %copy-start.1 = (bf16[4,256,1152]{2,1,0:T(8,128)(2,1)}, bf16[4,256,1152]{2,1,0:T(8,128)(2,1)S(1)}, u32[]{:S(2)}) copy-start(bf16[4,256,1152]{2,1,0:T(8,128)(2,1)S(1)} %get-tuple-element.70) | copy-start | bytes 7077892
  88.5 7.4 %copy-start.5 = (bf16[96,1024]{1,0:T(8,128)(2,1)S(1)}, bf16[96,1024]{1,0:T(8,128)(2,1)}, u32[]{:S(2)}) copy-start(bf16[96,1024]{1,0:T(8,128)(2,1)} %copy-done.4) | copy-start | bytes 589828
  88.5 7.4 %copy-start.7 = (bf16[96,1024]{1,0:T(8,128)(2,1)S(1)}, bf16[96,1024]{1,0:T(8,128)(2,1)}, u32[]{:S(2)}) copy-start(bf16[96,1024]{1,0:T(8,128)(2,1)} %copy-done.6) | copy-start | bytes 589828
  88.5 37.9 %all-to-all-start.1 = ((bf16[8,128,1152]{2,1,0:T(8,128)(2,1)}), bf16[8,128,1152]{2,1,0:T(8,128)(2,1)}, u32[]{:S(2)}, u32[]{:S(2)}) async-start(bf16[8,128,1152]{2,1,0:T(8,128)(2,1)} %bitcast.12), calls=%async_computation.1 | async-start | bytes 4718592 | tf_op jit(solution)/shard_map/all_to_all | solution.py:743
  96.6 11.5 %collective-permute-start.22 = (bf16[96,2048]{1,0:T(8,128)(2,1)S(1)}, bf16[96,2048]{1,0:T(8,128)(2,1)S(1)}, u32[]{:S(2)}, u32[]{:S(2)}) collective-permute-start(bf16[96,2048]{1,0:T(8,128)(2,1)S(1)} %get-tuple-element.64), channel_id=1, source_target_pairs={{0,2},{1,3},{2,4},{3,5},{4,6},{5,7},{6,8},{7,9},{8,10},{9,11},{10,... | collective-permute-start | bytes 1179656 | tf_op jit(solution)/shard_map/ppermute | solution.py:26
  96.7 11.4 %collective-permute-start.23 = (bf16[96,2048]{1,0:T(8,128)(2,1)S(1)}, bf16[96,2048]{1,0:T(8,128)(2,1)S(1)}, u32[]{:S(2)}, u32[]{:S(2)}) collective-permute-start(bf16[96,2048]{1,0:T(8,128)(2,1)S(1)} %get-tuple-element.65), channel_id=1, source_target_pairs={{0,14},{1,15},{2,0},{3,1},{4,2},{5,3},{6,4},{7,5},{8,6},{9,7},{10,... | collective-permute-start | bytes 1179656 | tf_op jit(solution)/shard_map/ppermute | solution.py:26
  108.8 10.6 %collective-permute-start.24 = (bf16[96,2048]{1,0:T(8,128)(2,1)S(1)}, bf16[96,2048]{1,0:T(8,128)(2,1)S(1)}, u32[]{:S(2)}, u32[]{:S(2)}) collective-permute-start(bf16[96,2048]{1,0:T(8,128)(2,1)S(1)} %get-tuple-element.66), channel_id=1, source_target_pairs={{0,2},{1,3},{2,4},{3,5},{4,6},{5,7},{6,8},{7,9},{8,10},{9,11},{10,... | collective-permute-start | bytes 1179656 | tf_op jit(solution)/shard_map/ppermute | solution.py:26
  109.5 9.9 %collective-permute-start.25 = (bf16[96,2048]{1,0:T(8,128)(2,1)S(1)}, bf16[96,2048]{1,0:T(8,128)(2,1)S(1)}, u32[]{:S(2)}, u32[]{:S(2)}) collective-permute-start(bf16[96,2048]{1,0:T(8,128)(2,1)S(1)} %get-tuple-element.67), channel_id=1, source_target_pairs={{0,14},{1,15},{2,0},{3,1},{4,2},{5,3},{6,4},{7,5},{8,6},{9,7},{10,... | collective-permute-start | bytes 1179656 | tf_op jit(solution)/shard_map/ppermute | solution.py:26
  120.9 9.0 %collective-permute-start.27 = (bf16[96,2048]{1,0:T(8,128)(2,1)}, bf16[96,2048]{1,0:T(8,128)(2,1)S(1)}, u32[]{:S(2)}, u32[]{:S(2)}) collective-permute-start(bf16[96,2048]{1,0:T(8,128)(2,1)} %get-tuple-element.69), channel_id=1, source_target_pairs={{0,14},{1,15},{2,0},{3,1},{4,2},{5,3},{6,4},{7,5},{8,6},{9,7},{10,... | collective-permute-start | bytes 1179656 | tf_op jit(solution)/shard_map/ppermute | solution.py:26
  123.9 9.4 %collective-permute-start.26 = (bf16[96,2048]{1,0:T(8,128)(2,1)}, bf16[96,2048]{1,0:T(8,128)(2,1)S(1)}, u32[]{:S(2)}, u32[]{:S(2)}) collective-permute-start(bf16[96,2048]{1,0:T(8,128)(2,1)} %get-tuple-element.68.refs_2_), channel_id=1, source_target_pairs={{0,2},{1,3},{2,4},{3,5},{4,6},{5,7},{6,8},{7,9},{8,10},{9,11},{10,... | collective-permute-start | bytes 1179656 | tf_op jit(solution)/shard_map/ppermute | solution.py:26
  134.0 7.5 %collective-permute-start.28 = (bf16[48,2048]{1,0:T(8,128)(2,1)S(1)}, bf16[48,2048]{1,0:T(8,128)(2,1)S(1)}, u32[]{:S(2)}, u32[]{:S(2)}) collective-permute-start(bf16[48,2048]{1,0:T(8,128)(2,1)S(1)} %get-tuple-element.73), channel_id=1, source_target_pairs={{0,1},{1,0},{2,3},{3,2},{4,5},{5,4},{6,7},{7,6},{8,9},{9,8},{10,11... | collective-permute-start | bytes 589832 | tf_op jit(solution)/shard_map/ppermute | solution.py:31
  134.2 7.3 %collective-permute-start.29 = (bf16[128,640]{1,0:T(8,128)(2,1)S(1)}, bf16[128,640]{1,0:T(8,128)(2,1)S(1)}, u32[]{:S(2)}, u32[]{:S(2)}) collective-permute-start(bf16[128,640]{1,0:T(8,128)(2,1)S(1)} %get-tuple-element.71.refs_5_), channel_id=1, source_target_pairs={{0,1},{1,0},{2,3},{3,2},{4,5},{5,4},{6,7},{7,6},{8,9},{9,8},{10,11... | collective-permute-start | bytes 491528 | tf_op jit(solution)/shard_map/ppermute | solution.py:31

commit v6 on v5

--- a/solution.py
+++ b/solution.py
@@ -112,7 +112,9 @@
     )
 
 
-def block_kernel(spot, own, side, core, both, w_query, w_key, w_value, out, w_send, sems):
+def block_kernel(
+    spot, own, side, core, both, w_query, w_key, w_value, out, w_send, done, sems
+):
     h = spot[H]
     rows = own.shape[1]
     kv_w = w_key.shape[0]
@@ -137,6 +139,7 @@
     out[:, 0, far, :] = side[...]
     out[:, 1, near, :] = core[...]
     out[:, 1, far, :] = both[...]
+    done[...] = jnp.zeros_like(done)
     for copy in copies:
         copy.wait()
 
@@ -150,8 +153,12 @@
         spot,
         (*parts, w_query, w_key, w_value),
         [VMEM] * 4 + [ANY] * 3,
-        [shape((part, 2, 2 * rows, wide)), shape((w_rows, w_query.shape[1]))],
-        [VMEM, VMEM],
+        [
+            shape((part, 2, 2 * rows, wide)),
+            shape((w_rows, w_query.shape[1])),
+            shape((8, DH), F32),
+        ],
+        [VMEM] * 3,
         [pltpu.SemaphoreType.DMA((3,))],
         vmem=64,
     )
@@ -705,11 +712,13 @@
     core = swap_quad(core, 1, 0)
     both = swap_quad(both, 1, 1)
     kv = lax.all_to_all(kv, "tensor", 0, 0, axis_index_groups=heads4, tiled=True)
-    block, w_send = token_block(spot, (own, side, core, both), w_query, w_key, w_value)
+    block, w_send, formed = token_block(
+        spot, (own, side, core, both), w_query, w_key, w_value
+    )
     w_side = swap(w_send, "tensor", 1)
     up1, down1 = shift(block, "tensor", 2), shift(block, "tensor", -2)
     own_a, own_b, kv_send, kv_keep = attend(
-        spot, kv, queries, out_grads, outputs, log_norms, [block]
+        spot, kv, queries, out_grads, outputs, log_norms, [formed]
     )
     w_side = again(spot, w_side, [up1, down1, own_a])
     far_a = swap(own_a, "tensor", 1)

time: 144 us -> 143 us (level)
  no operation moved by 1% of the time
where the time goes in v6:
time: 143 us
  starting transfers between devices  48.5 us (34%)
  waiting for transfers between devices  46.4 us (32%)
  Pallas kernels  39.3 us (27%)
  local copies, waits for them, and re-layouts  7.47 us (5%)
    pallas_call x18, Pallas kernels, call(): pl.pallas_call(whole, grid=grid, in_specs=[SMEM, *specs, *[ANY] * (n_late...  39.3 us
    ppermute x16, waiting for transfers between devices, shift(): return lax.ppermute(value, axis, pairs)  28.9 us
    ppermute x16, starting transfers between devices, shift(): return lax.ppermute(value, axis, pairs)  27.6 us
    ppermute x11, waiting for transfers between devices, swap(): return lax.ppermute(value, axis, pairs)  14.8 us
    all_to_all x1, starting transfers between devices, body(): lax.all_to_all(terms, 'dp', 0, 0, axis_index_groups=plane, tiled=True)  7.36 us
    unnamed x32, local copies, waits for them, and re-layouts  6.88 us
    ppermute x11, starting transfers between devices, swap(): return lax.ppermute(value, axis, pairs)  6.66 us
    all_to_all x1, starting transfers between devices, body(): lax.all_to_all(kv, 'tensor', 0, 0, axis_index_groups=heads4, tiled=True)  4.81 us
  transfers between devices with their start and end apart: 32, of which 15 were waited for; matrix products, arithmetic and copies ran while one was open for 0% of the time, Pallas kernels for 19%

profile of v6, /device:TPU:26, one launch (start us, length us, event | category | flops | bytes accessed | tf_op | source)
XLA Modules:
  0.0 142.7 jit_solution(2558375026899716533)
XLA Ops:
  1.3 2.0 %pack.1 = (bf16[4,48,256]{2,1,0:T(8,128)(2,1)}, bf16[4,48,256]{2,1,0:T(8,128)(2,1)}, bf16[4,48,256]{2,1,0:T(8,128)(2,1)}, bf16[4,48,256]{2,1,0:T(8,128)(2,1)}, bf16[4,64,768]{2,1,0:T(8,128)(2,1)}) custom-call(s32[5]{0:T(128)} %stack.23.refs_0_, bf16[48,4096]{1,0:T(8,128)(2,1)} %refs_1_.2, bf16[32,768]{1,0:T(8,128)(2,1)} %bitcast.17, bf16[32,768]{1,0:T(8,128)(2,1)} %bitcast.18), custom_call_target="tpu_custom_call" | custom-call | tf_op jit(solution)/shard_map/pack/pallas_call | solution.py:65
  3.3 0.7 collective-permute-start
  4.0 1.4 collective-permute-start.2
  5.4 4.8 %all-to-all-start = ((bf16[4,64,768]{2,1,0:T(8,128)(2,1)}), bf16[4,64,768]{2,1,0:T(8,128)(2,1)}, u32[]{:S(2)}, u32[]{:S(2)}) async-start(bf16[4,64,768]{2,1,0:T(8,128)(2,1)} %get-tuple-element.49), calls=%async_computation | async-start | bytes 786432 | tf_op jit(solution)/shard_map/all_to_all | solution.py:714
  10.3 3.1 %token_block.1 = (bf16[4,2,96,256]{3,2,1,0:T(8,128)(2,1)}, bf16[576,512]{1,0:T(8,128)(2,1)}, f32[8,128]{1,0:T(8,128)}) custom-call(s32[5]{0:T(128)} %stack.23.refs_0_, bf16[4,48,256]{2,1,0:T(8,128)(2,1)} %get-tuple-element.43.refs_1_, bf16[4,48,256]{2,1,0:T(8,128)(2,1)} %collective-permute-done.refs_2_, bf16[4,48,256]{2,1,0:T(8,128)(2,1)} %collective-permute-done.1.refs_3_, ...), custom_call_target="tpu_custom_call" | custom-call | tf_op jit(solution)/shard_map/token_block/pallas_call | solution.py:65
  13.9 6.4 %collective-permute-start.5 = (bf16[4,2,96,256]{3,2,1,0:T(8,128)(2,1)}, bf16[4,2,96,256]{3,2,1,0:T(8,128)(2,1)S(1)}, u32[]{:S(2)}, u32[]{:S(2)}) collective-permute-start(bf16[4,2,96,256]{3,2,1,0:T(8,128)(2,1)} %get-tuple-element.48.refs_1_), channel_id=1, source_target_pairs={{0,14},{1,15},{2,0},{3,1},{4,2},{5,3},{6,4},{7,5},{8,6},{9,7},{10,... | collective-permute-start | bytes 1179656 | tf_op jit(solution)/shard_map/ppermute | solution.py:26
  20.9 1.1 copy-done.10
  22.0 1.1 copy-done.11
  23.2 1.1 copy-done.12
  24.3 0.7 copy-done.14
  25.7 7.0 %attend.1 = (bf16[768,256]{1,0:T(8,128)(2,1)S(1)}, bf16[768,256]{1,0:T(8,128)(2,1)S(1)}, bf16[2,64,768]{2,1,0:T(8,128)(2,1)S(1)}, f32[2,64,768]{2,1,0:T(8,128)S(1)}) custom-call(s32[5]{0:T(128)S(1)} %copy-done.8, bf16[4,64,768]{2,1,0:T(8,128)(2,1)} %all-to-all-done.refs_1_, bf16[768,512]{1,0:T(8,128)(2,1)S(1)} %copy-done.10, ...), custom_call_target="tpu_custom_call" | custom-call | flops 1000000000 | tf_op jit(solution)/shard_map/attend/pallas_call | solution.py:65
  34.0 3.5 %collective-permute-start.11 = (bf16[4,2,96,256]{3,2,1,0:T(8,128)(2,1)S(1)}, bf16[4,2,96,256]{3,2,1,0:T(8,128)(2,1)S(1)}, u32[]{:S(2)}, u32[]{:S(2)}) collective-permute-start(bf16[4,2,96,256]{3,2,1,0:T(8,128)(2,1)S(1)} %collective-permute-done.5.refs_3_), channel_id=1, source_target_pairs={{0,14},{1,15},{2,0},{3,1},{4,2},{5,3},{6,4},{7,5},{8,6},{9,7},{10,... | collective-permute-start | bytes 1179656 | tf_op jit(solution)/shard_map/ppermute | solution.py:26
  37.5 1.2 collective-permute-start.12
  38.7 3.1 %collective-permute-done.9.refs_2_ = bf16[2,64,768]{2,1,0:T(8,128)(2,1)S(1)} collective-permute-done((bf16[2,64,768]{2,1,0:T(8,128)(2,1)S(1)}, bf16[2,64,768]{2,1,0:T(8,128)(2,1)S(1)}, u32[]{:S(2)}, u32[]{:S(2)}) %collective-permute-start.9) | collective-permute-done | bytes 196640 | tf_op jit(solution)/shard_map/ppermute | solution.py:31
  41.8 6.0 %collective-permute-done.6.refs_6_.refs_5_ = bf16[576,512]{1,0:T(8,128)(2,1)S(1)} collective-permute-done((bf16[576,512]{1,0:T(8,128)(2,1)S(1)}, bf16[576,512]{1,0:T(8,128)(2,1)S(1)}, u32[]{:S(2)}, u32[]{:S(2)}) %collective-permute-start.6) | collective-permute-done | bytes 589856 | tf_op jit(solution)/shard_map/ppermute | solution.py:31
  48.1 1.5 %collective-permute-start.14 = (bf16[768,256]{1,0:T(8,128)(2,1)S(1)}, bf16[768,256]{1,0:T(8,128)(2,1)S(1)}, u32[]{:S(2)}, u32[]{:S(2)}) collective-permute-start(bf16[768,256]{1,0:T(8,128)(2,1)S(1)} %get-tuple-element.57.refs_3_), channel_id=1, source_target_pairs={{0,1},{1,0},{2,3},{3,2},{4,5},{5,4},{6,7},{7,6},{8,9},{9,8},{10,11... | collective-permute-start | bytes 1179656 | tf_op jit(solution)/shard_map/ppermute | solution.py:31
  49.6 2.7 %collective-permute-start.16 = (bf16[4,2,96,256]{3,2,1,0:T(8,128)(2,1)S(1)}, bf16[4,2,96,256]{3,2,1,0:T(8,128)(2,1)S(1)}, u32[]{:S(2)}, u32[]{:S(2)}) collective-permute-start(bf16[4,2,96,256]{3,2,1,0:T(8,128)(2,1)S(1)} %collective-permute-done.11.refs_4_.refs_5_), channel_id=1, source_target_pairs={{0,14},{1,15},{2,0},{3,1},{4,2},{5,3},{6,4},{7,5},{8,6},{9,7},{10,... | collective-permute-start | bytes 1179656 | tf_op jit(solution)/shard_map/ppermute | solution.py:26
  53.5 1.5 %gather_weights.1 = (bf16[2048,1024]{1,0:T(8,128)(2,1)S(1)}, bf16[128,2048]{1,0:T(8,128)(2,1)S(1)}) custom-call(s32[5]{0:T(128)S(1)} %copy-done.9, bf16[4096,512]{1,0:T(8,128)(2,1)S(1)} %copy-done, bf16[32,4096]{1,0:T(8,128)(2,1)S(1)} %bitcast.14, bf16[32,4096]{1,0:T(8,128)(2,1)S(1)} %bitcast.16, bf16[576,512]{1,0:T(8,128)(2,1)S(1)} %again.1.refs_4_, ...), custom_call_target="tpu_custom_call" | custom-call | tf_op jit(solution)/shard_map/gather_weights/pallas_call | solution.py:65
  55.0 4.7 %early_parts.1 = (f32[8,96,2048]{2,1,0:T(8,128)S(1)}, bf16[768,768]{1,0:T(8,128)(2,1)S(1)}) custom-call(s32[5]{0:T(128)S(1)} %copy-done.9, bf16[2048,1024]{1,0:T(8,128)(2,1)S(1)} %get-tuple-element.55.refs_1_, bf16[768,256]{1,0:T(8,128)(2,1)S(1)} %get-tuple-element.51.refs_4_.refs_2_, bf16[768,256]{1,0:T(8,128)(2,1)S(1)} %get-tuple-element.57.refs_3_, ...), custom_call_target="tpu_custom_call" | custom-call | flops 1000000000 | tf_op jit(solution)/shard_map/early_parts/pallas_call | solution.py:65
  60.0 1.0 collective-permute-done.16.refs_7_.refs_2_
  61.0 3.4 %collective-permute-done.15.refs_6_.refs_1_ = bf16[4,2,96,256]{3,2,1,0:T(8,128)(2,1)S(1)} collective-permute-done((bf16[4,2,96,256]{3,2,1,0:T(8,128)(2,1)S(1)}, bf16[4,2,96,256]{3,2,1,0:T(8,128)(2,1)S(1)}, u32[]{:S(2)}, u32[]{:S(2)}) %collective-permute-start.15) | collective-permute-done | bytes 393248 | tf_op jit(solution)/shard_map/ppermute | solution.py:26
  64.4 0.7 kv_final.1.refs_4_.refs_10_
  65.3 1.2 first_parts.1
  67.1 3.2 %collective-permute-start.20 = (bf16[2,2,96,256]{3,2,1,0:T(8,128)(2,1)S(1)}, bf16[2,2,96,256]{3,2,1,0:T(8,128)(2,1)S(1)}, u32[]{:S(2)}, u32[]{:S(2)}) collective-permute-start(bf16[2,2,96,256]{3,2,1,0:T(8,128)(2,1)S(1)} %get-tuple-element.64), channel_id=1, source_target_pairs={{0,14},{1,15},{2,0},{3,1},{4,2},{5,3},{6,4},{7,5},{8,6},{9,7},{10,... | collective-permute-start | bytes 589832 | tf_op jit(solution)/shard_map/ppermute | solution.py:26
  70.3 0.9 collective-permute-start.18
  71.2 1.1 collective-permute-start.17
  72.4 3.5 %rest_parts.1.refs_12_.refs_3_.refs_4_ = bf16[7,96,2048]{2,1,0:T(8,128)(2,1)S(1)} custom-call(s32[5]{0:T(128)S(1)} %copy-done.9, bf16[2048,1024]{1,0:T(8,128)(2,1)S(1)} %get-tuple-element.55.refs_1_, bf16[128,2048]{1,0:T(8,128)(2,1)S(1)} %get-tuple-element.56.refs_2_, f32[8,96,2048]{2,1,0:T(8,128)S(1)} %get-tuple-element.58.refs_5_.refs_3_, ...), custom_call_target="tpu_custom_call" | custom-call | flops 1000000000 | tf_op jit(solution)/shard_map/rest_parts/pallas_call | solution.py:65
  76.0 3.1 %collective-permute-done.18.refs_14_.refs_2_ = bf16[96,1024]{1,0:T(8,128)(2,1)S(1)} collective-permute-done((bf16[96,1024]{1,0:T(8,128)(2,1)S(1)}, bf16[96,1024]{1,0:T(8,128)(2,1)S(1)}, u32[]{:S(2)}, u32[]{:S(2)}) %collective-permute-start.18) | collective-permute-done | bytes 196640 | tf_op jit(solution)/shard_map/ppermute | solution.py:26
  79.1 0.7 collective-permute-done.17.refs_13_.refs_1_
  79.8 6.9 %wgrad_parts.1 = (bf16[4,256,1152]{2,1,0:T(8,128)(2,1)S(1)}, f32[8,128]{1,0:T(8,128)S(1)}) custom-call(s32[5]{0:T(128)S(1)} %copy-done.9, bf16[4,2,96,256]{3,2,1,0:T(8,128)(2,1)S(1)} %copy-done.13, bf16[4,2,96,256]{3,2,1,0:T(8,128)(2,1)S(1)} %collective-permute-done.4.refs_2_, bf16[4,2,96,256]{3,2,1,0:T(8,128)(2,1)S(1)} %collective-permute-done.5.refs_3_, ...), custom_call_target="tpu_custom_call" | custom-call | flops 10000000000 | tf_op jit(solution)/shard_map/wgrad_parts/pallas_call | solution.py:65
  86.8 1.5 %copy-done.1 = bf16[4,256,1152]{2,1,0:T(8,128)(2,1)} copy-done((bf16[4,256,1152]{2,1,0:T(8,128)(2,1)}, bf16[4,256,1152]{2,1,0:T(8,128)(2,1)S(1)}, u32[]{:S(2)}) %copy-start.1) | copy-done | bytes 2359320
  88.2 7.4 %all-to-all-start.1 = ((bf16[8,128,1152]{2,1,0:T(8,128)(2,1)}), bf16[8,128,1152]{2,1,0:T(8,128)(2,1)}, u32[]{:S(2)}, u32[]{:S(2)}) async-start(bf16[8,128,1152]{2,1,0:T(8,128)(2,1)} %bitcast.12), calls=%async_computation.1 | async-start | bytes 4718592 | tf_op jit(solution)/shard_map/all_to_all | solution.py:752
  96.3 3.2 %collective-permute-start.23 = (bf16[96,2048]{1,0:T(8,128)(2,1)S(1)}, bf16[96,2048]{1,0:T(8,128)(2,1)S(1)}, u32[]{:S(2)}, u32[]{:S(2)}) collective-permute-start(bf16[96,2048]{1,0:T(8,128)(2,1)S(1)} %get-tuple-element.67), channel_id=1, source_target_pairs={{0,14},{1,15},{2,0},{3,1},{4,2},{5,3},{6,4},{7,5},{8,6},{9,7},{10,... | collective-permute-start | bytes 1179656 | tf_op jit(solution)/shard_map/ppermute | solution.py:26
  99.6 8.1 %collective-permute-done.22.refs_1_ = bf16[96,2048]{1,0:T(8,128)(2,1)S(1)} collective-permute-done((bf16[96,2048]{1,0:T(8,128)(2,1)S(1)}, bf16[96,2048]{1,0:T(8,128)(2,1)S(1)}, u32[]{:S(2)}, u32[]{:S(2)}) %collective-permute-start.22) | collective-permute-done | bytes 393248 | tf_op jit(solution)/shard_map/ppermute | solution.py:26
  107.7 0.7 ring_step.5
  108.4 0.8 collective-permute-start.24
  109.2 2.5 %collective-permute-start.25 = (bf16[96,2048]{1,0:T(8,128)(2,1)S(1)}, bf16[96,2048]{1,0:T(8,128)(2,1)S(1)}, u32[]{:S(2)}, u32[]{:S(2)}) collective-permute-start(bf16[96,2048]{1,0:T(8,128)(2,1)S(1)} %get-tuple-element.69), channel_id=1, source_target_pairs={{0,14},{1,15},{2,0},{3,1},{4,2},{5,3},{6,4},{7,5},{8,6},{9,7},{10,... | collective-permute-start | bytes 1179656 | tf_op jit(solution)/shard_map/ppermute | solution.py:26
  111.8 7.3 %collective-permute-done.24.refs_1_ = bf16[96,2048]{1,0:T(8,128)(2,1)S(1)} collective-permute-done((bf16[96,2048]{1,0:T(8,128)(2,1)S(1)}, bf16[96,2048]{1,0:T(8,128)(2,1)S(1)}, u32[]{:S(2)}, u32[]{:S(2)}) %collective-permute-start.24) | collective-permute-done | bytes 393248 | tf_op jit(solution)/shard_map/ppermute | solution.py:26
  119.1 1.5 %ring_step.6 = (bf16[96,2048]{1,0:T(8,128)(2,1)}, bf16[96,2048]{1,0:T(8,128)(2,1)}) custom-call(s32[5]{0:T(128)S(1)} %copy-done.9, bf16[96,2048]{1,0:T(8,128)(2,1)S(1)} %collective-permute-done.24.refs_1_, bf16[96,2048]{1,0:T(8,128)(2,1)S(1)} %collective-permute-done.25.refs_2_, bf16[7,96,2048]{2,1,0:T(8,128)(2,1)S(1)} %rest_parts.1.refs_12_.refs_3_.refs_4_, ...), custom_call_target="tpu_custom_call" | custom-call | tf_op jit(solution)/shard_map/ring_step/pallas_call | solution.py:65
  120.6 3.0 %collective-permute-start.27 = (bf16[96,2048]{1,0:T(8,128)(2,1)}, bf16[96,2048]{1,0:T(8,128)(2,1)S(1)}, u32[]{:S(2)}, u32[]{:S(2)}) collective-permute-start(bf16[96,2048]{1,0:T(8,128)(2,1)} %get-tuple-element.71), channel_id=1, source_target_pairs={{0,14},{1,15},{2,0},{3,1},{4,2},{5,3},{6,4},{7,5},{8,6},{9,7},{10,... | collective-permute-start | bytes 1179656 | tf_op jit(solution)/shard_map/ppermute | solution.py:26
  123.6 2.6 %all-to-all-done.1.refs_1_ = bf16[8,128,1152]{2,1,0:T(8,128)(2,1)} async-done(((bf16[8,128,1152]{2,1,0:T(8,128)(2,1)}), bf16[8,128,1152]{2,1,0:T(8,128)(2,1)}, u32[]{:S(2)}, u32[]{:S(2)}) %all-to-all-start.1) | async-done | bytes 2359328 | tf_op jit(solution)/shard_map/all_to_all | solution.py:752
  126.2 2.0 %wgrad_sum.1 = (f32[128,512]{1,0:T(8,128)S(1)}, f32[128,128]{1,0:T(8,128)S(1)}, bf16[128,640]{1,0:T(8,128)(2,1)S(1)}) custom-call(s32[5]{0:T(128)S(1)} %copy-done.9, bf16[8,128,1152]{2,1,0:T(8,128)(2,1)} %all-to-all-done.1.refs_1_, bf16[96,2048]{1,0:T(8,128)(2,1)} %get-tuple-element.70.refs_2_), custom_call_target="tpu_custom_call" | custom-call | tf_op jit(solution)/shard_map/wgrad_sum/pallas_call | solution.py:65
  128.1 1.5 %collective-permute-done.27.refs_2_ = bf16[96,2048]{1,0:T(8,128)(2,1)S(1)} collective-permute-done((bf16[96,2048]{1,0:T(8,128)(2,1)}, bf16[96,2048]{1,0:T(8,128)(2,1)S(1)}, u32[]{:S(2)}, u32[]{:S(2)}) %collective-permute-start.27) | collective-permute-done | bytes 393248 | tf_op jit(solution)/shard_map/ppermute | solution.py:26
  129.7 3.3 %collective-permute-done.26.refs_1_ = bf16[96,2048]{1,0:T(8,128)(2,1)S(1)} collective-permute-done((bf16[96,2048]{1,0:T(8,128)(2,1)}, bf16[96,2048]{1,0:T(8,128)(2,1)S(1)}, u32[]{:S(2)}, u32[]{:S(2)}) %collective-permute-start.26) | collective-permute-done | bytes 393248 | tf_op jit(solution)/shard_map/ppermute | solution.py:26
  133.0 0.7 ring_step.7
  133.8 1.9 %collective-permute-start.29 = (bf16[128,640]{1,0:T(8,128)(2,1)S(1)}, bf16[128,640]{1,0:T(8,128)(2,1)S(1)}, u32[]{:S(2)}, u32[]{:S(2)}) collective-permute-start(bf16[128,640]{1,0:T(8,128)(2,1)S(1)} %get-tuple-element.73.refs_5_), channel_id=1, source_target_pairs={{0,1},{1,0},{2,3},{3,2},{4,5},{5,4},{6,7},{7,6},{8,9},{9,8},{10,11... | collective-permute-start | bytes 491528 | tf_op jit(solution)/shard_map/ppermute | solution.py:31
  135.8 5.4 %collective-permute-done.29.refs_5_ = bf16[128,640]{1,0:T(8,128)(2,1)S(1)} collective-permute-done((bf16[128,640]{1,0:T(8,128)(2,1)S(1)}, bf16[128,640]{1,0:T(8,128)(2,1)S(1)}, u32[]{:S(2)}, u32[]{:S(2)}) %collective-permute-start.29) | collective-permute-done | bytes 163872 | tf_op jit(solution)/shard_map/ppermute | solution.py:31
  141.2 1.5 %final.1 = (bf16[48,4096]{1,0:T(8,128)(2,1)}, f32[256,512]{1,0:T(8,128)}, f32[32,256]{1,0:T(8,128)}, f32[32,256]{1,0:T(8,128)}) custom-call(s32[5]{0:T(128)S(1)} %copy-done.9, bf16[48,2048]{1,0:T(8,128)(2,1)S(1)} %get-tuple-element.74.refs_1_, bf16[48,2048]{1,0:T(8,128)(2,1)S(1)} %collective-permute-done.28.refs_2_, ...), custom_call_target="tpu_custom_call" | custom-call | tf_op jit(solution)/shard_map/final/pallas_call | solution.py:65
  (67 shorter events, 7.2 us)
Async XLA Ops:
  3.3 7.0 %collective-permute-start = (bf16[4,48,256]{2,1,0:T(8,128)(2,1)}, bf16[4,48,256]{2,1,0:T(8,128)(2,1)}, u32[]{:S(2)}, u32[]{:S(2)}) collective-permute-start(bf16[4,48,256]{2,1,0:T(8,128)(2,1)} %get-tuple-element.44), channel_id=1, source_target_pairs={{0,1},{1,0},{2,3},{3,2},{4,5},{5,4},{6,7},{7,6},{8,9},{9,8},{10,11... | collective-permute-start | bytes 294920 | tf_op jit(solution)/shard_map/ppermute | solution.py:39
  4.0 6.2 %collective-permute-start.1 = (bf16[4,48,256]{2,1,0:T(8,128)(2,1)}, bf16[4,48,256]{2,1,0:T(8,128)(2,1)}, u32[]{:S(2)}, u32[]{:S(2)}) collective-permute-start(bf16[4,48,256]{2,1,0:T(8,128)(2,1)} %get-tuple-element.45), channel_id=1, source_target_pairs={{0,16},{1,17},{2,18},{3,19},{4,20},{5,21},{6,22},{7,23},{8,24},{9,... | collective-permute-start | bytes 294920 | tf_op jit(solution)/shard_map/ppermute | solution.py:39
  4.0 6.2 %collective-permute-start.2 = (bf16[4,48,256]{2,1,0:T(8,128)(2,1)}, bf16[4,48,256]{2,1,0:T(8,128)(2,1)}, u32[]{:S(2)}, u32[]{:S(2)}) collective-permute-start(bf16[4,48,256]{2,1,0:T(8,128)(2,1)} %get-tuple-element.46), channel_id=1, source_target_pairs={{0,17},{1,16},{2,19},{3,18},{4,21},{5,20},{6,23},{7,22},{8,25},{9,... | collective-permute-start | bytes 294920 | tf_op jit(solution)/shard_map/ppermute | solution.py:39
  5.4 14.9 %all-to-all-start = ((bf16[4,64,768]{2,1,0:T(8,128)(2,1)}), bf16[4,64,768]{2,1,0:T(8,128)(2,1)}, u32[]{:S(2)}, u32[]{:S(2)}) async-start(bf16[4,64,768]{2,1,0:T(8,128)(2,1)} %get-tuple-element.49), calls=%async_computation | async-start | bytes 786432 | tf_op jit(solution)/shard_map/all_to_all | solution.py:714
  13.3 19.4 %copy-start.9 = (s32[5]{0:T(128)S(1)}, s32[5]{0:T(128)}, u32[]{:S(2)}) copy-start(s32[5]{0:T(128)} %stack.23.refs_0_) | copy-start | bytes 64
  13.3 19.4 %collective-permute-start.3 = (bf16[576,512]{1,0:T(8,128)(2,1)}, bf16[576,512]{1,0:T(8,128)(2,1)S(1)}, u32[]{:S(2)}, u32[]{:S(2)}) collective-permute-start(bf16[576,512]{1,0:T(8,128)(2,1)} %get-tuple-element.47), channel_id=1, source_target_pairs={{0,1},{1,0},{2,3},{3,2},{4,5},{5,4},{6,7},{7,6},{8,9},{9,8},{10,11... | collective-permute-start | bytes 1769480 | tf_op jit(solution)/shard_map/ppermute | solution.py:31
  13.9 18.8 %collective-permute-start.5 = (bf16[4,2,96,256]{3,2,1,0:T(8,128)(2,1)}, bf16[4,2,96,256]{3,2,1,0:T(8,128)(2,1)S(1)}, u32[]{:S(2)}, u32[]{:S(2)}) collective-permute-start(bf16[4,2,96,256]{3,2,1,0:T(8,128)(2,1)} %get-tuple-element.48.refs_1_), channel_id=1, source_target_pairs={{0,14},{1,15},{2,0},{3,1},{4,2},{5,3},{6,4},{7,5},{8,6},{9,7},{10,... | collective-permute-start | bytes 1179656 | tf_op jit(solution)/shard_map/ppermute | solution.py:26
  20.3 12.4 %collective-permute-start.4 = (bf16[4,2,96,256]{3,2,1,0:T(8,128)(2,1)}, bf16[4,2,96,256]{3,2,1,0:T(8,128)(2,1)S(1)}, u32[]{:S(2)}, u32[]{:S(2)}) collective-permute-start(bf16[4,2,96,256]{3,2,1,0:T(8,128)(2,1)} %get-tuple-element.48.refs_1_), channel_id=1, source_target_pairs={{0,2},{1,3},{2,4},{3,5},{4,6},{5,7},{6,8},{7,9},{8,10},{9,11},{10,... | collective-permute-start | bytes 1179656 | tf_op jit(solution)/shard_map/ppermute | solution.py:26
  20.3 0.6 copy-start.8
  20.9 1.1 copy-start.10
  22.0 1.1 copy-start.11
  23.2 1.1 copy-start.12
  24.3 0.7 copy-start.14
  25.0 0.7 copy-start.15
  32.7 20.8 %copy-start = (bf16[4096,512]{1,0:T(8,128)(2,1)S(1)}, bf16[4096,512]{1,0:T(8,128)(2,1)}, u32[]{:S(2)}) copy-start(bf16[4096,512]{1,0:T(8,128)(2,1)} %refs_1_.3) | copy-start | bytes 12582916
  32.7 20.8 %copy-start.2 = (bf16[4096,32]{0,1:T(8,128)(2,1)S(1)}, bf16[4096,32]{0,1:T(8,128)(2,1)}, u32[]{:S(2)}) copy-start(bf16[4096,32]{0,1:T(8,128)(2,1)} %param.18) | copy-start | bytes 786436
  32.7 20.8 %copy-start.3 = (bf16[4096,32]{0,1:T(8,128)(2,1)S(1)}, bf16[4096,32]{0,1:T(8,128)(2,1)}, u32[]{:S(2)}) copy-start(bf16[4096,32]{0,1:T(8,128)(2,1)} %param.19) | copy-start | bytes 786436
  33.3 14.5 %collective-permute-start.6 = (bf16[576,512]{1,0:T(8,128)(2,1)S(1)}, bf16[576,512]{1,0:T(8,128)(2,1)S(1)}, u32[]{:S(2)}, u32[]{:S(2)}) collective-permute-start(bf16[576,512]{1,0:T(8,128)(2,1)S(1)} %again.1.refs_4_), channel_id=1, source_target_pairs={{0,64},{16,80},{32,96},{48,112},{64,0},{80,16},{96,32},{112,48},{1... | collective-permute-start | bytes 1769480 | tf_op jit(solution)/shard_map/ppermute | solution.py:31
  34.0 7.8 %collective-permute-start.9 = (bf16[2,64,768]{2,1,0:T(8,128)(2,1)S(1)}, bf16[2,64,768]{2,1,0:T(8,128)(2,1)S(1)}, u32[]{:S(2)}, u32[]{:S(2)}) collective-permute-start(bf16[2,64,768]{2,1,0:T(8,128)(2,1)S(1)} %get-tuple-element.53), channel_id=1, source_target_pairs={{0,2},{1,3},{2,0},{3,1},{4,6},{5,7},{6,4},{7,5},{8,10},{9,11},{10,... | collective-permute-start | bytes 589832 | tf_op jit(solution)/shard_map/ppermute | solution.py:31
  34.0 14.1 %collective-permute-start.11 = (bf16[4,2,96,256]{3,2,1,0:T(8,128)(2,1)S(1)}, bf16[4,2,96,256]{3,2,1,0:T(8,128)(2,1)S(1)}, u32[]{:S(2)}, u32[]{:S(2)}) collective-permute-start(bf16[4,2,96,256]{3,2,1,0:T(8,128)(2,1)S(1)} %collective-permute-done.5.refs_3_), channel_id=1, source_target_pairs={{0,14},{1,15},{2,0},{3,1},{4,2},{5,3},{6,4},{7,5},{8,6},{9,7},{10,... | collective-permute-start | bytes 1179656 | tf_op jit(solution)/shard_map/ppermute | solution.py:26
  37.5 12.1 %collective-permute-start.10 = (bf16[4,2,96,256]{3,2,1,0:T(8,128)(2,1)S(1)}, bf16[4,2,96,256]{3,2,1,0:T(8,128)(2,1)S(1)}, u32[]{:S(2)}, u32[]{:S(2)}) collective-permute-start(bf16[4,2,96,256]{3,2,1,0:T(8,128)(2,1)S(1)} %collective-permute-done.4.refs_2_), channel_id=1, source_target_pairs={{0,2},{1,3},{2,4},{3,5},{4,6},{5,7},{6,8},{7,9},{8,10},{9,11},{10,... | collective-permute-start | bytes 1179656 | tf_op jit(solution)/shard_map/ppermute | solution.py:26
  37.5 14.8 %collective-permute-start.12 = (bf16[768,256]{1,0:T(8,128)(2,1)S(1)}, bf16[768,256]{1,0:T(8,128)(2,1)S(1)}, u32[]{:S(2)}, u32[]{:S(2)}) collective-permute-start(bf16[768,256]{1,0:T(8,128)(2,1)S(1)} %get-tuple-element.51.refs_4_.refs_2_), channel_id=1, source_target_pairs={{0,1},{1,0},{2,3},{3,2},{4,5},{5,4},{6,7},{7,6},{8,9},{9,8},{10,11... | collective-permute-start | bytes 1179656 | tf_op jit(solution)/shard_map/ppermute | solution.py:31
  41.8 11.1 %collective-permute-start.7 = (bf16[576,512]{1,0:T(8,128)(2,1)S(1)}, bf16[576,512]{1,0:T(8,128)(2,1)S(1)}, u32[]{:S(2)}, u32[]{:S(2)}) collective-permute-start(bf16[576,512]{1,0:T(8,128)(2,1)S(1)} %again.1.refs_4_), channel_id=1, source_target_pairs={{0,16},{16,0},{32,48},{48,32},{64,80},{80,64},{96,112},{112,96},{1... | collective-permute-start | bytes 1769480 | tf_op jit(solution)/shard_map/ppermute | solution.py:31
  47.8 5.7 %collective-permute-start.8 = (bf16[576,512]{1,0:T(8,128)(2,1)S(1)}, bf16[576,512]{1,0:T(8,128)(2,1)S(1)}, u32[]{:S(2)}, u32[]{:S(2)}) collective-permute-start(bf16[576,512]{1,0:T(8,128)(2,1)S(1)} %collective-permute-done.6.refs_6_.refs_5_), channel_id=1, source_target_pairs={{0,16},{16,0},{32,48},{48,32},{64,80},{80,64},{96,112},{112,96},{1... | collective-permute-start | bytes 1769480 | tf_op jit(solution)/shard_map/ppermute | solution.py:31
  48.1 11.9 %collective-permute-start.14 = (bf16[768,256]{1,0:T(8,128)(2,1)S(1)}, bf16[768,256]{1,0:T(8,128)(2,1)S(1)}, u32[]{:S(2)}, u32[]{:S(2)}) collective-permute-start(bf16[768,256]{1,0:T(8,128)(2,1)S(1)} %get-tuple-element.57.refs_3_), channel_id=1, source_target_pairs={{0,1},{1,0},{2,3},{3,2},{4,5},{5,4},{6,7},{7,6},{8,9},{9,8},{10,11... | collective-permute-start | bytes 1179656 | tf_op jit(solution)/shard_map/ppermute | solution.py:31
  49.6 11.5 %collective-permute-start.16 = (bf16[4,2,96,256]{3,2,1,0:T(8,128)(2,1)S(1)}, bf16[4,2,96,256]{3,2,1,0:T(8,128)(2,1)S(1)}, u32[]{:S(2)}, u32[]{:S(2)}) collective-permute-start(bf16[4,2,96,256]{3,2,1,0:T(8,128)(2,1)S(1)} %collective-permute-done.11.refs_4_.refs_5_), channel_id=1, source_target_pairs={{0,14},{1,15},{2,0},{3,1},{4,2},{5,3},{6,4},{7,5},{8,6},{9,7},{10,... | collective-permute-start | bytes 1179656 | tf_op jit(solution)/shard_map/ppermute | solution.py:26
  52.3 12.2 %collective-permute-start.15 = (bf16[4,2,96,256]{3,2,1,0:T(8,128)(2,1)S(1)}, bf16[4,2,96,256]{3,2,1,0:T(8,128)(2,1)S(1)}, u32[]{:S(2)}, u32[]{:S(2)}) collective-permute-start(bf16[4,2,96,256]{3,2,1,0:T(8,128)(2,1)S(1)} %collective-permute-done.10.refs_3_.refs_4_), channel_id=1, source_target_pairs={{0,2},{1,3},{2,4},{3,5},{4,6},{5,7},{6,8},{7,9},{8,10},{9,11},{10,... | collective-permute-start | bytes 1179656 | tf_op jit(solution)/shard_map/ppermute | solution.py:26
  52.9 11.6 %collective-permute-start.13 = (bf16[2,64,768]{2,1,0:T(8,128)(2,1)S(1)}, bf16[2,64,768]{2,1,0:T(8,128)(2,1)S(1)}, u32[]{:S(2)}, u32[]{:S(2)}) collective-permute-start(bf16[2,64,768]{2,1,0:T(8,128)(2,1)S(1)} %get-tuple-element.54.refs_8_), channel_id=1, source_target_pairs={{0,1},{1,0},{2,3},{3,2},{4,5},{5,4},{6,7},{7,6},{8,9},{9,8},{10,11... | collective-permute-start | bytes 589832 | tf_op jit(solution)/shard_map/ppermute | solution.py:31
  65.2 14.6 %collective-permute-start.21 = (bf16[768,1152]{1,0:T(8,128)(2,1)S(1)}, bf16[768,1152]{1,0:T(8,128)(2,1)S(1)}, u32[]{:S(2)}, u32[]{:S(2)}) collective-permute-start(bf16[768,1152]{1,0:T(8,128)(2,1)S(1)} %kv_final.1.refs_4_.refs_10_), channel_id=1, source_target_pairs={{0,16},{16,0},{32,48},{48,32},{64,80},{80,64},{96,112},{112,96},{1... | collective-permute-start | bytes 5308424 | tf_op jit(solution)/shard_map/ppermute | solution.py:31
  67.0 9.0 %collective-permute-start.19 = (bf16[2,2,96,256]{3,2,1,0:T(8,128)(2,1)S(1)}, bf16[2,2,96,256]{3,2,1,0:T(8,128)(2,1)S(1)}, u32[]{:S(2)}, u32[]{:S(2)}) collective-permute-start(bf16[2,2,96,256]{3,2,1,0:T(8,128)(2,1)S(1)} %get-tuple-element.63), channel_id=1, source_target_pairs={{0,2},{1,3},{2,4},{3,5},{4,6},{5,7},{6,8},{7,9},{8,10},{9,11},{10,... | collective-permute-start | bytes 589832 | tf_op jit(solution)/shard_map/ppermute | solution.py:26
  67.1 8.9 %collective-permute-start.20 = (bf16[2,2,96,256]{3,2,1,0:T(8,128)(2,1)S(1)}, bf16[2,2,96,256]{3,2,1,0:T(8,128)(2,1)S(1)}, u32[]{:S(2)}, u32[]{:S(2)}) collective-permute-start(bf16[2,2,96,256]{3,2,1,0:T(8,128)(2,1)S(1)} %get-tuple-element.64), channel_id=1, source_target_pairs={{0,14},{1,15},{2,0},{3,1},{4,2},{5,3},{6,4},{7,5},{8,6},{9,7},{10,... | collective-permute-start | bytes 589832 | tf_op jit(solution)/shard_map/ppermute | solution.py:26
  70.3 8.8 %collective-permute-start.18 = (bf16[96,1024]{1,0:T(8,128)(2,1)S(1)}, bf16[96,1024]{1,0:T(8,128)(2,1)S(1)}, u32[]{:S(2)}, u32[]{:S(2)}) collective-permute-start(bf16[96,1024]{1,0:T(8,128)(2,1)S(1)} %get-tuple-element.62), channel_id=1, source_target_pairs={{0,14},{1,15},{2,0},{3,1},{4,2},{5,3},{6,4},{7,5},{8,6},{9,7},{10,... | collective-permute-start | bytes 589832 | tf_op jit(solution)/shard_map/ppermute | solution.py:26
  71.2 8.6 %copy-start.13 = (bf16[4,2,96,256]{3,2,1,0:T(8,128)(2,1)S(1)}, bf16[4,2,96,256]{3,2,1,0:T(8,128)(2,1)}, u32[]{:S(2)}) copy-start(bf16[4,2,96,256]{3,2,1,0:T(8,128)(2,1)} %get-tuple-element.48.refs_1_) | copy-start | bytes 1179652
  71.2 8.6 %collective-permute-start.17 = (bf16[96,1024]{1,0:T(8,128)(2,1)S(1)}, bf16[96,1024]{1,0:T(8,128)(2,1)S(1)}, u32[]{:S(2)}, u32[]{:S(2)}) collective-permute-start(bf16[96,1024]{1,0:T(8,128)(2,1)S(1)} %get-tuple-element.61.refs_5_), channel_id=1, source_target_pairs={{0,2},{1,3},{2,4},{3,5},{4,6},{5,7},{6,8},{7,9},{8,10},{9,11},{10,... | collective-permute-start | bytes 589832 | tf_op jit(solution)/shard_map/ppermute | solution.py:26
  79.1 7.7 %copy-start.4 = (bf16[96,1024]{1,0:T(8,128)(2,1)}, bf16[96,1024]{1,0:T(8,128)(2,1)S(1)}, u32[]{:S(2)}) copy-start(bf16[96,1024]{1,0:T(8,128)(2,1)S(1)} %collective-permute-done.18.refs_14_.refs_2_) | copy-start | bytes 589828
  79.8 6.9 %copy-start.6 = (bf16[96,1024]{1,0:T(8,128)(2,1)}, bf16[96,1024]{1,0:T(8,128)(2,1)S(1)}, u32[]{:S(2)}) copy-start(bf16[96,1024]{1,0:T(8,128)(2,1)S(1)} %collective-permute-done.17.refs_13_.refs_1_) | copy-start | bytes 589828
  86.7 1.5 %copy-start.1 = (bf16[4,256,1152]{2,1,0:T(8,128)(2,1)}, bf16[4,256,1152]{2,1,0:T(8,128)(2,1)S(1)}, u32[]{:S(2)}) copy-start(bf16[4,256,1152]{2,1,0:T(8,128)(2,1)S(1)} %get-tuple-element.72) | copy-start | bytes 7077892
  88.2 7.4 %copy-start.5 = (bf16[96,1024]{1,0:T(8,128)(2,1)S(1)}, bf16[96,1024]{1,0:T(8,128)(2,1)}, u32[]{:S(2)}) copy-start(bf16[96,1024]{1,0:T(8,128)(2,1)} %copy-done.4) | copy-start | bytes 589828
  88.2 7.4 %copy-start.7 = (bf16[96,1024]{1,0:T(8,128)(2,1)S(1)}, bf16[96,1024]{1,0:T(8,128)(2,1)}, u32[]{:S(2)}) copy-start(bf16[96,1024]{1,0:T(8,128)(2,1)} %copy-done.6) | copy-start | bytes 589828
  88.2 37.9 %all-to-all-start.1 = ((bf16[8,128,1152]{2,1,0:T(8,128)(2,1)}), bf16[8,128,1152]{2,1,0:T(8,128)(2,1)}, u32[]{:S(2)}, u32[]{:S(2)}) async-start(bf16[8,128,1152]{2,1,0:T(8,128)(2,1)} %bitcast.12), calls=%async_computation.1 | async-start | bytes 4718592 | tf_op jit(solution)/shard_map/all_to_all | solution.py:752
  96.2 11.5 %collective-permute-start.22 = (bf16[96,2048]{1,0:T(8,128)(2,1)S(1)}, bf16[96,2048]{1,0:T(8,128)(2,1)S(1)}, u32[]{:S(2)}, u32[]{:S(2)}) collective-permute-start(bf16[96,2048]{1,0:T(8,128)(2,1)S(1)} %get-tuple-element.66), channel_id=1, source_target_pairs={{0,2},{1,3},{2,4},{3,5},{4,6},{5,7},{6,8},{7,9},{8,10},{9,11},{10,... | collective-permute-start | bytes 1179656 | tf_op jit(solution)/shard_map/ppermute | solution.py:26
  96.3 11.4 %collective-permute-start.23 = (bf16[96,2048]{1,0:T(8,128)(2,1)S(1)}, bf16[96,2048]{1,0:T(8,128)(2,1)S(1)}, u32[]{:S(2)}, u32[]{:S(2)}) collective-permute-start(bf16[96,2048]{1,0:T(8,128)(2,1)S(1)} %get-tuple-element.67), channel_id=1, source_target_pairs={{0,14},{1,15},{2,0},{3,1},{4,2},{5,3},{6,4},{7,5},{8,6},{9,7},{10,... | collective-permute-start | bytes 1179656 | tf_op jit(solution)/shard_map/ppermute | solution.py:26
  108.4 10.6 %collective-permute-start.24 = (bf16[96,2048]{1,0:T(8,128)(2,1)S(1)}, bf16[96,2048]{1,0:T(8,128)(2,1)S(1)}, u32[]{:S(2)}, u32[]{:S(2)}) collective-permute-start(bf16[96,2048]{1,0:T(8,128)(2,1)S(1)} %get-tuple-element.68), channel_id=1, source_target_pairs={{0,2},{1,3},{2,4},{3,5},{4,6},{5,7},{6,8},{7,9},{8,10},{9,11},{10,... | collective-permute-start | bytes 1179656 | tf_op jit(solution)/shard_map/ppermute | solution.py:26
  109.2 9.9 %collective-permute-start.25 = (bf16[96,2048]{1,0:T(8,128)(2,1)S(1)}, bf16[96,2048]{1,0:T(8,128)(2,1)S(1)}, u32[]{:S(2)}, u32[]{:S(2)}) collective-permute-start(bf16[96,2048]{1,0:T(8,128)(2,1)S(1)} %get-tuple-element.69), channel_id=1, source_target_pairs={{0,14},{1,15},{2,0},{3,1},{4,2},{5,3},{6,4},{7,5},{8,6},{9,7},{10,... | collective-permute-start | bytes 1179656 | tf_op jit(solution)/shard_map/ppermute | solution.py:26
  120.6 9.0 %collective-permute-start.27 = (bf16[96,2048]{1,0:T(8,128)(2,1)}, bf16[96,2048]{1,0:T(8,128)(2,1)S(1)}, u32[]{:S(2)}, u32[]{:S(2)}) collective-permute-start(bf16[96,2048]{1,0:T(8,128)(2,1)} %get-tuple-element.71), channel_id=1, source_target_pairs={{0,14},{1,15},{2,0},{3,1},{4,2},{5,3},{6,4},{7,5},{8,6},{9,7},{10,... | collective-permute-start | bytes 1179656 | tf_op jit(solution)/shard_map/ppermute | solution.py:26
  123.6 9.4 %collective-permute-start.26 = (bf16[96,2048]{1,0:T(8,128)(2,1)}, bf16[96,2048]{1,0:T(8,128)(2,1)S(1)}, u32[]{:S(2)}, u32[]{:S(2)}) collective-permute-start(bf16[96,2048]{1,0:T(8,128)(2,1)} %get-tuple-element.70.refs_2_), channel_id=1, source_target_pairs={{0,2},{1,3},{2,4},{3,5},{4,6},{5,7},{6,8},{7,9},{8,10},{9,11},{10,... | collective-permute-start | bytes 1179656 | tf_op jit(solution)/shard_map/ppermute | solution.py:26
  133.7 7.5 %collective-permute-start.28 = (bf16[48,2048]{1,0:T(8,128)(2,1)S(1)}, bf16[48,2048]{1,0:T(8,128)(2,1)S(1)}, u32[]{:S(2)}, u32[]{:S(2)}) collective-permute-start(bf16[48,2048]{1,0:T(8,128)(2,1)S(1)} %get-tuple-element.75), channel_id=1, source_target_pairs={{0,1},{1,0},{2,3},{3,2},{4,5},{5,4},{6,7},{7,6},{8,9},{9,8},{10,11... | collective-permute-start | bytes 589832 | tf_op jit(solution)/shard_map/ppermute | solution.py:31
  133.8 7.3 %collective-permute-start.29 = (bf16[128,640]{1,0:T(8,128)(2,1)S(1)}, bf16[128,640]{1,0:T(8,128)(2,1)S(1)}, u32[]{:S(2)}, u32[]{:S(2)}) collective-permute-start(bf16[128,640]{1,0:T(8,128)(2,1)S(1)} %get-tuple-element.73.refs_5_), channel_id=1, source_target_pairs={{0,1},{1,0},{2,3},{3,2},{4,5},{5,4},{6,7},{7,6},{8,9},{9,8},{10,11... | collective-permute-start | bytes 491528 | tf_op jit(solution)/shard_map/ppermute | solution.py:31
